TPU v7x, 32 devices: a whole 2x2x4 slice. The times are simulated.
32 devices in a mesh: rep: 1, cache: 32 (over z, y, x, core), owner: 1.
Axes of the slice: x: 2, y: 2, z: 4, core: 2. Of those that a mesh axis runs over, the one named last changes fastest.
Arguments:
- cache_rows: bfloat16 [65536, 128], P(('rep', 'cache')), may hold values from -1.796875 to 1.796875
- store_rows: bfloat16 [32768, 128], P(('rep', 'cache', 'owner')), may hold values from -1.796875 to 1.796875
- miss_block: int32 [32, 2], P(('rep', 'cache', 'owner')), may hold values from 0 to 7
- miss_slot: int32 [32, 2], P(('rep', 'cache')), may hold values from 0 to 16, as said below
- lookup_slot: int32 [32, 32, 624], P(('rep', 'cache', 'owner')), may hold values from 0 to 2047, as said below
- lookup_bag: int32 [32, 32, 624], P(('rep', 'cache', 'owner')), may hold values from 0 to 9984, as said below
- dense_rows: bfloat16 [12288, 128], P(('rep', 'cache', 'owner')), may hold values from -1.796875 to 1.796875
- w_first: bfloat16 [479, 2048], P(None, 'owner'), may hold values from -0.25 to 0.25
- w_second: bfloat16 [2048, 512], P('owner'), may hold values from -0.125 to 0.125
- w_out: float32 [512], replicated, may hold values from -0.25 to 0.25
Outputs:
- logits: float32 [12288], P(('rep', 'cache', 'owner'))
Inputs may be any that keep to these rules, and one draw needn't show every extreme that they name: `miss_slot`: A value of 16 means no fill; the other values of a row are distinct; owner o's entries are o * 2 onward, used ones first, and in every row some owner uses all 2. `lookup_slot`: the cache slot map already applied: a local slot of cache shard d; 0 where the entry is empty. `lookup_bag`: 9984 marks an empty entry; in each bucket the used entries come first, and every device has a bucket with all 624 used.
All inputs are finite; a program needn't handle non-finite values.
Results may differ from a plain program's by a relative error of at most 0.006.
Values may be sent and summed in bfloat16 or wider, within the bound.
No kernel may reach another device: no remote copies, remote signals or barrier semaphores. Data moves between devices by JAX's collectives and lax.ppermute only.
A program may use at most 64 MiB of HBM per device.

v0:
```python
import jax
import jax.numpy as jnp
import numpy as np
from jax import lax
from jax.sharding import PartitionSpec as P

F = 26
BLOCK = 128
BAGS = 9984


def interact(dense_rows, pooled):
    stacked = jnp.concatenate([dense_rows[:, None, :], pooled], axis=1).astype(jnp.float32)
    products = jnp.einsum("qie,qje->qij", stacked, stacked, precision=lax.Precision.HIGHEST)
    upper_rows, upper_cols = np.triu_indices(F + 1, 1)
    paired = products[:, upper_rows, upper_cols].astype(jnp.bfloat16)
    return jnp.concatenate([dense_rows, paired], axis=1)


def per_device(
    cache_rows,
    store_rows,
    miss_block,
    miss_slot,
    lookup_slot,
    lookup_bag,
    dense_rows,
    w_first,
    w_second,
    w_out,
):
    emb_width = cache_rows.shape[1]
    blocks = store_rows.reshape(-1, BLOCK, emb_width)[miss_block[0]]
    filled_blocks = lax.all_gather(blocks, "owner", axis=0, tiled=True)
    cache_now = (
        cache_rows.reshape(-1, BLOCK, emb_width).at[miss_slot[0]].set(filled_blocks, mode="drop")
    )
    cache_now = cache_now.reshape(-1, emb_width)
    arrived = lax.all_to_all(
        cache_now[lax.all_to_all(lookup_slot[0], "cache", split_axis=0, concat_axis=0, tiled=True)],
        "cache",
        split_axis=0,
        concat_axis=0,
        tiled=True,
    )
    bag_ids = lookup_bag[0]
    groups = 4
    stride = arrived.shape[0] // groups
    pooled = jnp.zeros((BAGS, emb_width), jnp.float32)
    for group in range(groups):
        rows_part = (
            arrived[group * stride : (group + 1) * stride]
            .reshape(-1, emb_width)
            .astype(jnp.float32)
        )
        pooled = pooled + jax.ops.segment_sum(
            rows_part,
            bag_ids[group * stride : (group + 1) * stride].reshape(-1),
            num_segments=BAGS,
            mode="drop",
        )
    queries = dense_rows.shape[0]
    inter_in = interact(dense_rows, pooled.astype(jnp.bfloat16).reshape(queries, F, emb_width))
    group_inputs = lax.all_gather(inter_in, "owner", axis=0, tiled=True)
    row_block = lax.slice_in_dim(group_inputs, 0, lax.axis_size("owner") * queries, axis=0)
    hidden = jax.nn.relu(jnp.dot(row_block, w_first, preferred_element_type=jnp.float32)).astype(
        jnp.bfloat16
    )
    second = lax.psum_scatter(
        jnp.dot(hidden, w_second, preferred_element_type=jnp.float32),
        "owner",
        scatter_dimension=0,
        tiled=True,
    )
    return jnp.sum(jax.nn.relu(second) * w_out, axis=1)


def solution(mesh):
    in_specs = (
        P(("rep", "cache"), None),
        P(("rep", "cache", "owner"), None),
        P(("rep", "cache", "owner"), None),
        P(("rep", "cache"), None),
        P(("rep", "cache", "owner"), None, None),
        P(("rep", "cache", "owner"), None, None),
        P(("rep", "cache", "owner"), None),
        P(None, "owner"),
        P("owner", None),
        P(),
    )
    out_specs = P(("rep", "cache", "owner"))
    return jax.shard_map(
        per_device, mesh=mesh, in_specs=in_specs, out_specs=out_specs, check_vma=False
    )
```

profile of v0, /device:TPU:0, one launch (start us, length us, event | category | flops | bytes accessed | tf_op | source)
XLA Modules:
  0.0 344.3 jit_solution(14358920786027148987)
XLA Ops:
  0.0 1.2 copy.27
  1.2 1.6 all_to_all.11
  2.8 7.3 %all-to-all-start = ((s32[32,1,624]{2,1,0:T(1,128)}), s32[32,1,624]{2,1,0:T(1,128)S(1)}, u32[]{:S(2)}, u32[]{:S(2)}) async-start(s32[32,1,624]{2,1,0:T(1,128)} %all_to_all.11), calls=%async_computation | async-start | bytes 163840 | tf_op jit(solution)/shard_map/all_to_all | solution.py:40
  10.1 0.7 fusion.25
  10.7 1.5 gather_fusion
  12.2 0.7 fusion.24
  12.9 0.6 scatter_fusion
  13.5 4.1 %all-to-all-done = s32[32,1,624]{2,1,0:T(1,128)S(1)} async-done(((s32[32,1,624]{2,1,0:T(1,128)}), s32[32,1,624]{2,1,0:T(1,128)S(1)}, u32[]{:S(2)}, u32[]{:S(2)}) %all-to-all-start) | async-done | bytes 79904 | tf_op jit(solution)/shard_map/all_to_all | solution.py:40
  18.0 40.5 %gather_fusion.1 = bf16[19968,128]{1,0:T(8,128)(2,1)} fusion(bf16[2048,128]{1,0:T(8,128)(2,1)S(1)} %bitcast.29, s32[20480]{0:T(1024)S(1)} %pad_clamp_fusion), kind=kCustom, calls=%fused_computation.1 | custom fusion | bytes 10303488 | tf_op jit(solution)/shard_map/gather | solution.py:40
  58.5 3.7 %all-to-all-start.1 = ((bf16[32,624,128]{2,1,0:T(8,128)(2,1)}), bf16[32,624,128]{2,1,0:T(8,128)(2,1)}, u32[]{:S(2)}, u32[]{:S(2)}) async-start(bf16[32,624,128]{2,1,0:T(8,128)(2,1)} %bitcast.30), calls=%async_computation.1 | async-start | bytes 10223616 | tf_op jit(solution)/shard_map/all_to_all | solution.py:39
  62.8 0.8 copy.21
  63.6 112.5 %all-to-all-done.1 = bf16[32,624,128]{2,1,0:T(8,128)(2,1)} async-done(((bf16[32,624,128]{2,1,0:T(8,128)(2,1)}), bf16[32,624,128]{2,1,0:T(8,128)(2,1)}, u32[]{:S(2)}, u32[]{:S(2)}) %all-to-all-start.1) | async-done | bytes 5111840 | tf_op jit(solution)/shard_map/all_to_all | solution.py:39
  176.2 4.4 %fusion.30 = (bf16[8,624,128]{2,1,0:T(8,128)(2,1)}, bf16[8,624,128]{2,1,0:T(8,128)(2,1)S(1)}, bf16[8,624,128]{2,1,0:T(8,128)(2,1)}, bf16[8,624,128]{2,1,0:T(8,128)(2,1)}) fusion(bf16[32,624,128]{2,1,0:T(8,128)(2,1)} %all-to-all-done.1), kind=kLoop, calls=%fused_computation.43 | loop fusion | bytes 10223616 | tf_op jit(solution)/shard_map/slice | solution.py:52
  180.5 30.9 %scatter_custom_fusion.1 = f32[9984,128]{1,0:T(8,128)} fusion(s32[4992]{0:T(1024)S(1)} %reshape.160, bf16[4992,128]{1,0:T(8,128)(2,1)} %bitcast.34, f32[]{:T(128)} %constant.9.clone.1), kind=kCustom, calls=%fused_computation.20 | custom fusion | flops 1277952 | bytes 6389764 | tf_op jit(solution)/shard_map/scatter-add | solution.py:56
  211.4 30.9 %scatter_custom_fusion.2 = f32[9984,128]{1,0:T(8,128)} fusion(s32[4992]{0:T(1024)S(1)} %reshape.168, bf16[4992,128]{1,0:T(8,128)(2,1)} %bitcast.33, f32[]{:T(128)} %constant.9.clone.1), kind=kCustom, calls=%fused_computation.18 | custom fusion | flops 1277952 | bytes 6389764 | tf_op jit(solution)/shard_map/scatter-add | solution.py:56
  242.4 6.3 %add.60 = f32[9984,128]{1,0:T(8,128)} add(f32[9984,128]{1,0:T(8,128)} %scatter_custom_fusion.1, f32[9984,128]{1,0:T(8,128)} %scatter_custom_fusion.2) | non-fusion elementwise | flops 1277952 | bytes 15335424 | tf_op jit(solution)/shard_map/add | solution.py:56
  248.6 30.9 %scatter_custom_fusion.4 = f32[9984,128]{1,0:T(8,128)} fusion(s32[4992]{0:T(1024)S(1)} %reshape.184, bf16[4992,128]{1,0:T(8,128)(2,1)} %bitcast.32, f32[]{:T(128)} %constant.9.clone.1), kind=kCustom, calls=%fused_computation.14 | custom fusion | flops 1277952 | bytes 6389764 | tf_op jit(solution)/shard_map/scatter-add | solution.py:56
  279.5 33.0 %scatter_custom_fusion.3 = f32[9984,128]{1,0:T(8,128)} fusion(f32[9984,128]{1,0:T(8,128)} %add.60, s32[4992]{0:T(1024)S(1)} %reshape.176, bf16[4992,128]{1,0:T(8,128)(2,1)S(1)} %bitcast.31), kind=kCustom, calls=%fused_computation.16 | custom fusion | flops 1277952 | bytes 6389760 | tf_op jit(solution)/shard_map/scatter-add | solution.py:56
  312.6 5.8 %add_convert_fusion = bf16[9984,128]{1,0:T(8,128)(2,1)} fusion(f32[9984,128]{1,0:T(8,128)} %scatter_custom_fusion.3, f32[9984,128]{1,0:T(8,128)} %scatter_custom_fusion.4), kind=kLoop, calls=%fused_computation.8 | loop fusion | flops 2555904 | bytes 12779520 | tf_op jit(solution)/shard_map/convert_element_type | solution.py:63
  318.3 5.3 %reshape.123 = bf16[384,26,128]{2,1,0:T(8,128)(2,1)} reshape(bf16[9984,128]{1,0:T(8,128)(2,1)} %add_convert_fusion) | data formatting | bytes 5111808 | tf_op jit(solution)/shard_map/reshape | solution.py:63
  323.6 6.6 %fusion = bf16[384,27,27]{2,1,0:T(8,128)(2,1)} fusion(bf16[384,26,128]{2,1,0:T(8,128)(2,1)} %reshape.123, bf16[384,1,128]{2,1,0:T(2,128)(2,1)S(1)} %copy-done.3), kind=kOutput, calls=%fused_computation.9 | convolution fusion | flops 76972032 | bytes 3214080 | tf_op jit(solution)/shard_map/qie,qje->qij/dot_general | solution.py:14
  330.2 4.8 %copy.22 = bf16[384,27,27]{0,2,1:T(8,128)(2,1)S(1)} copy(bf16[384,27,27]{2,1,0:T(8,128)(2,1)} %fusion) | data formatting | bytes 1119744 | tf_op jit(solution)/shard_map/qie,qje->qij/dot_general | solution.py:14
  335.0 5.2 %gather_fusion.2 = bf16[351,384]{1,0:T(8,128)(2,1)S(1)} fusion(bf16[384,27,27]{0,2,1:T(8,128)(2,1)S(1)} %copy.22, s32[351]{0:T(512)S(1)} %copy-done.1), kind=kCustom, calls=%fused_computation.2 | custom fusion | bytes 541944 | tf_op jit(solution)/shard_map/gather | solution.py:16
  340.3 4.0 %fusion.16 = f32[384]{0:T(512)} fusion(bf16[2048,512]{1,0:T(8,128)(2,1)S(1)} %copy-done, bf16[479,2048]{1,0:T(8,128)(2,1)} %param.21, f32[512]{0:T(512)S(1)} %copy-done.5, bf16[384,351]{0,1:T(8,128)(2,1)S(1)} %bitcast.36, bf16[384,128]{0,1:T(8,128)(2,1)S(1)} %copy.23), kind=kOutput, calls=%fused_computation.27 | convolution fusion | flops 1561606272 | bytes 4430592 | tf_op jit(solution)/shard_map/dot_general | solution.py:70
  (22 shorter events, 0.8 us)
Async XLA Ops:
  0.0 340.3 %copy-start = (bf16[2048,512]{1,0:T(8,128)(2,1)S(1)}, bf16[2048,512]{1,0:T(8,128)(2,1)}, u32[]{:S(2)}) copy-start(bf16[2048,512]{1,0:T(8,128)(2,1)} %param.22) | copy-start | bytes 6291460
  2.8 14.9 %all-to-all-start = ((s32[32,1,624]{2,1,0:T(1,128)}), s32[32,1,624]{2,1,0:T(1,128)S(1)}, u32[]{:S(2)}, u32[]{:S(2)}) async-start(s32[32,1,624]{2,1,0:T(1,128)} %all_to_all.11), calls=%async_computation | async-start | bytes 163840 | tf_op jit(solution)/shard_map/all_to_all | solution.py:40
  58.5 3.7 %copy-start.4 = (s32[1,32,624]{2,1,0:T(8,128)S(1)}, s32[1,32,624]{2,1,0:T(8,128)}, u32[]{:S(2)}) copy-start(s32[1,32,624]{2,1,0:T(8,128)} %param.19) | copy-start | bytes 239620
  58.5 4.1 %copy-start.2 = (bf16[384,128]{1,0:T(8,128)(2,1)S(1)}, bf16[384,128]{1,0:T(8,128)(2,1)}, u32[]{:S(2)}) copy-start(bf16[384,128]{1,0:T(8,128)(2,1)} %param.20) | copy-start | bytes 294916
  58.5 117.6 %all-to-all-start.1 = ((bf16[32,624,128]{2,1,0:T(8,128)(2,1)}), bf16[32,624,128]{2,1,0:T(8,128)(2,1)}, u32[]{:S(2)}, u32[]{:S(2)}) async-start(bf16[32,624,128]{2,1,0:T(8,128)(2,1)} %bitcast.30), calls=%async_computation.1 | async-start | bytes 10223616 | tf_op jit(solution)/shard_map/all_to_all | solution.py:39
  318.3 5.3 %copy-start.3 = (bf16[384,1,128]{2,1,0:T(2,128)(2,1)S(1)}, bf16[384,1,128]{2,1,0:T(2,128)(2,1)}, u32[]{:S(2)}) copy-start(bf16[384,1,128]{2,1,0:T(2,128)(2,1)} %copy.21) | copy-start | bytes 294916
  330.2 4.8 %copy-start.1 = (s32[351]{0:T(512)S(1)}, s32[351]{0:T(512)}, u32[]{:S(2)}) copy-start(s32[351]{0:T(512)} %constant.54) | copy-start | bytes 4216
  330.2 10.0 %copy-start.5 = (f32[512]{0:T(512)S(1)}, f32[512]{0:T(512)}, u32[]{:S(2)}) copy-start(f32[512]{0:T(512)} %param.23) | copy-start | bytes 6148
where the time goes:
time: 345 us; the launch traced here: 344 us
  other arithmetic  139 us (40%)
  waiting for transfers between devices  117 us (34%)
  local copies, waits for them, and re-layouts  66.4 us (19%)
  starting transfers between devices  11 us (3%)
  matrix products  10.6 us (3%)
    scatter-add x4, other arithmetic, per_device(): jax.ops.segment_sum(rows_part, bag_ids[group * stride:(group + 1) * strid...  126 us
    all_to_all x1, waiting for transfers between devices, per_device(): lax.all_to_all(cache_now[lax.all_to_all(lookup_slot[0], 'cache', split_ax...  113 us
    gather x1, local copies, waits for them, and re-layouts, per_device(): cache_now[lax.all_to_all(lookup_slot[0], 'cache', split_axis=0, concat_ax...  40.5 us
    all_to_all x1, starting transfers between devices, per_device(): lax.all_to_all(lookup_slot[0], 'cache', split_axis=0, concat_axis=0, tile...  7.3 us
  transfers between devices with their start and end apart: 2, of which 2 were waited for; matrix products, arithmetic and copies ran while one was open for 1% of the time, Pallas kernels for 0%

commit v1 on v0

v1 whole, which is shorter than its diff:
```python
import functools

import jax
import jax.numpy as jnp
from jax import lax
from jax.experimental import pallas as pl
from jax.experimental.pallas import tpu as pltpu
from jax.sharding import PartitionSpec as P

F = 26
BLOCK = 128
VECS = F + 1
LANES = 128
CHAINS = 4
UNROLL = 8
VMEM = 56 << 20


def fill_kernel(slot_ref, block_ref, cache_ref, fills_ref, out_ref, sem):
    def of_block(ref, index):
        return ref.at[pl.ds(pl.multiple_of(index * BLOCK, BLOCK), BLOCK)]

    n_slots = out_ref.shape[0] // BLOCK
    n_fills = slot_ref.shape[0]

    def kept(index):
        hit = slot_ref[0] == index
        for k in range(1, n_fills):
            hit = jnp.logical_or(hit, slot_ref[k] == index)
        return jnp.logical_not(hit)

    def cache_copy(index):
        return pltpu.make_async_copy(of_block(cache_ref, index), of_block(out_ref, index), sem.at[index])

    def fill_copy(k):
        slot = jnp.minimum(slot_ref[k], n_slots - 1)
        return pltpu.make_async_copy(
            of_block(fills_ref, block_ref[k]), of_block(out_ref, slot), sem.at[n_slots + k]
        )

    for index in range(n_slots):
        pl.when(kept(index))(lambda index=index: cache_copy(index).start())
    for k in range(n_fills):
        pl.when(slot_ref[k] < n_slots)(lambda k=k: fill_copy(k).start())
    for index in range(n_slots):
        pl.when(kept(index))(lambda index=index: cache_copy(index).wait())
    for k in range(n_fills):
        pl.when(slot_ref[k] < n_slots)(lambda k=k: fill_copy(k).wait())


def fill(cache_rows, fills, miss_slot, fill_block):
    n_sems = cache_rows.shape[0] // BLOCK + miss_slot.shape[0]
    return pl.pallas_call(
        fill_kernel,
        out_shape=jax.ShapeDtypeStruct(cache_rows.shape, cache_rows.dtype),
        in_specs=[pl.BlockSpec(memory_space=pltpu.SMEM)] * 2 + [pl.BlockSpec(memory_space=pl.ANY)] * 2,
        out_specs=pl.BlockSpec(memory_space=pl.ANY),
        scratch_shapes=[pltpu.SemaphoreType.DMA((n_sems,))],
        name="fill",
    )(miss_slot, fill_block, cache_rows, fills)


def pool_shards(slot_ref, bag_ref, count_ref, shards, sems, held, table, sums, cap):
    copies = [pltpu.make_async_copy(ref, held.at[s], sems.at[s]) for s, ref in enumerate(shards)]
    for copy in copies:
        copy.start()
    yield
    for s, copy in enumerate(copies):
        copy.wait()
        table[...] = held[s].astype(jnp.float32)

        def add_entries(step, _):
            first = s * cap + step * UNROLL
            for group in range(UNROLL // CHAINS):
                entries = [first + group * CHAINS + k for k in range(CHAINS)]
                slots = [slot_ref[e] for e in entries]
                bags = [bag_ref[e] for e in entries]
                rows = [table[pl.ds(slot, 1), :] for slot in slots]
                olds = [sums[k][pl.ds(bags[k], 1), :] for k in range(CHAINS)]
                for k in range(CHAINS):
                    sums[k][pl.ds(bags[k], 1), :] = olds[k] + rows[k]
            return 0

        lax.fori_loop(0, count_ref[s], add_entries, 0)


def start_sums(sums, total_ref, sem):
    if total_ref is None:
        sums[0][...] = jnp.zeros_like(sums[0])
    else:
        pltpu.make_async_copy(total_ref, sums[0], sem).start()
    for one in sums[1:]:
        one[...] = jnp.zeros_like(one)
    if total_ref is not None:
        pltpu.make_async_copy(total_ref, sums[0], sem).wait()


def pool_kernel(n_shards, has_total, cap, slot_ref, bag_ref, count_ref, *refs):
    shards, refs = refs[:n_shards], refs[n_shards:]
    total_in, refs = (refs[0], refs[1:]) if has_total else (None, refs)
    total_out, held, table, *sums, sems, total_sem = refs
    pooling = pool_shards(slot_ref, bag_ref, count_ref, shards, sems, held, table, sums, cap)
    next(pooling)
    start_sums(sums, total_in, total_sem)
    for _ in pooling:
        pass
    rows = sums[0].shape[0]
    step = LANES
    n_steps = rows // step

    def add_up(index, _):
        part = pl.ds(pl.multiple_of(index * step, 8), step)
        total = sums[0][part, :]
        for one in sums[1:]:
            total = total + one[part, :]
        sums[0][part, :] = total
        return 0

    lax.fori_loop(0, n_steps, add_up, 0)
    copy = pltpu.make_async_copy(sums[0], total_out, total_sem)
    copy.start()
    copy.wait()


def interact(sums, dense_ref, masked, queries):
    lane = lax.broadcasted_iota(jnp.int32, (8, 256), 1)
    row = lax.broadcasted_iota(jnp.int32, (8, 256), 0)
    own_query = (lane & 7) == row

    def sixteen_queries(step, _):
        dense = dense_ref[pl.ds(pl.multiple_of(step * 16, 16), 16), :].astype(jnp.float32)
        halves = []
        for half in range(2):
            query = pl.multiple_of(step * 16 + half * 8, 8)
            vectors = [dense[half * 8 : half * 8 + 8]]
            for feature in range(F):
                rows = pl.ds(pl.multiple_of(feature * queries + query, 8), 8)
                total = sums[0][rows, :]
                for one in sums[1:]:
                    total = total + one[rows, :]
                vectors.append(total)
            vectors += [jnp.zeros((8, LANES), jnp.float32)] * (32 - VECS)
            stacked = jnp.concatenate(vectors, axis=0).astype(jnp.bfloat16)
            halves.append(
                lax.dot_general(
                    stacked, stacked, (((1,), (1,)), ((), ())), preferred_element_type=jnp.float32
                )
            )
        for i in range(F):
            pair = [
                jnp.where(own_query, products[8 * i : 8 * i + 8, :], 0.0) for products in halves
            ]
            masked[i, pl.ds(pl.multiple_of(step * 16, 16), 16), :] = jnp.concatenate(
                pair, axis=0
            ).astype(jnp.bfloat16)
        return 0

    lax.fori_loop(0, queries // 16, sixteen_queries, 0)


def inter_columns(masked, dense_ref, inter, queries):
    spread = lax.broadcasted_iota(jnp.int32, (256, LANES), 0) // 8
    vector = lax.broadcasted_iota(jnp.int32, (256, LANES), 1)
    pick = jnp.where(spread == vector, 1.0, 0.0).astype(jnp.bfloat16)
    lane = lax.broadcasted_iota(jnp.int32, (queries, LANES), 1)
    tiles = [jnp.zeros((queries, LANES), jnp.float32) for _ in range(3)]
    first = 0
    for i in range(F):
        length = F - i
        picked = jnp.dot(masked[i], pick, preferred_element_type=jnp.float32)
        shift = (first - (i + 1)) % LANES
        if shift:
            picked = pltpu.roll(picked, shift, 1)
        for tile in range(3):
            low, high = max(first, tile * LANES), min(first + length, (tile + 1) * LANES)
            if low < high:
                inside = jnp.logical_and(lane >= low - tile * LANES, lane < high - tile * LANES)
                tiles[tile] = jnp.where(inside, picked, tiles[tile])
        first += length
    inter[:, :LANES] = dense_ref[...]
    for tile in range(3):
        inter[:, (tile + 1) * LANES : (tile + 2) * LANES] = tiles[tile].astype(jnp.bfloat16)


def final_kernel(n_shards, cap, with_head, slot_ref, bag_ref, count_ref, *refs):
    shards, refs = refs[:n_shards], refs[n_shards:]
    total_in, dense_ref, refs = refs[0], refs[1], refs[2:]
    if with_head:
        w_first, w_second, w_out, logits, inter, masked, first_held, second_held, weight_sems, *refs = refs
        weights = [
            pltpu.make_async_copy(w_first, first_held, weight_sems.at[0]),
            pltpu.make_async_copy(w_second, second_held, weight_sems.at[1]),
        ]
        for copy in weights:
            copy.start()
    else:
        inter, masked, *refs = refs
    held, table, *sums, sems, total_sem = refs
    queries = dense_ref.shape[0]
    pooling = pool_shards(slot_ref, bag_ref, count_ref, shards, sems, held, table, sums, cap)
    next(pooling)
    start_sums(sums, total_in, total_sem)
    for _ in pooling:
        pass
    interact(sums, dense_ref, masked, queries)
    inter_columns(masked, dense_ref, inter, queries)
    if not with_head:
        return
    for copy in weights:
        copy.wait()
    step = LANES
    for part in range(queries // step):
        rows = slice(part * step, (part + 1) * step)
        hidden = jnp.dot(inter[rows, :], first_held[...], preferred_element_type=jnp.float32)
        hidden = jnp.maximum(hidden, 0.0).astype(jnp.bfloat16)
        second = jnp.dot(hidden, second_held[...], preferred_element_type=jnp.float32)
        scored = jnp.maximum(second, 0.0) * w_out[...]
        folded = scored[:, :LANES]
        for tile in range(1, scored.shape[1] // LANES):
            folded = folded + scored[:, tile * LANES : (tile + 1) * LANES]
        logits[:, rows] = jnp.sum(folded.T, axis=0, keepdims=True)


def pool_scratch(n_shards, shard_rows, sum_rows):
    return (
        [pltpu.VMEM((n_shards, shard_rows, LANES), jnp.bfloat16), pltpu.VMEM((shard_rows, LANES), jnp.float32)]
        + [pltpu.VMEM((sum_rows, LANES), jnp.float32)] * CHAINS
        + [pltpu.SemaphoreType.DMA((n_shards,)), pltpu.SemaphoreType.DMA]
    )


SMEM_SPEC = pl.BlockSpec(memory_space=pltpu.SMEM)
ANY_SPEC = pl.BlockSpec(memory_space=pl.ANY)
VMEM_SPEC = pl.BlockSpec(memory_space=pltpu.VMEM)


def pool(slots, bags, counts, shards, total, cap, sum_rows):
    n_shards = len(shards)
    totals = [] if total is None else [total]
    return pl.pallas_call(
        functools.partial(pool_kernel, n_shards, total is not None, cap),
        out_shape=jax.ShapeDtypeStruct((sum_rows, LANES), jnp.float32),
        in_specs=[SMEM_SPEC] * 3 + [ANY_SPEC] * (n_shards + len(totals)),
        out_specs=ANY_SPEC,
        scratch_shapes=pool_scratch(n_shards, shards[0].shape[0], sum_rows),
        compiler_params=pltpu.CompilerParams(vmem_limit_bytes=VMEM),
        cost_estimate=pl.CostEstimate(flops=0, bytes_accessed=n_shards * 4_000_000, transcendentals=0),
        name="pool",
    )(slots, bags, counts, *shards, *totals)


def finish(slots, bags, counts, shards, total, cap, sum_rows, dense_rows, head):
    n_shards = len(shards)
    queries = dense_rows.shape[0]
    width = 4 * LANES
    masked = pltpu.VMEM((F, queries, 256), jnp.bfloat16)
    if head is None:
        head_args, head_specs = [], []
        out_shape = jax.ShapeDtypeStruct((queries, width), jnp.bfloat16)
        scratch = [masked]
    else:
        head_args, head_specs = list(head), [ANY_SPEC, ANY_SPEC, VMEM_SPEC]
        out_shape = jax.ShapeDtypeStruct((1, queries), jnp.float32)
        scratch = [
            pltpu.VMEM((queries, width), jnp.bfloat16),
            masked,
            pltpu.VMEM(head[0].shape, jnp.bfloat16),
            pltpu.VMEM(head[1].shape, jnp.bfloat16),
            pltpu.SemaphoreType.DMA((2,)),
        ]
    return pl.pallas_call(
        functools.partial(final_kernel, n_shards, cap, head is not None),
        out_shape=out_shape,
        in_specs=[SMEM_SPEC] * 3 + [ANY_SPEC] * (n_shards + 1) + [VMEM_SPEC] + head_specs,
        out_specs=VMEM_SPEC,
        scratch_shapes=scratch + pool_scratch(n_shards, shards[0].shape[0], sum_rows),
        compiler_params=pltpu.CompilerParams(vmem_limit_bytes=VMEM),
        name="finish",
    )(slots, bags, counts, *shards, total, dense_rows, *head_args)


def per_device(
    n_planes,
    cache_rows,
    store_rows,
    miss_block,
    miss_slot,
    lookup_slot,
    lookup_bag,
    dense_rows,
    w_first,
    w_second,
    w_out,
):
    emb_width = cache_rows.shape[1]
    queries = dense_rows.shape[0]
    bags = queries * F
    owners = lax.axis_size("owner")
    n_shards = n_planes * 8

    if owners == 1:
        fills, fill_block = store_rows, miss_block[0]
    else:
        fills = store_rows.reshape(-1, BLOCK, emb_width)[miss_block[0]]
        fills = lax.all_gather(fills, "owner", axis=0, tiled=True)
        fill_block = jnp.arange(fills.shape[0], dtype=jnp.int32)
        fills = fills.reshape(-1, emb_width)
    own = fill(cache_rows, fills, miss_slot[0], fill_block)

    def device(z, y, x, core):
        return ((z * 2 + y) * 2 + x) * 2 + core

    def hop(move):
        pairs = []
        for index in range(n_shards):
            at = (index // 8, index // 4 % 2, index // 2 % 2, index % 2)
            pairs.append((index, device(*move(*at))))
        return lambda array: lax.ppermute(array, "cache", pairs)

    next_plane = hop(lambda z, y, x, core: ((z + 1) % n_planes, y, x, core))
    first_hop = hop(lambda z, y, x, core: (z, y, 1 - x, core) if core == 0 else (z, 1 - y, x, core))
    second_hop = hop(lambda z, y, x, core: (z, 1 - y, x, core) if core == 0 else (z, y, 1 - x, core))
    other_core = hop(lambda z, y, x, core: (z, y, x, 1 - core))

    me = lax.axis_index("cache")
    z, y, x, core = me // 8, me // 4 % 2, me // 2 % 2, me % 2
    planes, order = [], []
    piece = own
    for shift in range(n_planes):
        if shift:
            piece = next_plane(piece)
        crossed = first_hop(piece)
        mine = [piece, crossed, second_hop(piece), second_hop(crossed)]
        planes.append(mine + [other_core(one) for one in mine])
        for side in (core, 1 - core):
            from_z = (z - shift) % n_planes
            for flip_first, flip_second in ((0, 0), (1, 0), (0, 1), (1, 1)):
                flip_x = jnp.where(side == 0, flip_first, flip_second)
                flip_y = jnp.where(side == 0, flip_second, flip_first)
                order.append(device(from_z, y ^ flip_y, x ^ flip_x, side))
    order = jnp.stack(order)

    cap = lookup_slot.shape[2]
    cap += -cap % UNROLL
    spare = ((0, 0), (0, cap - lookup_slot.shape[2]))
    slots = jnp.pad(lookup_slot[0], spare)[order]
    bag_ids = jnp.pad(lookup_bag[0], spare, constant_values=bags)[order]
    used = jnp.sum((bag_ids < bags).astype(jnp.int32), axis=1)
    steps = (used + UNROLL - 1) // UNROLL
    sum_rows = bags + 8
    places = jnp.where(bag_ids < bags, bag_ids % F * queries + bag_ids // F, bags)

    groups = [list(range(n_planes - 2))[: n_planes // 2]]
    groups += [[plane] for plane in range(len(groups[0]), n_planes)]
    total = None
    for group in groups:
        part = slice(8 * group[0], 8 * group[-1] + 8)
        args = (slots[part].reshape(-1), places[part].reshape(-1), steps[part])
        shards = [one for plane in group for one in planes[plane]]
        if group is not groups[-1]:
            total = pool(*args, shards, total, cap, sum_rows)
    short = -w_first.shape[0] % LANES
    w_first = jnp.pad(w_first, ((0, short), (0, 0)))
    if owners == 1:
        head = (w_first, w_second, w_out.reshape(1, -1))
        logits = finish(*args, shards, total, cap, sum_rows, dense_rows, head)
        return logits.reshape(-1)
    inter_in = finish(*args, shards, total, cap, sum_rows, dense_rows, None)
    group_inputs = lax.all_gather(inter_in, "owner", axis=0, tiled=True)
    hidden = jax.nn.relu(jnp.dot(group_inputs, w_first, preferred_element_type=jnp.float32))
    second = lax.psum_scatter(
        jnp.dot(hidden.astype(jnp.bfloat16), w_second, preferred_element_type=jnp.float32),
        "owner",
        scatter_dimension=0,
        tiled=True,
    )
    return jnp.sum(jax.nn.relu(second) * w_out, axis=1)


def solution(mesh):
    in_specs = (
        P(("rep", "cache"), None),
        P(("rep", "cache", "owner"), None),
        P(("rep", "cache", "owner"), None),
        P(("rep", "cache"), None),
        P(("rep", "cache", "owner"), None, None),
        P(("rep", "cache", "owner"), None, None),
        P(("rep", "cache", "owner"), None),
        P(None, "owner"),
        P("owner", None),
        P(),
    )
    out_specs = P(("rep", "cache", "owner"))
    return jax.shard_map(
        functools.partial(per_device, mesh.shape["cache"] // 8),
        mesh=mesh,
        in_specs=in_specs,
        out_specs=out_specs,
        check_vma=False,
    )
```

time: 345 us -> 175 us (0.51)
  other arithmetic: 139 us -> 1.48 us
  Pallas kernels: 0 us -> 84.7 us
  waiting for transfers between devices: 117 us -> 54.7 us
  local copies, waits for them, and re-layouts: 66.4 us -> 7.76 us
  starting transfers between devices: 11 us -> 23.8 us
  matrix products: 10.6 us -> 0 us
    scatter-add x4 -> x0, other arithmetic: 126 us -> none  [per_device(): jax.ops.segment_sum(rows_part, bag_ids[group * stride:(group + 1) * strid...]
    all_to_all x2 -> x0, waiting for transfers between devices: 117 us -> none  [the longest x1 113 us: per_device(): lax.all_to_all(cache_now[lax.all_to_all(lookup_slot[0], 'cache', split_ax...]
    pallas_call x0 -> x4, Pallas kernels: none -> 84.7 us  [the longest x2 41.7 us: pool(): pl.pallas_call(functools.partial(pool_kernel, n_shards, total is not None...]
    ppermute x0 -> x31, waiting for transfers between devices: none -> 54.7 us  [hop(): return lambda array: lax.ppermute(array, 'cache', pairs)]
    gather x3 -> x2, local copies, waits for them, and re-layouts: 47.2 us -> 1.23 us  [the longest x1 0.61 us: per_device(): slots = jnp.pad(lookup_slot[0], spare)[order]]
    ppermute x0 -> x31, starting transfers between devices: none -> 23.8 us  [hop(): return lambda array: lax.ppermute(array, 'cache', pairs)]
    all_to_all x2 -> x0, starting transfers between devices: 11 us -> none  [the longest x1 7.3 us: per_device(): lax.all_to_all(lookup_slot[0], 'cache', split_axis=0, concat_axis=0, tile...]
    dot_general x2 -> x0, matrix products: 10.6 us -> none  [the longest x1 6.61 us: interact(): jnp.einsum('qie,qje->qij', stacked, stacked, precision=lax.Precision.HIGH...]
  transfers between devices with their start and end apart: 2 -> 31, of which waited for: 2 -> 10; matrix products, arithmetic and copies ran while one was open for 1% -> 5% of each run, Pallas kernels for 0% -> 24%
where the time goes in v1:
time: 175 us; the launch traced here: 173 us
  Pallas kernels  84.7 us (48%)
  waiting for transfers between devices  54.7 us (31%)
  starting transfers between devices  23.8 us (14%)
  local copies, waits for them, and re-layouts  7.76 us (4%)
    ppermute x31, waiting for transfers between devices, hop(): return lambda array: lax.ppermute(array, 'cache', pairs)  54.7 us
    pallas_call x2, Pallas kernels, pool(): pl.pallas_call(functools.partial(pool_kernel, n_shards, total is not None...  41.7 us
    pallas_call x1, Pallas kernels, finish(): pl.pallas_call(functools.partial(final_kernel, n_shards, cap, head is not...  25.1 us
    ppermute x31, starting transfers between devices, hop(): return lambda array: lax.ppermute(array, 'cache', pairs)  23.8 us
    pallas_call x1, Pallas kernels, fill(): pl.pallas_call(fill_kernel, out_shape=jax.ShapeDtypeStruct(cache_rows.sha...  17.9 us
    reshape x6, local copies, waits for them, and re-layouts, per_device(): args = (slots[part].reshape(-1), places[part].reshape(-1), steps[part])  4.14 us
  transfers between devices with their start and end apart: 31, of which 10 were waited for; matrix products, arithmetic and copies ran while one was open for 5% of the time, Pallas kernels for 24%

profile of v1, /device:TPU:0, one launch (start us, length us, event | category | flops | bytes accessed | tf_op | source)
XLA Modules:
  0.0 173.0 jit_solution(3691655830603650751)
XLA Ops:
  0.0 17.9 %fill.1.refs_0_ = bf16[2048,128]{1,0:T(8,128)(2,1)} custom-call(s32[2]{0:T(128)} %bitcast.44, s32[2]{0:T(128)} %bitcast.45, bf16[2048,128]{1,0:T(8,128)(2,1)} %cache_ref.1, bf16[1024,128]{1,0:T(8,128)(2,1)} %fills_ref.1), custom_call_target="tpu_custom_call" | custom-call | tf_op jit(solution)/shard_map/fill/pallas_call | solution.py:53
  18.0 3.0 %collective-permute-start.18 = (bf16[2048,128]{1,0:T(8,128)(2,1)}, bf16[2048,128]{1,0:T(8,128)(2,1)S(1)}, u32[]{:S(2)}, u32[]{:S(2)}) collective-permute-start(bf16[2048,128]{1,0:T(8,128)(2,1)} %fill.1.refs_0_), channel_id=1, source_target_pairs={{0,4},{1,3},{2,6},{3,1},{4,0},{5,7},{6,2},{7,5},{8,12},{9,11},{10,... | collective-permute-start | bytes 1572872 | tf_op jit(solution)/shard_map/ppermute | solution.py:318
  21.0 1.5 collective-permute-start.17
  22.5 1.6 collective-permute-start
  24.1 9.5 %collective-permute-done.18.refs_2_ = bf16[2048,128]{1,0:T(8,128)(2,1)S(1)} collective-permute-done((bf16[2048,128]{1,0:T(8,128)(2,1)}, bf16[2048,128]{1,0:T(8,128)(2,1)S(1)}, u32[]{:S(2)}, u32[]{:S(2)}) %collective-permute-start.18) | collective-permute-done | bytes 524320 | tf_op jit(solution)/shard_map/ppermute | solution.py:318
  34.1 2.3 %collective-permute-start.19 = (bf16[2048,128]{1,0:T(8,128)(2,1)S(1)}, bf16[2048,128]{1,0:T(8,128)(2,1)S(1)}, u32[]{:S(2)}, u32[]{:S(2)}) collective-permute-start(bf16[2048,128]{1,0:T(8,128)(2,1)S(1)} %collective-permute-done.17.refs_1_), channel_id=1, source_target_pairs={{0,4},{1,3},{2,6},{3,1},{4,0},{5,7},{6,2},{7,5},{8,12},{9,11},{10,... | collective-permute-start | bytes 1572872 | tf_op jit(solution)/shard_map/ppermute | solution.py:318
  39.3 8.9 %collective-permute-done.19.refs_3_ = bf16[2048,128]{1,0:T(8,128)(2,1)S(1)} collective-permute-done((bf16[2048,128]{1,0:T(8,128)(2,1)S(1)}, bf16[2048,128]{1,0:T(8,128)(2,1)S(1)}, u32[]{:S(2)}, u32[]{:S(2)}) %collective-permute-start.19) | collective-permute-done | bytes 524320 | tf_op jit(solution)/shard_map/ppermute | solution.py:318
  48.2 6.6 %collective-permute-done.25.refs_10_ = bf16[2048,128]{1,0:T(8,128)(2,1)S(1)} collective-permute-done((bf16[2048,128]{1,0:T(8,128)(2,1)S(1)}, bf16[2048,128]{1,0:T(8,128)(2,1)S(1)}, u32[]{:S(2)}, u32[]{:S(2)}) %collective-permute-start.25) | collective-permute-done | bytes 524320 | tf_op jit(solution)/shard_map/ppermute | solution.py:318
  55.4 2.0 %collective-permute-start.26 = (bf16[2048,128]{1,0:T(8,128)(2,1)S(1)}, bf16[2048,128]{1,0:T(8,128)(2,1)}, u32[]{:S(2)}, u32[]{:S(2)}) collective-permute-start(bf16[2048,128]{1,0:T(8,128)(2,1)S(1)} %collective-permute-done.24.refs_9_), channel_id=1, source_target_pairs={{0,4},{1,3},{2,6},{3,1},{4,0},{5,7},{6,2},{7,5},{8,12},{9,11},{10,... | collective-permute-start | bytes 1572872 | tf_op jit(solution)/shard_map/ppermute | solution.py:318
  57.4 1.6 collective-permute-start.2
  60.3 8.6 %collective-permute-done.26.refs_11_ = bf16[2048,128]{1,0:T(8,128)(2,1)} collective-permute-done((bf16[2048,128]{1,0:T(8,128)(2,1)S(1)}, bf16[2048,128]{1,0:T(8,128)(2,1)}, u32[]{:S(2)}, u32[]{:S(2)}) %collective-permute-start.26) | collective-permute-done | bytes 524320 | tf_op jit(solution)/shard_map/ppermute | solution.py:318
  68.9 3.3 %collective-permute-done.2.refs_0_ = bf16[2048,128]{1,0:T(8,128)(2,1)} collective-permute-done((bf16[2048,128]{1,0:T(8,128)(2,1)S(1)}, bf16[2048,128]{1,0:T(8,128)(2,1)}, u32[]{:S(2)}, u32[]{:S(2)}) %collective-permute-start.2) | collective-permute-done | bytes 524320 | tf_op jit(solution)/shard_map/ppermute | solution.py:318
  72.2 1.3 collective-permute-start.3
  74.1 1.6 collective-permute-start.12
  75.6 1.8 %collective-permute-done.11.refs_2_ = bf16[2048,128]{1,0:T(8,128)(2,1)} collective-permute-done((bf16[2048,128]{1,0:T(8,128)(2,1)S(1)}, bf16[2048,128]{1,0:T(8,128)(2,1)}, u32[]{:S(2)}, u32[]{:S(2)}) %collective-permute-start.11) | collective-permute-done | bytes 524320 | tf_op jit(solution)/shard_map/ppermute | solution.py:318
  77.4 2.3 %collective-permute-start.4 = (bf16[2048,128]{1,0:T(8,128)(2,1)}, bf16[2048,128]{1,0:T(8,128)(2,1)}, u32[]{:S(2)}, u32[]{:S(2)}) collective-permute-start(bf16[2048,128]{1,0:T(8,128)(2,1)} %collective-permute-done.2.refs_0_), channel_id=1, source_target_pairs={{0,4},{1,3},{2,6},{3,1},{4,0},{5,7},{6,2},{7,5},{8,12},{9,11},{10,... | collective-permute-start | bytes 1572872 | tf_op jit(solution)/shard_map/ppermute | solution.py:318
  79.7 6.3 %collective-permute-done.3.refs_1_ = bf16[2048,128]{1,0:T(8,128)(2,1)} collective-permute-done((bf16[2048,128]{1,0:T(8,128)(2,1)}, bf16[2048,128]{1,0:T(8,128)(2,1)}, u32[]{:S(2)}, u32[]{:S(2)}) %collective-permute-start.3) | collective-permute-done | bytes 524320 | tf_op jit(solution)/shard_map/ppermute | solution.py:318
  86.1 1.5 collective-permute-start.5
  89.7 3.0 %collective-permute-done.4.refs_2_ = bf16[2048,128]{1,0:T(8,128)(2,1)} collective-permute-done((bf16[2048,128]{1,0:T(8,128)(2,1)}, bf16[2048,128]{1,0:T(8,128)(2,1)}, u32[]{:S(2)}, u32[]{:S(2)}) %collective-permute-start.4) | collective-permute-done | bytes 524320 | tf_op jit(solution)/shard_map/ppermute | solution.py:318
  93.0 5.3 %collective-permute-done.5.refs_3_ = bf16[2048,128]{1,0:T(8,128)(2,1)} collective-permute-done((bf16[2048,128]{1,0:T(8,128)(2,1)}, bf16[2048,128]{1,0:T(8,128)(2,1)}, u32[]{:S(2)}, u32[]{:S(2)}) %collective-permute-start.5) | collective-permute-done | bytes 524320 | tf_op jit(solution)/shard_map/ppermute | solution.py:318
  102.7 1.5 pad.4.refs_10_
  104.8 24.0 %pool.2.refs_8_ = f32[9992,128]{1,0:T(8,128)} custom-call(s32[9984]{0:T(1024)} %reshape.1253.slot_ref, s32[9984]{0:T(1024)} %reshape.1254.bag_ref, s32[16]{0:T(128)} %bitcast.42, bf16[2048,128]{1,0:T(8,128)(2,1)} %fill.1.refs_0_, bf16[2048,128]{1,0:T(8,128)(2,1)} %copy-done.6, bf16[2048,128]{1,0:T(8,128)(2,1)} %copy-done.5, bf16[2048,128]{1,0:T(8,128)(2,1)} %copy-done.11, ...), custom_call_target="tpu_custom_call" | custom-call | bytes 64000000 | tf_op jit(solution)/shard_map/pool/pallas_call | solution.py:240
  128.9 17.6 %pool.3.refs_8_ = f32[9992,128]{1,0:T(8,128)} custom-call(s32[4992]{0:T(1024)} %reshape.1251.slot_ref, s32[4992]{0:T(1024)} %reshape.1252.bag_ref, s32[8]{0:T(128)} %get-tuple-element.11.count_ref, bf16[2048,128]{1,0:T(8,128)(2,1)} %copy-done.3, bf16[2048,128]{1,0:T(8,128)(2,1)} %copy-done.4, bf16[2048,128]{1,0:T(8,128)(2,1)} %collective-permute-done.11.refs_2_, ...), custom_call_target="tpu_custom_call" | custom-call | bytes 32000000 | tf_op jit(solution)/shard_map/pool/pallas_call | solution.py:240
  146.6 25.1 %finish.1 = f32[1,384]{1,0:T(1,128)} custom-call(s32[4992]{0:T(1024)} %reshape.1249.slot_ref, s32[4992]{0:T(1024)} %reshape.1250.bag_ref, s32[8]{0:T(128)} %get-tuple-element.12.count_ref, bf16[2048,128]{1,0:T(8,128)(2,1)} %collective-permute-done.2.refs_0_, bf16[2048,128]{1,0:T(8,128)(2,1)} %collective-permute-done.3.refs_1_, ...), custom_call_target="tpu_custom_call" | custom-call | tf_op jit(solution)/shard_map/finish/pallas_call | solution.py:271
  (100 shorter events, 14.0 us)
Async XLA Ops:
  18.0 15.6 %collective-permute-start.18 = (bf16[2048,128]{1,0:T(8,128)(2,1)}, bf16[2048,128]{1,0:T(8,128)(2,1)S(1)}, u32[]{:S(2)}, u32[]{:S(2)}) collective-permute-start(bf16[2048,128]{1,0:T(8,128)(2,1)} %fill.1.refs_0_), channel_id=1, source_target_pairs={{0,4},{1,3},{2,6},{3,1},{4,0},{5,7},{6,2},{7,5},{8,12},{9,11},{10,... | collective-permute-start | bytes 1572872 | tf_op jit(solution)/shard_map/ppermute | solution.py:318
  21.0 12.6 %collective-permute-start.17 = (bf16[2048,128]{1,0:T(8,128)(2,1)}, bf16[2048,128]{1,0:T(8,128)(2,1)S(1)}, u32[]{:S(2)}, u32[]{:S(2)}) collective-permute-start(bf16[2048,128]{1,0:T(8,128)(2,1)} %fill.1.refs_0_), channel_id=1, source_target_pairs={{0,2},{1,5},{2,0},{3,7},{4,6},{5,1},{6,4},{7,3},{8,10},{9,13},{10,... | collective-permute-start | bytes 1572872 | tf_op jit(solution)/shard_map/ppermute | solution.py:318
  22.5 15.2 %collective-permute-start = (bf16[2048,128]{1,0:T(8,128)(2,1)}, bf16[2048,128]{1,0:T(8,128)(2,1)S(1)}, u32[]{:S(2)}, u32[]{:S(2)}) collective-permute-start(bf16[2048,128]{1,0:T(8,128)(2,1)} %fill.1.refs_0_), channel_id=1, source_target_pairs={{0,8},{1,9},{2,10},{3,11},{4,12},{5,13},{6,14},{7,15},{8,16},{9,17... | collective-permute-start | bytes 1572872 | tf_op jit(solution)/shard_map/ppermute | solution.py:318
  24.1 14.1 %collective-permute-start.20 = (bf16[2048,128]{1,0:T(8,128)(2,1)}, bf16[2048,128]{1,0:T(8,128)(2,1)S(1)}, u32[]{:S(2)}, u32[]{:S(2)}) collective-permute-start(bf16[2048,128]{1,0:T(8,128)(2,1)} %fill.1.refs_0_), channel_id=1, source_target_pairs={{0,1},{1,0},{2,3},{3,2},{4,5},{5,4},{6,7},{7,6},{8,9},{9,8},{10,11... | collective-permute-start | bytes 1572872 | tf_op jit(solution)/shard_map/ppermute | solution.py:318
  34.1 14.1 %collective-permute-start.19 = (bf16[2048,128]{1,0:T(8,128)(2,1)S(1)}, bf16[2048,128]{1,0:T(8,128)(2,1)S(1)}, u32[]{:S(2)}, u32[]{:S(2)}) collective-permute-start(bf16[2048,128]{1,0:T(8,128)(2,1)S(1)} %collective-permute-done.17.refs_1_), channel_id=1, source_target_pairs={{0,4},{1,3},{2,6},{3,1},{4,0},{5,7},{6,2},{7,5},{8,12},{9,11},{10,... | collective-permute-start | bytes 1572872 | tf_op jit(solution)/shard_map/ppermute | solution.py:318
  37.7 17.1 %collective-permute-start.25 = (bf16[2048,128]{1,0:T(8,128)(2,1)S(1)}, bf16[2048,128]{1,0:T(8,128)(2,1)S(1)}, u32[]{:S(2)}, u32[]{:S(2)}) collective-permute-start(bf16[2048,128]{1,0:T(8,128)(2,1)S(1)} %collective-permute-done.refs_8_), channel_id=1, source_target_pairs={{0,4},{1,3},{2,6},{3,1},{4,0},{5,7},{6,2},{7,5},{8,12},{9,11},{10,... | collective-permute-start | bytes 1572872 | tf_op jit(solution)/shard_map/ppermute | solution.py:318
  38.2 16.6 %collective-permute-start.24 = (bf16[2048,128]{1,0:T(8,128)(2,1)S(1)}, bf16[2048,128]{1,0:T(8,128)(2,1)S(1)}, u32[]{:S(2)}, u32[]{:S(2)}) collective-permute-start(bf16[2048,128]{1,0:T(8,128)(2,1)S(1)} %collective-permute-done.refs_8_), channel_id=1, source_target_pairs={{0,2},{1,5},{2,0},{3,7},{4,6},{5,1},{6,4},{7,3},{8,10},{9,13},{10,... | collective-permute-start | bytes 1572872 | tf_op jit(solution)/shard_map/ppermute | solution.py:318
  38.8 16.6 %collective-permute-start.27 = (bf16[2048,128]{1,0:T(8,128)(2,1)S(1)}, bf16[2048,128]{1,0:T(8,128)(2,1)S(1)}, u32[]{:S(2)}, u32[]{:S(2)}) collective-permute-start(bf16[2048,128]{1,0:T(8,128)(2,1)S(1)} %collective-permute-done.refs_8_), channel_id=1, source_target_pairs={{0,1},{1,0},{2,3},{3,2},{4,5},{5,4},{6,7},{7,6},{8,9},{9,8},{10,11... | collective-permute-start | bytes 1572872 | tf_op jit(solution)/shard_map/ppermute | solution.py:318
  38.8 18.6 %collective-permute-start.1 = (bf16[2048,128]{1,0:T(8,128)(2,1)S(1)}, bf16[2048,128]{1,0:T(8,128)(2,1)S(1)}, u32[]{:S(2)}, u32[]{:S(2)}) collective-permute-start(bf16[2048,128]{1,0:T(8,128)(2,1)S(1)} %collective-permute-done.refs_8_), channel_id=1, source_target_pairs={{0,8},{1,9},{2,10},{3,11},{4,12},{5,13},{6,14},{7,15},{8,16},{9,17... | collective-permute-start | bytes 1572872 | tf_op jit(solution)/shard_map/ppermute | solution.py:318
  55.4 13.5 %collective-permute-start.26 = (bf16[2048,128]{1,0:T(8,128)(2,1)S(1)}, bf16[2048,128]{1,0:T(8,128)(2,1)}, u32[]{:S(2)}, u32[]{:S(2)}) collective-permute-start(bf16[2048,128]{1,0:T(8,128)(2,1)S(1)} %collective-permute-done.24.refs_9_), channel_id=1, source_target_pairs={{0,4},{1,3},{2,6},{3,1},{4,0},{5,7},{6,2},{7,5},{8,12},{9,11},{10,... | collective-permute-start | bytes 1572872 | tf_op jit(solution)/shard_map/ppermute | solution.py:318
  57.4 14.8 %collective-permute-start.2 = (bf16[2048,128]{1,0:T(8,128)(2,1)S(1)}, bf16[2048,128]{1,0:T(8,128)(2,1)}, u32[]{:S(2)}, u32[]{:S(2)}) collective-permute-start(bf16[2048,128]{1,0:T(8,128)(2,1)S(1)} %collective-permute-done.1.refs_0_), channel_id=1, source_target_pairs={{0,8},{1,9},{2,10},{3,11},{4,12},{5,13},{6,14},{7,15},{8,16},{9,17... | collective-permute-start | bytes 1572872 | tf_op jit(solution)/shard_map/ppermute | solution.py:318
  59.0 15.0 %collective-permute-start.10 = (bf16[2048,128]{1,0:T(8,128)(2,1)S(1)}, bf16[2048,128]{1,0:T(8,128)(2,1)S(1)}, u32[]{:S(2)}, u32[]{:S(2)}) collective-permute-start(bf16[2048,128]{1,0:T(8,128)(2,1)S(1)} %collective-permute-done.1.refs_0_), channel_id=1, source_target_pairs={{0,2},{1,5},{2,0},{3,7},{4,6},{5,1},{6,4},{7,3},{8,10},{9,13},{10,... | collective-permute-start | bytes 1572872 | tf_op jit(solution)/shard_map/ppermute | solution.py:318
  59.7 14.4 %collective-permute-start.13 = (bf16[2048,128]{1,0:T(8,128)(2,1)S(1)}, bf16[2048,128]{1,0:T(8,128)(2,1)}, u32[]{:S(2)}, u32[]{:S(2)}) collective-permute-start(bf16[2048,128]{1,0:T(8,128)(2,1)S(1)} %collective-permute-done.1.refs_0_), channel_id=1, source_target_pairs={{0,1},{1,0},{2,3},{3,2},{4,5},{5,4},{6,7},{7,6},{8,9},{9,8},{10,11... | collective-permute-start | bytes 1572872 | tf_op jit(solution)/shard_map/ppermute | solution.py:318
  59.7 17.7 %collective-permute-start.11 = (bf16[2048,128]{1,0:T(8,128)(2,1)S(1)}, bf16[2048,128]{1,0:T(8,128)(2,1)}, u32[]{:S(2)}, u32[]{:S(2)}) collective-permute-start(bf16[2048,128]{1,0:T(8,128)(2,1)S(1)} %collective-permute-done.1.refs_0_), channel_id=1, source_target_pairs={{0,4},{1,3},{2,6},{3,1},{4,0},{5,7},{6,2},{7,5},{8,12},{9,11},{10,... | collective-permute-start | bytes 1572872 | tf_op jit(solution)/shard_map/ppermute | solution.py:318
  72.2 13.9 %collective-permute-start.3 = (bf16[2048,128]{1,0:T(8,128)(2,1)}, bf16[2048,128]{1,0:T(8,128)(2,1)}, u32[]{:S(2)}, u32[]{:S(2)}) collective-permute-start(bf16[2048,128]{1,0:T(8,128)(2,1)} %collective-permute-done.2.refs_0_), channel_id=1, source_target_pairs={{0,2},{1,5},{2,0},{3,7},{4,6},{5,1},{6,4},{7,3},{8,10},{9,13},{10,... | collective-permute-start | bytes 1572872 | tf_op jit(solution)/shard_map/ppermute | solution.py:318
  74.0 15.2 %collective-permute-start.14 = (bf16[2048,128]{1,0:T(8,128)(2,1)S(1)}, bf16[2048,128]{1,0:T(8,128)(2,1)}, u32[]{:S(2)}, u32[]{:S(2)}) collective-permute-start(bf16[2048,128]{1,0:T(8,128)(2,1)S(1)} %collective-permute-done.10.refs_1_), channel_id=1, source_target_pairs={{0,1},{1,0},{2,3},{3,2},{4,5},{5,4},{6,7},{7,6},{8,9},{9,8},{10,11... | collective-permute-start | bytes 1572872 | tf_op jit(solution)/shard_map/ppermute | solution.py:318
  74.1 15.6 %collective-permute-start.12 = (bf16[2048,128]{1,0:T(8,128)(2,1)S(1)}, bf16[2048,128]{1,0:T(8,128)(2,1)}, u32[]{:S(2)}, u32[]{:S(2)}) collective-permute-start(bf16[2048,128]{1,0:T(8,128)(2,1)S(1)} %collective-permute-done.10.refs_1_), channel_id=1, source_target_pairs={{0,4},{1,3},{2,6},{3,1},{4,0},{5,7},{6,2},{7,5},{8,12},{9,11},{10,... | collective-permute-start | bytes 1572872 | tf_op jit(solution)/shard_map/ppermute | solution.py:318
  77.4 15.3 %collective-permute-start.4 = (bf16[2048,128]{1,0:T(8,128)(2,1)}, bf16[2048,128]{1,0:T(8,128)(2,1)}, u32[]{:S(2)}, u32[]{:S(2)}) collective-permute-start(bf16[2048,128]{1,0:T(8,128)(2,1)} %collective-permute-done.2.refs_0_), channel_id=1, source_target_pairs={{0,4},{1,3},{2,6},{3,1},{4,0},{5,7},{6,2},{7,5},{8,12},{9,11},{10,... | collective-permute-start | bytes 1572872 | tf_op jit(solution)/shard_map/ppermute | solution.py:318
  86.1 12.3 %collective-permute-start.5 = (bf16[2048,128]{1,0:T(8,128)(2,1)}, bf16[2048,128]{1,0:T(8,128)(2,1)}, u32[]{:S(2)}, u32[]{:S(2)}) collective-permute-start(bf16[2048,128]{1,0:T(8,128)(2,1)} %collective-permute-done.3.refs_1_), channel_id=1, source_target_pairs={{0,4},{1,3},{2,6},{3,1},{4,0},{5,7},{6,2},{7,5},{8,12},{9,11},{10,... | collective-permute-start | bytes 1572872 | tf_op jit(solution)/shard_map/ppermute | solution.py:318
  89.0 57.5 %collective-permute-start.6 = (bf16[2048,128]{1,0:T(8,128)(2,1)}, bf16[2048,128]{1,0:T(8,128)(2,1)}, u32[]{:S(2)}, u32[]{:S(2)}) collective-permute-start(bf16[2048,128]{1,0:T(8,128)(2,1)} %collective-permute-done.2.refs_0_), channel_id=1, source_target_pairs={{0,1},{1,0},{2,3},{3,2},{4,5},{5,4},{6,7},{7,6},{8,9},{9,8},{10,11... | collective-permute-start | bytes 1572872 | tf_op jit(solution)/shard_map/ppermute | solution.py:318
  89.1 57.4 %collective-permute-start.7 = (bf16[2048,128]{1,0:T(8,128)(2,1)}, bf16[2048,128]{1,0:T(8,128)(2,1)}, u32[]{:S(2)}, u32[]{:S(2)}) collective-permute-start(bf16[2048,128]{1,0:T(8,128)(2,1)} %collective-permute-done.3.refs_1_), channel_id=1, source_target_pairs={{0,1},{1,0},{2,3},{3,2},{4,5},{5,4},{6,7},{7,6},{8,9},{9,8},{10,11... | collective-permute-start | bytes 1572872 | tf_op jit(solution)/shard_map/ppermute | solution.py:318
  89.6 39.3 %collective-permute-start.16 = (bf16[2048,128]{1,0:T(8,128)(2,1)}, bf16[2048,128]{1,0:T(8,128)(2,1)}, u32[]{:S(2)}, u32[]{:S(2)}) collective-permute-start(bf16[2048,128]{1,0:T(8,128)(2,1)} %collective-permute-done.12.refs_3_), channel_id=1, source_target_pairs={{0,1},{1,0},{2,3},{3,2},{4,5},{5,4},{6,7},{7,6},{8,9},{9,8},{10,11... | collective-permute-start | bytes 1572872 | tf_op jit(solution)/shard_map/ppermute | solution.py:318
  92.7 53.8 %collective-permute-start.8 = (bf16[2048,128]{1,0:T(8,128)(2,1)}, bf16[2048,128]{1,0:T(8,128)(2,1)}, u32[]{:S(2)}, u32[]{:S(2)}) collective-permute-start(bf16[2048,128]{1,0:T(8,128)(2,1)} %collective-permute-done.4.refs_2_), channel_id=1, source_target_pairs={{0,1},{1,0},{2,3},{3,2},{4,5},{5,4},{6,7},{7,6},{8,9},{9,8},{10,11... | collective-permute-start | bytes 1572872 | tf_op jit(solution)/shard_map/ppermute | solution.py:318
  98.4 48.2 %collective-permute-start.9 = (bf16[2048,128]{1,0:T(8,128)(2,1)}, bf16[2048,128]{1,0:T(8,128)(2,1)}, u32[]{:S(2)}, u32[]{:S(2)}) collective-permute-start(bf16[2048,128]{1,0:T(8,128)(2,1)} %collective-permute-done.5.refs_3_), channel_id=1, source_target_pairs={{0,1},{1,0},{2,3},{3,2},{4,5},{5,4},{6,7},{7,6},{8,9},{9,8},{10,11... | collective-permute-start | bytes 1572872 | tf_op jit(solution)/shard_map/ppermute | solution.py:318
  (26 other events, 749.5 us)

commit v2 on v1

v2 whole, which is shorter than its diff:
```python
import functools

import jax
import jax.numpy as jnp
from jax import lax
from jax.experimental import pallas as pl
from jax.experimental.pallas import tpu as pltpu
from jax.sharding import PartitionSpec as P

F = 26
BLOCK = 128
VECS = F + 1
LANES = 128
CHAINS = 4
UNROLL = 8
VMEM = 32 << 20
SMEM_SPEC = pl.BlockSpec(memory_space=pltpu.SMEM)
ANY_SPEC = pl.BlockSpec(memory_space=pl.ANY)
HBM_SPEC = pl.BlockSpec(memory_space=pltpu.HBM)
VMEM_SPEC = pl.BlockSpec(memory_space=pltpu.VMEM)


def fill_kernel(slot_ref, block_ref, cache_ref, fills_ref, out_ref, sem):
    def of_block(ref, index):
        return ref.at[pl.ds(pl.multiple_of(index * BLOCK, BLOCK), BLOCK)]

    n_slots = out_ref.shape[0] // BLOCK
    n_fills = slot_ref.shape[0]

    def kept(index):
        hit = slot_ref[0] == index
        for k in range(1, n_fills):
            hit = jnp.logical_or(hit, slot_ref[k] == index)
        return jnp.logical_not(hit)

    def cache_copy(index):
        return pltpu.make_async_copy(of_block(cache_ref, index), of_block(out_ref, index), sem.at[index])

    def fill_copy(k):
        slot = jnp.minimum(slot_ref[k], n_slots - 1)
        return pltpu.make_async_copy(
            of_block(fills_ref, block_ref[k]), of_block(out_ref, slot), sem.at[n_slots + k]
        )

    for k in range(n_fills):
        pl.when(slot_ref[k] < n_slots)(lambda k=k: fill_copy(k).start())
    for index in range(n_slots):
        pl.when(kept(index))(lambda index=index: cache_copy(index).start())
    for index in range(n_slots):
        pl.when(kept(index))(lambda index=index: cache_copy(index).wait())
    for k in range(n_fills):
        pl.when(slot_ref[k] < n_slots)(lambda k=k: fill_copy(k).wait())


def fill(cache_rows, fills, miss_slot, fill_block):
    n_sems = cache_rows.shape[0] // BLOCK + miss_slot.shape[0]
    return pl.pallas_call(
        fill_kernel,
        out_shape=jax.ShapeDtypeStruct(cache_rows.shape, cache_rows.dtype),
        in_specs=[SMEM_SPEC] * 2 + [ANY_SPEC] * 2,
        out_specs=VMEM_SPEC,
        scratch_shapes=[pltpu.SemaphoreType.DMA((n_sems,))],
        name="fill",
    )(miss_slot, fill_block, cache_rows, fills)


def gate_kernel(*refs):
    pass


def gate(arrays, after):
    n_arrays = len(arrays)
    return pl.pallas_call(
        gate_kernel,
        out_shape=[jax.ShapeDtypeStruct(one.shape, one.dtype) for one in arrays],
        in_specs=[HBM_SPEC] * n_arrays + [SMEM_SPEC],
        out_specs=[HBM_SPEC] * n_arrays,
        input_output_aliases={index: index for index in range(n_arrays)},
        compiler_params=pltpu.CompilerParams(vmem_limit_bytes=1 << 20),
        name="gate",
    )(*arrays, after)


def pool_shards(first, entry_refs, entry_held, count_ref, shards, sems, held, table, sums):
    copies = [
        pltpu.make_async_copy(ref.at[pl.ds(first, 8)], to, sems.at[len(shards) + index])
        for index, (ref, to) in enumerate(zip(entry_refs, entry_held))
    ]
    copies += [pltpu.make_async_copy(ref, held.at[s], sems.at[s]) for s, ref in enumerate(shards)]
    for copy in copies:
        copy.start()
    yield
    for copy in copies[:2]:
        copy.wait()
    slot_ref, bag_ref = entry_held
    skipped = 2 if first == 0 else 0
    for s, copy in enumerate(copies[2:]):
        copy.wait()
        table[...] = held[s].astype(jnp.float32)
        row = s + skipped

        def add_entries(step, _):
            first = step * UNROLL
            for group in range(UNROLL // CHAINS):
                entries = [first + group * CHAINS + k for k in range(CHAINS)]
                slots = [slot_ref[row, e] for e in entries]
                bags = [bag_ref[row, e] for e in entries]
                rows = [table[pl.ds(slot, 1), :] for slot in slots]
                olds = [sums[k][pl.ds(bags[k], 1), :] for k in range(CHAINS)]
                for k in range(CHAINS):
                    sums[k][pl.ds(bags[k], 1), :] = olds[k] + rows[k]
            return 0

        lax.fori_loop(0, count_ref[first + row], add_entries, 0)


def pool_kernel(first, n_shards, is_first, count_ref, slot_ref, bag_ref, *refs):
    shards, refs = refs[:n_shards], refs[n_shards:]
    if not is_first:
        refs = refs[CHAINS:]
    sums, (done, *entry_held, held, table, sems) = refs[:CHAINS], refs[CHAINS:]
    pooling = pool_shards(
        first, (slot_ref, bag_ref), entry_held, count_ref, shards, sems, held, table, sums
    )
    next(pooling)
    if is_first:
        for one in sums:
            one[...] = jnp.zeros_like(one)
    for _ in pooling:
        pass
    done[0] = 0


def interact(sums, dense_ref, masked, queries):
    lane = lax.broadcasted_iota(jnp.int32, (8, 256), 1)
    row = lax.broadcasted_iota(jnp.int32, (8, 256), 0)
    own_query = (lane & 7) == row

    def sixteen_queries(step, _):
        dense = dense_ref[pl.ds(pl.multiple_of(step * 16, 16), 16), :].astype(jnp.float32)
        halves = []
        for half in range(2):
            query = pl.multiple_of(step * 16 + half * 8, 8)
            vectors = [dense[half * 8 : half * 8 + 8]]
            for feature in range(F):
                rows = pl.ds(pl.multiple_of(feature * queries + query, 8), 8)
                total = sums[0][rows, :]
                for one in sums[1:]:
                    total = total + one[rows, :]
                vectors.append(total)
            vectors += [jnp.zeros((8, LANES), jnp.float32)] * (32 - VECS)
            stacked = jnp.concatenate(vectors, axis=0).astype(jnp.bfloat16)
            halves.append(
                lax.dot_general(
                    stacked, stacked, (((1,), (1,)), ((), ())), preferred_element_type=jnp.float32
                )
            )
        for i in range(F):
            pair = [
                jnp.where(own_query, products[8 * i : 8 * i + 8, :], 0.0) for products in halves
            ]
            masked[i, pl.ds(pl.multiple_of(step * 16, 16), 16), :] = jnp.concatenate(
                pair, axis=0
            ).astype(jnp.bfloat16)
        return 0

    lax.fori_loop(0, queries // 16, sixteen_queries, 0)


def inter_columns(masked, dense_ref, inter, queries):
    spread = lax.broadcasted_iota(jnp.int32, (256, LANES), 0) // 8
    vector = lax.broadcasted_iota(jnp.int32, (256, LANES), 1)
    pick = jnp.where(spread == vector, 1.0, 0.0).astype(jnp.bfloat16)
    lane = lax.broadcasted_iota(jnp.int32, (queries, LANES), 1)
    tiles = [jnp.zeros((queries, LANES), jnp.float32) for _ in range(3)]
    first = 0
    for i in range(F):
        length = F - i
        picked = jnp.dot(masked[i], pick, preferred_element_type=jnp.float32)
        shift = (first - (i + 1)) % LANES
        if shift:
            picked = pltpu.roll(picked, shift, 1)
        for tile in range(3):
            low, high = max(first, tile * LANES), min(first + length, (tile + 1) * LANES)
            if low < high:
                inside = jnp.logical_and(lane >= low - tile * LANES, lane < high - tile * LANES)
                tiles[tile] = jnp.where(inside, picked, tiles[tile])
        first += length
    inter[:, :LANES] = dense_ref[...]
    for tile in range(3):
        inter[:, (tile + 1) * LANES : (tile + 2) * LANES] = tiles[tile].astype(jnp.bfloat16)


def final_kernel(first, n_shards, with_head, count_ref, slot_ref, bag_ref, *refs):
    shards, refs = refs[:n_shards], refs[n_shards:]
    old_sums, dense_ref, refs = refs[:CHAINS], refs[CHAINS], refs[CHAINS + 1 :]
    if with_head:
        w_first, w_second, w_out, logits, *refs = refs
    else:
        inter, *refs = refs
    refs = refs[CHAINS:]
    if with_head:
        inter, first_held, second_held, weight_sems, *refs = refs
        weights = [
            pltpu.make_async_copy(w_first, first_held, weight_sems.at[0]),
            pltpu.make_async_copy(w_second, second_held, weight_sems.at[1]),
        ]
        for copy in weights:
            copy.start()
    masked, *entry_held, held, table, sems = refs
    queries = dense_ref.shape[0]
    for _ in pool_shards(
        first, (slot_ref, bag_ref), entry_held, count_ref, shards, sems, held, table, old_sums
    ):
        pass
    interact(old_sums, dense_ref, masked, queries)
    inter_columns(masked, dense_ref, inter, queries)
    if not with_head:
        return
    for copy in weights:
        copy.wait()
    step = LANES
    inputs = first_held.shape[0]
    for part in range(queries // step):
        rows = slice(part * step, (part + 1) * step)
        hidden = jnp.dot(inter[rows, :inputs], first_held[...], preferred_element_type=jnp.float32)
        hidden = jnp.maximum(hidden, 0.0).astype(jnp.bfloat16)
        second = jnp.dot(hidden, second_held[...], preferred_element_type=jnp.float32)
        scored = jnp.maximum(second, 0.0) * w_out[...]
        folded = scored[:, :LANES]
        for tile in range(1, scored.shape[1] // LANES):
            folded = folded + scored[:, tile * LANES : (tile + 1) * LANES]
        logits[rows] = jnp.sum(folded.T, axis=0)


def pool_scratch(n_shards, shard_rows, cap):
    return [
        pltpu.SMEM((8, cap), jnp.int32),
        pltpu.SMEM((8, cap), jnp.int32),
        pltpu.VMEM((n_shards, shard_rows, LANES), jnp.bfloat16),
        pltpu.VMEM((shard_rows, LANES), jnp.float32),
        pltpu.SemaphoreType.DMA((n_shards + 2,)),
    ]


def pool(first, entries, shards, sums, sum_rows):
    n_shards = len(shards)
    is_first = sums is None
    sums = [] if is_first else sums
    *sums, done = pl.pallas_call(
        functools.partial(pool_kernel, first, n_shards, is_first),
        out_shape=[pltpu.VMEM((sum_rows, LANES), jnp.float32)] * CHAINS
        + [jax.ShapeDtypeStruct((1,), jnp.int32)],
        in_specs=[SMEM_SPEC] + [HBM_SPEC] * (2 + n_shards) + [VMEM_SPEC] * len(sums),
        out_specs=[VMEM_SPEC] * CHAINS + [SMEM_SPEC],
        input_output_aliases={3 + n_shards + k: k for k in range(len(sums))},
        scratch_shapes=pool_scratch(n_shards, shards[0].shape[0], entries[1].shape[1]),
        compiler_params=pltpu.CompilerParams(vmem_limit_bytes=VMEM),
        cost_estimate=pl.CostEstimate(flops=0, bytes_accessed=n_shards * 6_000_000, transcendentals=0),
        name="pool",
    )(*entries, *shards, *sums)
    return sums, done


def finish(first, entries, shards, sums, dense_rows, head):
    n_shards = len(shards)
    queries = dense_rows.shape[0]
    width = 4 * LANES
    masked = pltpu.VMEM((F, queries, 256), jnp.bfloat16)
    if head is None:
        head_args, head_specs = [], []
        out_shape = jax.ShapeDtypeStruct((queries, width), jnp.bfloat16)
        scratch = [masked]
    else:
        head_args, head_specs = list(head), [HBM_SPEC, HBM_SPEC, VMEM_SPEC]
        out_shape = jax.ShapeDtypeStruct((queries,), jnp.float32)
        scratch = [
            pltpu.VMEM((queries, width), jnp.bfloat16),
            pltpu.VMEM(head[0].shape, jnp.bfloat16),
            pltpu.VMEM(head[1].shape, jnp.bfloat16),
            pltpu.SemaphoreType.DMA((2,)),
            masked,
        ]
    out = pl.pallas_call(
        functools.partial(final_kernel, first, n_shards, head is not None),
        out_shape=[out_shape] + [pltpu.VMEM(one.shape, one.dtype) for one in sums],
        in_specs=[SMEM_SPEC] + [HBM_SPEC] * (2 + n_shards) + [VMEM_SPEC] * (CHAINS + 1) + head_specs,
        out_specs=[VMEM_SPEC] * (CHAINS + 1),
        input_output_aliases={3 + n_shards + k: 1 + k for k in range(CHAINS)},
        scratch_shapes=scratch + pool_scratch(n_shards, shards[0].shape[0], entries[1].shape[1]),
        compiler_params=pltpu.CompilerParams(vmem_limit_bytes=VMEM),
        name="finish",
    )(*entries, *shards, *sums, dense_rows, *head_args)
    return out[0]


def per_device(
    n_planes,
    cache_rows,
    store_rows,
    miss_block,
    miss_slot,
    lookup_slot,
    lookup_bag,
    dense_rows,
    w_first,
    w_second,
    w_out,
):
    emb_width = cache_rows.shape[1]
    queries = dense_rows.shape[0]
    bags = queries * F
    owners = lax.axis_size("owner")
    n_shards = n_planes * 8

    if owners == 1:
        fills, fill_block = store_rows, miss_block[0]
    else:
        fills = store_rows.reshape(-1, BLOCK, emb_width)[miss_block[0]]
        fills = lax.all_gather(fills, "owner", axis=0, tiled=True)
        fill_block = jnp.arange(fills.shape[0], dtype=jnp.int32)
        fills = fills.reshape(-1, emb_width)
    own = fill(cache_rows, fills, miss_slot[0], fill_block)

    def device(z, y, x, core):
        return ((z * 2 + y) * 2 + x) * 2 + core

    def hop(move):
        pairs = []
        for index in range(n_shards):
            at = (index // 8, index // 4 % 2, index // 2 % 2, index % 2)
            pairs.append((index, device(*move(*at))))
        return lambda array: lax.ppermute(array, "cache", pairs)

    next_plane = hop(lambda z, y, x, core: ((z + 1) % n_planes, y, x, core))
    first_hop = hop(lambda z, y, x, core: (z, y, 1 - x, core) if core == 0 else (z, 1 - y, x, core))
    second_hop = hop(lambda z, y, x, core: (z, 1 - y, x, core) if core == 0 else (z, y, 1 - x, core))
    other_core = hop(lambda z, y, x, core: (z, y, x, 1 - core))

    me = lax.axis_index("cache")
    z, y, x, core = me // 8, me // 4 % 2, me // 2 % 2, me % 2

    def origin(shift, flip_first, flip_second, side):
        flip_x = jnp.where(side == 0, flip_first, flip_second)
        flip_y = jnp.where(side == 0, flip_second, flip_first)
        return device((z - shift) % n_planes, y ^ flip_y, x ^ flip_x, side)

    def both_cores(shift, *flips):
        return [origin(shift, *flips, side) for side in (core, 1 - core)]

    order = []
    for shift in range(n_planes + 1):
        before, now = max(shift - 1, 0), min(shift, n_planes - 1)
        order += both_cores(before, 1, 1)
        for flips in ((0, 0), (1, 0), (0, 1)):
            order += both_cores(now, *flips)
    order = jnp.stack(order)
    cap = lookup_slot.shape[2]
    cap += -cap % UNROLL
    spare = ((0, 0), (0, cap - lookup_slot.shape[2]))
    slots = jnp.pad(lookup_slot[0], spare)[order]
    bag_ids = jnp.pad(lookup_bag[0], spare, constant_values=bags)[order]
    used = jnp.sum((bag_ids < bags).astype(jnp.int32), axis=1)
    steps = (used + UNROLL - 1) // UNROLL
    sum_rows = bags + 8
    places = jnp.where(bag_ids < bags, bag_ids % F * queries + bag_ids // F, bags)
    entries = (steps, slots, places)

    sums, far = None, []
    piece, crossed, turned = own, first_hop(own), second_hop(own)
    next_piece = next_plane(piece)
    for shift in range(n_planes):
        near = [piece, other_core(piece), crossed, other_core(crossed), turned, other_core(turned)]
        next_far = second_hop(crossed)
        if shift < n_planes - 1:
            next_crossed, next_turned = first_hop(next_piece), second_hop(next_piece)
            passed = [next_piece, next_crossed, next_turned]
            if shift < n_planes - 2:
                passed.append(next_plane(next_piece))
        sums, done = pool(8 * shift, entries, far + near, sums, sum_rows)
        if shift < n_planes - 1:
            next_far, piece, crossed, turned, *next_piece = gate([next_far] + passed, done)
            next_piece = next_piece[0] if next_piece else None
        far = [next_far, other_core(next_far)]
    args = (8 * n_planes, entries, far, sums, dense_rows)
    if owners == 1:
        return finish(*args, (w_first, w_second, w_out.reshape(1, -1)))
    inter_in = finish(*args, None)[:, : w_first.shape[0]]
    group_inputs = lax.all_gather(inter_in, "owner", axis=0, tiled=True)
    hidden = jax.nn.relu(jnp.dot(group_inputs, w_first, preferred_element_type=jnp.float32))
    second = lax.psum_scatter(
        jnp.dot(hidden.astype(jnp.bfloat16), w_second, preferred_element_type=jnp.float32),
        "owner",
        scatter_dimension=0,
        tiled=True,
    )
    return jnp.sum(jax.nn.relu(second) * w_out, axis=1)


def solution(mesh):
    in_specs = (
        P(("rep", "cache"), None),
        P(("rep", "cache", "owner"), None),
        P(("rep", "cache", "owner"), None),
        P(("rep", "cache"), None),
        P(("rep", "cache", "owner"), None, None),
        P(("rep", "cache", "owner"), None, None),
        P(("rep", "cache", "owner"), None),
        P(None, "owner"),
        P("owner", None),
        P(),
    )
    out_specs = P(("rep", "cache", "owner"))
    return jax.shard_map(
        functools.partial(per_device, mesh.shape["cache"] // 8),
        mesh=mesh,
        in_specs=in_specs,
        out_specs=out_specs,
        check_vma=False,
    )
```

time: 175 us -> 130 us (0.74)
  waiting for transfers between devices: 54.7 us -> 22.2 us
  Pallas kernels: 84.7 us -> 77.1 us
  starting transfers between devices: 23.8 us -> 21.6 us
    ppermute x31, waiting for transfers between devices: 54.7 us -> 22.2 us  [hop(): return lambda array: lax.ppermute(array, 'cache', pairs)]
    pallas_call x1, Pallas kernels: 17.9 us -> 2.77 us  [fill(): pl.pallas_call(fill_kernel, out_shape=jax.ShapeDtypeStruct(cache_rows.sha...]
    pallas_call x3 -> x8, Pallas kernels: 66.8 us -> 74.3 us  [the longest x4 57.2 us: pool(): pl.pallas_call(functools.partial(pool_kernel, first, n_shards, is_first),...]
    unnamed x38, local copies, waits for them, and re-layouts: 0.07 us -> 5.58 us
    reshape x6 -> x0, local copies, waits for them, and re-layouts: 4.14 us -> none  [per_device(): args = (slots[part].reshape(-1), places[part].reshape(-1), steps[part])]
    ppermute x31, starting transfers between devices: 23.8 us -> 21.6 us  [hop(): return lambda array: lax.ppermute(array, 'cache', pairs)]
  transfers between devices with their start and end apart: 31 -> 31, of which waited for: 10 -> 8; matrix products, arithmetic and copies ran while one was open for 5% -> 2% of each run, Pallas kernels for 24% -> 44%
where the time goes in v2:
time: 130 us; the launch traced here: 129 us
  Pallas kernels  77.1 us (59%)
  waiting for transfers between devices  22.2 us (17%)
  starting transfers between devices  21.6 us (17%)
  local copies, waits for them, and re-layouts  7.91 us (6%)
    pallas_call x4, Pallas kernels, pool(): pl.pallas_call(functools.partial(pool_kernel, first, n_shards, is_first),...  57.2 us
    ppermute x31, waiting for transfers between devices, hop(): return lambda array: lax.ppermute(array, 'cache', pairs)  22.2 us
    ppermute x31, starting transfers between devices, hop(): return lambda array: lax.ppermute(array, 'cache', pairs)  21.6 us
    pallas_call x1, Pallas kernels, finish(): pl.pallas_call(functools.partial(final_kernel, first, n_shards, head is n...  15.1 us
    unnamed x38, local copies, waits for them, and re-layouts  5.58 us
    pallas_call x1, Pallas kernels, fill(): pl.pallas_call(fill_kernel, out_shape=jax.ShapeDtypeStruct(cache_rows.sha...  2.77 us
  transfers between devices with their start and end apart: 31, of which 8 were waited for; matrix products, arithmetic and copies ran while one was open for 2% of the time, Pallas kernels for 44%

profile of v2, /device:TPU:0, one launch (start us, length us, event | category | flops | bytes accessed | tf_op | source)
XLA Modules:
  0.0 129.5 jit_solution(4838828335012661480)
XLA Ops:
  0.0 2.8 %fill.1.refs_0_ = bf16[2048,128]{1,0:T(8,128)(2,1)} custom-call(s32[2]{0:T(128)} %bitcast.42, s32[2]{0:T(128)} %bitcast.43, bf16[2048,128]{1,0:T(8,128)(2,1)} %cache_ref.1, bf16[1024,128]{1,0:T(8,128)(2,1)} %fills_ref.1), custom_call_target="tpu_custom_call" | custom-call | tf_op jit(solution)/shard_map/fill/pallas_call | solution.py:57
  2.8 3.0 %collective-permute-start.8 = (bf16[2048,128]{1,0:T(8,128)(2,1)}, bf16[2048,128]{1,0:T(8,128)(2,1)S(1)}, u32[]{:S(2)}, u32[]{:S(2)}) collective-permute-start(bf16[2048,128]{1,0:T(8,128)(2,1)} %fill.1.refs_0_), channel_id=1, source_target_pairs={{0,4},{1,3},{2,6},{3,1},{4,0},{5,7},{6,2},{7,5},{8,12},{9,11},{10,... | collective-permute-start | bytes 1572872 | tf_op jit(solution)/shard_map/ppermute | solution.py:333
  5.8 1.6 %collective-permute-start.2 = (bf16[2048,128]{1,0:T(8,128)(2,1)}, bf16[2048,128]{1,0:T(8,128)(2,1)S(1)}, u32[]{:S(2)}, u32[]{:S(2)}) collective-permute-start(bf16[2048,128]{1,0:T(8,128)(2,1)} %fill.1.refs_0_), channel_id=1, source_target_pairs={{0,8},{1,9},{2,10},{3,11},{4,12},{5,13},{6,14},{7,15},{8,16},{9,17... | collective-permute-start | bytes 1572872 | tf_op jit(solution)/shard_map/ppermute | solution.py:333
  7.4 1.5 %collective-permute-start = (bf16[2048,128]{1,0:T(8,128)(2,1)}, bf16[2048,128]{1,0:T(8,128)(2,1)S(1)}, u32[]{:S(2)}, u32[]{:S(2)}) collective-permute-start(bf16[2048,128]{1,0:T(8,128)(2,1)} %fill.1.refs_0_), channel_id=1, source_target_pairs={{0,2},{1,5},{2,0},{3,7},{4,6},{5,1},{6,4},{7,3},{8,10},{9,13},{10,... | collective-permute-start | bytes 1572872 | tf_op jit(solution)/shard_map/ppermute | solution.py:333
  8.9 7.9 %collective-permute-done.8.refs_4_ = bf16[2048,128]{1,0:T(8,128)(2,1)S(1)} collective-permute-done((bf16[2048,128]{1,0:T(8,128)(2,1)}, bf16[2048,128]{1,0:T(8,128)(2,1)S(1)}, u32[]{:S(2)}, u32[]{:S(2)}) %collective-permute-start.8) | collective-permute-done | bytes 524320 | tf_op jit(solution)/shard_map/ppermute | solution.py:333
  16.9 4.4 %collective-permute-done.2.refs_1_ = bf16[2048,128]{1,0:T(8,128)(2,1)S(1)} collective-permute-done((bf16[2048,128]{1,0:T(8,128)(2,1)}, bf16[2048,128]{1,0:T(8,128)(2,1)S(1)}, u32[]{:S(2)}, u32[]{:S(2)}) %collective-permute-start.2) | collective-permute-done | bytes 524320 | tf_op jit(solution)/shard_map/ppermute | solution.py:333
  21.3 1.5 %collective-permute-start.4 = (bf16[2048,128]{1,0:T(8,128)(2,1)S(1)}, bf16[2048,128]{1,0:T(8,128)(2,1)S(1)}, u32[]{:S(2)}, u32[]{:S(2)}) collective-permute-start(bf16[2048,128]{1,0:T(8,128)(2,1)S(1)} %collective-permute-done.2.refs_1_), channel_id=1, source_target_pairs={{0,4},{1,3},{2,6},{3,1},{4,0},{5,7},{6,2},{7,5},{8,12},{9,11},{10,... | collective-permute-start | bytes 1572872 | tf_op jit(solution)/shard_map/ppermute | solution.py:333
  25.4 1.6 %gather_fusion = s32[40,624]{1,0:T(8,128)S(1)} fusion(s32[32,624]{1,0:T(8,128)} %bitcast.41, s32[1024]{0:T(1024)S(1)} %pad_clamp_fusion), kind=kCustom, calls=%fused_computation | custom fusion | bytes 199840 | tf_op jit(solution)/shard_map/gather | solution.py:362
  27.2 1.0 copy-done.7
  28.2 1.0 copy-done.9
  29.3 12.8 %pool.4 = (f32[9992,128]{1,0:T(8,128)S(1)}, f32[9992,128]{1,0:T(8,128)S(1)}, f32[9992,128]{1,0:T(8,128)S(1)}, f32[9992,128]{1,0:T(8,128)S(1)}, s32[1]{0:T(128)}) custom-call(s32[40]{0:T(128)S(1)} %and_select_fusion.count_ref, s32[40,624]{1,0:T(8,128)S(1)} %gather_fusion.1, s32[40,624]{1,0:T(8,128)S(1)} %get-tuple-element.73.bag_ref, ...), custom_call_target="tpu_custom_call" | custom-call | bytes 36000000 | tf_op jit(solution)/shard_map/pool/pallas_call | solution.py:250
  42.8 1.2 collective-permute-start.14
  44.6 0.8 collective-permute-start.10
  46.3 0.9 collective-permute-start.12
  47.1 2.3 %collective-permute-start.11 = (bf16[2048,128]{1,0:T(8,128)(2,1)S(1)}, bf16[2048,128]{1,0:T(8,128)(2,1)S(1)}, u32[]{:S(2)}, u32[]{:S(2)}) collective-permute-start(bf16[2048,128]{1,0:T(8,128)(2,1)S(1)} %get-tuple-element.41.refs_1_), channel_id=1, source_target_pairs={{0,2},{1,5},{2,0},{3,7},{4,6},{5,1},{6,4},{7,3},{8,10},{9,13},{10,... | collective-permute-start | bytes 1572872 | tf_op jit(solution)/shard_map/ppermute | solution.py:333
  50.2 13.3 %pool.5 = (f32[9992,128]{1,0:T(8,128)S(1)}, f32[9992,128]{1,0:T(8,128)S(1)}, f32[9992,128]{1,0:T(8,128)S(1)}, f32[9992,128]{1,0:T(8,128)S(1)}, s32[1]{0:T(128)}) custom-call(s32[40]{0:T(128)S(1)} %and_select_fusion.count_ref, s32[40,624]{1,0:T(8,128)S(1)} %gather_fusion.1, ...), custom_call_target="tpu_custom_call", output_to_operand_aliasing={{0}: (11, {}), {1}: (12, {}), {2}: (13, {}), {3}: (14, {})} | custom-call | bytes 48000000 | tf_op jit(solution)/shard_map/pool/pallas_call | solution.py:250
  63.6 1.4 %collective-permute-done.12.refs_3_ = bf16[2048,128]{1,0:T(8,128)(2,1)S(1)} collective-permute-done((bf16[2048,128]{1,0:T(8,128)(2,1)S(1)}, bf16[2048,128]{1,0:T(8,128)(2,1)S(1)}, u32[]{:S(2)}, u32[]{:S(2)}) %collective-permute-start.12) | collective-permute-done | bytes 524320 | tf_op jit(solution)/shard_map/ppermute | solution.py:333
  67.6 1.1 collective-permute-start.20
  68.8 1.5 %collective-permute-start.19 = (bf16[2048,128]{1,0:T(8,128)(2,1)S(1)}, bf16[2048,128]{1,0:T(8,128)(2,1)S(1)}, u32[]{:S(2)}, u32[]{:S(2)}) collective-permute-start(bf16[2048,128]{1,0:T(8,128)(2,1)S(1)} %get-tuple-element.51.refs_1_), channel_id=1, source_target_pairs={{0,2},{1,5},{2,0},{3,7},{4,6},{5,1},{6,4},{7,3},{8,10},{9,13},{10,... | collective-permute-start | bytes 1572872 | tf_op jit(solution)/shard_map/ppermute | solution.py:333
  71.3 15.1 %pool.6 = (f32[9992,128]{1,0:T(8,128)S(1)}, f32[9992,128]{1,0:T(8,128)S(1)}, f32[9992,128]{1,0:T(8,128)S(1)}, f32[9992,128]{1,0:T(8,128)S(1)}, s32[1]{0:T(128)}) custom-call(s32[40]{0:T(128)S(1)} %and_select_fusion.count_ref, s32[40,624]{1,0:T(8,128)S(1)} %gather_fusion.1, ...), custom_call_target="tpu_custom_call", output_to_operand_aliasing={{0}: (11, {}), {1}: (12, {}), {2}: (13, {}), {3}: (14, {})} | custom-call | bytes 48000000 | tf_op jit(solution)/shard_map/pool/pallas_call | solution.py:250
  87.9 0.9 collective-permute-start.25
  89.8 7.3 %collective-permute-done.25.refs_0_ = bf16[2048,128]{1,0:T(8,128)(2,1)S(1)} collective-permute-done((bf16[2048,128]{1,0:T(8,128)(2,1)S(1)}, bf16[2048,128]{1,0:T(8,128)(2,1)S(1)}, u32[]{:S(2)}, u32[]{:S(2)}) %collective-permute-start.25) | collective-permute-done | bytes 524320 | tf_op jit(solution)/shard_map/ppermute | solution.py:333
  98.1 16.0 %pool.7 = (f32[9992,128]{1,0:T(8,128)S(1)}, f32[9992,128]{1,0:T(8,128)S(1)}, f32[9992,128]{1,0:T(8,128)S(1)}, f32[9992,128]{1,0:T(8,128)S(1)}, s32[1]{0:T(128)}) custom-call(s32[40]{0:T(128)S(1)} %and_select_fusion.count_ref, s32[40,624]{1,0:T(8,128)S(1)} %gather_fusion.1, ...), custom_call_target="tpu_custom_call", output_to_operand_aliasing={{0}: (11, {}), {1}: (12, {}), {2}: (13, {}), {3}: (14, {})} | custom-call | bytes 48000000 | tf_op jit(solution)/shard_map/pool/pallas_call | solution.py:250
  114.2 15.1 %finish.1 = (f32[384]{0:T(512)}, f32[9992,128]{1,0:T(8,128)S(1)}, f32[9992,128]{1,0:T(8,128)S(1)}, f32[9992,128]{1,0:T(8,128)S(1)}, f32[9992,128]{1,0:T(8,128)S(1)}) custom-call(s32[40]{0:T(128)S(1)} %and_select_fusion.count_ref, s32[40,624]{1,0:T(8,128)S(1)} %gather_fusion.1, ...), custom_call_target="tpu_custom_call", output_to_operand_aliasing={{1}: (5, {}), {2}: (6, {}), {3}: (7, {}), {4}: (8, {})} | custom-call | tf_op jit(solution)/shard_map/finish/pallas_call | solution.py:284
  (92 shorter events, 12.9 us)
Async XLA Ops:
  2.8 14.0 %collective-permute-start.8 = (bf16[2048,128]{1,0:T(8,128)(2,1)}, bf16[2048,128]{1,0:T(8,128)(2,1)S(1)}, u32[]{:S(2)}, u32[]{:S(2)}) collective-permute-start(bf16[2048,128]{1,0:T(8,128)(2,1)} %fill.1.refs_0_), channel_id=1, source_target_pairs={{0,4},{1,3},{2,6},{3,1},{4,0},{5,7},{6,2},{7,5},{8,12},{9,11},{10,... | collective-permute-start | bytes 1572872 | tf_op jit(solution)/shard_map/ppermute | solution.py:333
  5.8 15.5 %collective-permute-start.2 = (bf16[2048,128]{1,0:T(8,128)(2,1)}, bf16[2048,128]{1,0:T(8,128)(2,1)S(1)}, u32[]{:S(2)}, u32[]{:S(2)}) collective-permute-start(bf16[2048,128]{1,0:T(8,128)(2,1)} %fill.1.refs_0_), channel_id=1, source_target_pairs={{0,8},{1,9},{2,10},{3,11},{4,12},{5,13},{6,14},{7,15},{8,16},{9,17... | collective-permute-start | bytes 1572872 | tf_op jit(solution)/shard_map/ppermute | solution.py:333
  7.4 15.4 %collective-permute-start.6 = (bf16[2048,128]{1,0:T(8,128)(2,1)}, bf16[2048,128]{1,0:T(8,128)(2,1)S(1)}, u32[]{:S(2)}, u32[]{:S(2)}) collective-permute-start(bf16[2048,128]{1,0:T(8,128)(2,1)} %fill.1.refs_0_), channel_id=1, source_target_pairs={{0,1},{1,0},{2,3},{3,2},{4,5},{5,4},{6,7},{7,6},{8,9},{9,8},{10,11... | collective-permute-start | bytes 1572872 | tf_op jit(solution)/shard_map/ppermute | solution.py:333
  7.4 16.8 %collective-permute-start = (bf16[2048,128]{1,0:T(8,128)(2,1)}, bf16[2048,128]{1,0:T(8,128)(2,1)S(1)}, u32[]{:S(2)}, u32[]{:S(2)}) collective-permute-start(bf16[2048,128]{1,0:T(8,128)(2,1)} %fill.1.refs_0_), channel_id=1, source_target_pairs={{0,2},{1,5},{2,0},{3,7},{4,6},{5,1},{6,4},{7,3},{8,10},{9,13},{10,... | collective-permute-start | bytes 1572872 | tf_op jit(solution)/shard_map/ppermute | solution.py:333
  16.8 7.4 %collective-permute-start.9 = (bf16[2048,128]{1,0:T(8,128)(2,1)S(1)}, bf16[2048,128]{1,0:T(8,128)(2,1)}, u32[]{:S(2)}, u32[]{:S(2)}) collective-permute-start(bf16[2048,128]{1,0:T(8,128)(2,1)S(1)} %collective-permute-done.8.refs_4_), channel_id=1, source_target_pairs={{0,1},{1,0},{2,3},{3,2},{4,5},{5,4},{6,7},{7,6},{8,9},{9,8},{10,11... | collective-permute-start | bytes 1572872 | tf_op jit(solution)/shard_map/ppermute | solution.py:333
  21.3 20.8 %collective-permute-start.5 = (bf16[2048,128]{1,0:T(8,128)(2,1)S(1)}, bf16[2048,128]{1,0:T(8,128)(2,1)S(1)}, u32[]{:S(2)}, u32[]{:S(2)}) collective-permute-start(bf16[2048,128]{1,0:T(8,128)(2,1)S(1)} %collective-permute-done.2.refs_1_), channel_id=1, source_target_pairs={{0,8},{1,9},{2,10},{3,11},{4,12},{5,13},{6,14},{7,15},{8,16},{9,17... | collective-permute-start | bytes 1572872 | tf_op jit(solution)/shard_map/ppermute | solution.py:333
  21.3 20.8 %collective-permute-start.4 = (bf16[2048,128]{1,0:T(8,128)(2,1)S(1)}, bf16[2048,128]{1,0:T(8,128)(2,1)S(1)}, u32[]{:S(2)}, u32[]{:S(2)}) collective-permute-start(bf16[2048,128]{1,0:T(8,128)(2,1)S(1)} %collective-permute-done.2.refs_1_), channel_id=1, source_target_pairs={{0,4},{1,3},{2,6},{3,1},{4,0},{5,7},{6,2},{7,5},{8,12},{9,11},{10,... | collective-permute-start | bytes 1572872 | tf_op jit(solution)/shard_map/ppermute | solution.py:333
  23.6 18.5 %collective-permute-start.3 = (bf16[2048,128]{1,0:T(8,128)(2,1)S(1)}, bf16[2048,128]{1,0:T(8,128)(2,1)S(1)}, u32[]{:S(2)}, u32[]{:S(2)}) collective-permute-start(bf16[2048,128]{1,0:T(8,128)(2,1)S(1)} %collective-permute-done.2.refs_1_), channel_id=1, source_target_pairs={{0,2},{1,5},{2,0},{3,7},{4,6},{5,1},{6,4},{7,3},{8,10},{9,13},{10,... | collective-permute-start | bytes 1572872 | tf_op jit(solution)/shard_map/ppermute | solution.py:333
  24.2 17.9 %collective-permute-start.1 = (bf16[2048,128]{1,0:T(8,128)(2,1)S(1)}, bf16[2048,128]{1,0:T(8,128)(2,1)S(1)}, u32[]{:S(2)}, u32[]{:S(2)}) collective-permute-start(bf16[2048,128]{1,0:T(8,128)(2,1)S(1)} %collective-permute-done.refs_2_), channel_id=1, source_target_pairs={{0,4},{1,3},{2,6},{3,1},{4,0},{5,7},{6,2},{7,5},{8,12},{9,11},{10,... | collective-permute-start | bytes 1572872 | tf_op jit(solution)/shard_map/ppermute | solution.py:333
  44.5 4.9 %collective-permute-start.16 = (bf16[2048,128]{1,0:T(8,128)(2,1)S(1)}, bf16[2048,128]{1,0:T(8,128)(2,1)S(1)}, u32[]{:S(2)}, u32[]{:S(2)}) collective-permute-start(bf16[2048,128]{1,0:T(8,128)(2,1)S(1)} %get-tuple-element.40.refs_4_), channel_id=1, source_target_pairs={{0,1},{1,0},{2,3},{3,2},{4,5},{5,4},{6,7},{7,6},{8,9},{9,8},{10,11... | collective-permute-start | bytes 1572872 | tf_op jit(solution)/shard_map/ppermute | solution.py:333
  44.6 19.0 %collective-permute-start.10 = (bf16[2048,128]{1,0:T(8,128)(2,1)S(1)}, bf16[2048,128]{1,0:T(8,128)(2,1)S(1)}, u32[]{:S(2)}, u32[]{:S(2)}) collective-permute-start(bf16[2048,128]{1,0:T(8,128)(2,1)S(1)} %get-tuple-element.40.refs_4_), channel_id=1, source_target_pairs={{0,4},{1,3},{2,6},{3,1},{4,0},{5,7},{6,2},{7,5},{8,12},{9,11},{10,... | collective-permute-start | bytes 1572872 | tf_op jit(solution)/shard_map/ppermute | solution.py:333
  45.5 18.0 %collective-permute-start.13 = (bf16[2048,128]{1,0:T(8,128)(2,1)S(1)}, bf16[2048,128]{1,0:T(8,128)(2,1)S(1)}, u32[]{:S(2)}, u32[]{:S(2)}) collective-permute-start(bf16[2048,128]{1,0:T(8,128)(2,1)S(1)} %get-tuple-element.41.refs_1_), channel_id=1, source_target_pairs={{0,8},{1,9},{2,10},{3,11},{4,12},{5,13},{6,14},{7,15},{8,16},{9,17... | collective-permute-start | bytes 1572872 | tf_op jit(solution)/shard_map/ppermute | solution.py:333
  46.3 18.7 %collective-permute-start.12 = (bf16[2048,128]{1,0:T(8,128)(2,1)S(1)}, bf16[2048,128]{1,0:T(8,128)(2,1)S(1)}, u32[]{:S(2)}, u32[]{:S(2)}) collective-permute-start(bf16[2048,128]{1,0:T(8,128)(2,1)S(1)} %get-tuple-element.41.refs_1_), channel_id=1, source_target_pairs={{0,4},{1,3},{2,6},{3,1},{4,0},{5,7},{6,2},{7,5},{8,12},{9,11},{10,... | collective-permute-start | bytes 1572872 | tf_op jit(solution)/shard_map/ppermute | solution.py:333
  47.1 17.9 %collective-permute-start.11 = (bf16[2048,128]{1,0:T(8,128)(2,1)S(1)}, bf16[2048,128]{1,0:T(8,128)(2,1)S(1)}, u32[]{:S(2)}, u32[]{:S(2)}) collective-permute-start(bf16[2048,128]{1,0:T(8,128)(2,1)S(1)} %get-tuple-element.41.refs_1_), channel_id=1, source_target_pairs={{0,2},{1,5},{2,0},{3,7},{4,6},{5,1},{6,4},{7,3},{8,10},{9,13},{10,... | collective-permute-start | bytes 1572872 | tf_op jit(solution)/shard_map/ppermute | solution.py:333
  66.2 4.0 %collective-permute-start.24 = (bf16[2048,128]{1,0:T(8,128)(2,1)S(1)}, bf16[2048,128]{1,0:T(8,128)(2,1)S(1)}, u32[]{:S(2)}, u32[]{:S(2)}) collective-permute-start(bf16[2048,128]{1,0:T(8,128)(2,1)S(1)} %get-tuple-element.54.refs_6_), channel_id=1, source_target_pairs={{0,1},{1,0},{2,3},{3,2},{4,5},{5,4},{6,7},{7,6},{8,9},{9,8},{10,11... | collective-permute-start | bytes 1572872 | tf_op jit(solution)/shard_map/ppermute | solution.py:333
  66.8 19.6 %collective-permute-start.18 = (bf16[2048,128]{1,0:T(8,128)(2,1)S(1)}, bf16[2048,128]{1,0:T(8,128)(2,1)S(1)}, u32[]{:S(2)}, u32[]{:S(2)}) collective-permute-start(bf16[2048,128]{1,0:T(8,128)(2,1)S(1)} %get-tuple-element.50.refs_4_), channel_id=1, source_target_pairs={{0,4},{1,3},{2,6},{3,1},{4,0},{5,7},{6,2},{7,5},{8,12},{9,11},{10,... | collective-permute-start | bytes 1572872 | tf_op jit(solution)/shard_map/ppermute | solution.py:333
  67.6 19.5 %collective-permute-start.20 = (bf16[2048,128]{1,0:T(8,128)(2,1)S(1)}, bf16[2048,128]{1,0:T(8,128)(2,1)S(1)}, u32[]{:S(2)}, u32[]{:S(2)}) collective-permute-start(bf16[2048,128]{1,0:T(8,128)(2,1)S(1)} %get-tuple-element.51.refs_1_), channel_id=1, source_target_pairs={{0,4},{1,3},{2,6},{3,1},{4,0},{5,7},{6,2},{7,5},{8,12},{9,11},{10,... | collective-permute-start | bytes 1572872 | tf_op jit(solution)/shard_map/ppermute | solution.py:333
  68.8 18.4 %collective-permute-start.19 = (bf16[2048,128]{1,0:T(8,128)(2,1)S(1)}, bf16[2048,128]{1,0:T(8,128)(2,1)S(1)}, u32[]{:S(2)}, u32[]{:S(2)}) collective-permute-start(bf16[2048,128]{1,0:T(8,128)(2,1)S(1)} %get-tuple-element.51.refs_1_), channel_id=1, source_target_pairs={{0,2},{1,5},{2,0},{3,7},{4,6},{5,1},{6,4},{7,3},{8,10},{9,13},{10,... | collective-permute-start | bytes 1572872 | tf_op jit(solution)/shard_map/ppermute | solution.py:333
  87.9 9.2 %collective-permute-start.25 = (bf16[2048,128]{1,0:T(8,128)(2,1)S(1)}, bf16[2048,128]{1,0:T(8,128)(2,1)S(1)}, u32[]{:S(2)}, u32[]{:S(2)}) collective-permute-start(bf16[2048,128]{1,0:T(8,128)(2,1)S(1)} %get-tuple-element.60.refs_4_), channel_id=1, source_target_pairs={{0,4},{1,3},{2,6},{3,1},{4,0},{5,7},{6,2},{7,5},{8,12},{9,11},{10,... | collective-permute-start | bytes 1572872 | tf_op jit(solution)/shard_map/ppermute | solution.py:333
  88.7 8.4 %collective-permute-start.27 = (bf16[2048,128]{1,0:T(8,128)(2,1)S(1)}, bf16[2048,128]{1,0:T(8,128)(2,1)S(1)}, u32[]{:S(2)}, u32[]{:S(2)}) collective-permute-start(bf16[2048,128]{1,0:T(8,128)(2,1)S(1)} %get-tuple-element.61.refs_0_), channel_id=1, source_target_pairs={{0,1},{1,0},{2,3},{3,2},{4,5},{5,4},{6,7},{7,6},{8,9},{9,8},{10,11... | collective-permute-start | bytes 1572872 | tf_op jit(solution)/shard_map/ppermute | solution.py:333
  88.8 8.4 %collective-permute-start.28 = (bf16[2048,128]{1,0:T(8,128)(2,1)S(1)}, bf16[2048,128]{1,0:T(8,128)(2,1)S(1)}, u32[]{:S(2)}, u32[]{:S(2)}) collective-permute-start(bf16[2048,128]{1,0:T(8,128)(2,1)S(1)} %get-tuple-element.62.refs_2_), channel_id=1, source_target_pairs={{0,1},{1,0},{2,3},{3,2},{4,5},{5,4},{6,7},{7,6},{8,9},{9,8},{10,11... | collective-permute-start | bytes 1572872 | tf_op jit(solution)/shard_map/ppermute | solution.py:333
  89.3 7.9 %collective-permute-start.30 = (bf16[2048,128]{1,0:T(8,128)(2,1)S(1)}, bf16[2048,128]{1,0:T(8,128)(2,1)S(1)}, u32[]{:S(2)}, u32[]{:S(2)}) collective-permute-start(bf16[2048,128]{1,0:T(8,128)(2,1)S(1)} %get-tuple-element.63.refs_6_), channel_id=1, source_target_pairs={{0,1},{1,0},{2,3},{3,2},{4,5},{5,4},{6,7},{7,6},{8,9},{9,8},{10,11... | collective-permute-start | bytes 1572872 | tf_op jit(solution)/shard_map/ppermute | solution.py:333
  89.3 7.9 %collective-permute-start.29 = (bf16[2048,128]{1,0:T(8,128)(2,1)S(1)}, bf16[2048,128]{1,0:T(8,128)(2,1)S(1)}, u32[]{:S(2)}, u32[]{:S(2)}) collective-permute-start(bf16[2048,128]{1,0:T(8,128)(2,1)S(1)} %get-tuple-element.60.refs_4_), channel_id=1, source_target_pairs={{0,1},{1,0},{2,3},{3,2},{4,5},{5,4},{6,7},{7,6},{8,9},{9,8},{10,11... | collective-permute-start | bytes 1572872 | tf_op jit(solution)/shard_map/ppermute | solution.py:333
  97.1 17.1 %collective-permute-start.26 = (bf16[2048,128]{1,0:T(8,128)(2,1)S(1)}, bf16[2048,128]{1,0:T(8,128)(2,1)S(1)}, u32[]{:S(2)}, u32[]{:S(2)}) collective-permute-start(bf16[2048,128]{1,0:T(8,128)(2,1)S(1)} %collective-permute-done.25.refs_0_), channel_id=1, source_target_pairs={{0,1},{1,0},{2,3},{3,2},{4,5},{5,4},{6,7},{7,6},{8,9},{9,8},{10,11... | collective-permute-start | bytes 1572872 | tf_op jit(solution)/shard_map/ppermute | solution.py:333
  (26 other events, 135.1 us)

commit v3 on v2

--- a/solution.py
+++ b/solution.py
@@ -12,7 +12,7 @@
 VECS = F + 1
 LANES = 128
 CHAINS = 4
-UNROLL = 8
+UNROLL = 32
 VMEM = 32 << 20
 SMEM_SPEC = pl.BlockSpec(memory_space=pltpu.SMEM)
 ANY_SPEC = pl.BlockSpec(memory_space=pl.ANY)
@@ -73,17 +73,18 @@
     return pl.pallas_call(
         gate_kernel,
         out_shape=[jax.ShapeDtypeStruct(one.shape, one.dtype) for one in arrays],
-        in_specs=[HBM_SPEC] * n_arrays + [SMEM_SPEC],
-        out_specs=[HBM_SPEC] * n_arrays,
+        in_specs=[ANY_SPEC] * n_arrays + [SMEM_SPEC],
+        out_specs=[ANY_SPEC] * n_arrays,
         input_output_aliases={index: index for index in range(n_arrays)},
         compiler_params=pltpu.CompilerParams(vmem_limit_bytes=1 << 20),
         name="gate",
     )(*arrays, after)
 
 
-def pool_shards(first, entry_refs, entry_held, count_ref, shards, sems, held, table, sums):
+def pool_shards(first, rows, entry_refs, entry_held, count_ref, shards, sems, held, table, sums):
+    cap = entry_held[0].shape[0] // 8
     copies = [
-        pltpu.make_async_copy(ref.at[pl.ds(first, 8)], to, sems.at[len(shards) + index])
+        pltpu.make_async_copy(ref.at[pl.ds(first * cap, 8 * cap)], to, sems.at[len(shards) + index])
         for index, (ref, to) in enumerate(zip(entry_refs, entry_held))
     ]
     copies += [pltpu.make_async_copy(ref, held.at[s], sems.at[s]) for s, ref in enumerate(shards)]
@@ -93,34 +94,33 @@
     for copy in copies[:2]:
         copy.wait()
     slot_ref, bag_ref = entry_held
-    skipped = 2 if first == 0 else 0
     for s, copy in enumerate(copies[2:]):
         copy.wait()
         table[...] = held[s].astype(jnp.float32)
-        row = s + skipped
+        row = rows[s]
 
         def add_entries(step, _):
-            first = step * UNROLL
+            start = row * cap + step * UNROLL
             for group in range(UNROLL // CHAINS):
-                entries = [first + group * CHAINS + k for k in range(CHAINS)]
-                slots = [slot_ref[row, e] for e in entries]
-                bags = [bag_ref[row, e] for e in entries]
-                rows = [table[pl.ds(slot, 1), :] for slot in slots]
+                entries = [start + group * CHAINS + k for k in range(CHAINS)]
+                slots = [slot_ref[e] for e in entries]
+                bags = [bag_ref[e] for e in entries]
+                found = [table[pl.ds(slot, 1), :] for slot in slots]
                 olds = [sums[k][pl.ds(bags[k], 1), :] for k in range(CHAINS)]
                 for k in range(CHAINS):
-                    sums[k][pl.ds(bags[k], 1), :] = olds[k] + rows[k]
+                    sums[k][pl.ds(bags[k], 1), :] = olds[k] + found[k]
             return 0
 
         lax.fori_loop(0, count_ref[first + row], add_entries, 0)
 
 
-def pool_kernel(first, n_shards, is_first, count_ref, slot_ref, bag_ref, *refs):
-    shards, refs = refs[:n_shards], refs[n_shards:]
+def pool_kernel(first, rows, is_first, count_ref, slot_ref, bag_ref, *refs):
+    shards, refs = refs[: len(rows)], refs[len(rows) :]
     if not is_first:
         refs = refs[CHAINS:]
     sums, (done, *entry_held, held, table, sems) = refs[:CHAINS], refs[CHAINS:]
     pooling = pool_shards(
-        first, (slot_ref, bag_ref), entry_held, count_ref, shards, sems, held, table, sums
+        first, rows, (slot_ref, bag_ref), entry_held, count_ref, shards, sems, held, table, sums
     )
     next(pooling)
     if is_first:
@@ -210,7 +210,7 @@
     masked, *entry_held, held, table, sems = refs
     queries = dense_ref.shape[0]
     for _ in pool_shards(
-        first, (slot_ref, bag_ref), entry_held, count_ref, shards, sems, held, table, old_sums
+        first, (0, 1), (slot_ref, bag_ref), entry_held, count_ref, shards, sems, held, table, old_sums
     ):
         pass
     interact(old_sums, dense_ref, masked, queries)
@@ -235,26 +235,26 @@
 
 def pool_scratch(n_shards, shard_rows, cap):
     return [
-        pltpu.SMEM((8, cap), jnp.int32),
-        pltpu.SMEM((8, cap), jnp.int32),
+        pltpu.SMEM((8 * cap,), jnp.int32),
+        pltpu.SMEM((8 * cap,), jnp.int32),
         pltpu.VMEM((n_shards, shard_rows, LANES), jnp.bfloat16),
         pltpu.VMEM((shard_rows, LANES), jnp.float32),
         pltpu.SemaphoreType.DMA((n_shards + 2,)),
     ]
 
 
-def pool(first, entries, shards, sums, sum_rows):
+def pool(first, entries, shards, sums, sum_rows, rows=(0, 1)):
     n_shards = len(shards)
     is_first = sums is None
     sums = [] if is_first else sums
     *sums, done = pl.pallas_call(
-        functools.partial(pool_kernel, first, n_shards, is_first),
+        functools.partial(pool_kernel, first, rows, is_first),
         out_shape=[pltpu.VMEM((sum_rows, LANES), jnp.float32)] * CHAINS
         + [jax.ShapeDtypeStruct((1,), jnp.int32)],
-        in_specs=[SMEM_SPEC] + [HBM_SPEC] * (2 + n_shards) + [VMEM_SPEC] * len(sums),
+        in_specs=[SMEM_SPEC] + [HBM_SPEC] * 2 + [ANY_SPEC] * n_shards + [VMEM_SPEC] * len(sums),
         out_specs=[VMEM_SPEC] * CHAINS + [SMEM_SPEC],
         input_output_aliases={3 + n_shards + k: k for k in range(len(sums))},
-        scratch_shapes=pool_scratch(n_shards, shards[0].shape[0], entries[1].shape[1]),
+        scratch_shapes=pool_scratch(n_shards, shards[0].shape[0], entries[1].shape[0] // entries[0].shape[0]),
         compiler_params=pltpu.CompilerParams(vmem_limit_bytes=VMEM),
         cost_estimate=pl.CostEstimate(flops=0, bytes_accessed=n_shards * 6_000_000, transcendentals=0),
         name="pool",
@@ -284,10 +284,10 @@
     out = pl.pallas_call(
         functools.partial(final_kernel, first, n_shards, head is not None),
         out_shape=[out_shape] + [pltpu.VMEM(one.shape, one.dtype) for one in sums],
-        in_specs=[SMEM_SPEC] + [HBM_SPEC] * (2 + n_shards) + [VMEM_SPEC] * (CHAINS + 1) + head_specs,
+        in_specs=[SMEM_SPEC] + [HBM_SPEC] * 2 + [ANY_SPEC] * n_shards + [VMEM_SPEC] * (CHAINS + 1) + head_specs,
         out_specs=[VMEM_SPEC] * (CHAINS + 1),
         input_output_aliases={3 + n_shards + k: 1 + k for k in range(CHAINS)},
-        scratch_shapes=scratch + pool_scratch(n_shards, shards[0].shape[0], entries[1].shape[1]),
+        scratch_shapes=scratch + pool_scratch(n_shards, shards[0].shape[0], entries[1].shape[0] // entries[0].shape[0]),
         compiler_params=pltpu.CompilerParams(vmem_limit_bytes=VMEM),
         name="finish",
     )(*entries, *shards, *sums, dense_rows, *head_args)
@@ -348,15 +348,16 @@
     def both_cores(shift, *flips):
         return [origin(shift, *flips, side) for side in (core, 1 - core)]
 
-    order = []
-    for shift in range(n_planes + 1):
-        before, now = max(shift - 1, 0), min(shift, n_planes - 1)
-        order += both_cores(before, 1, 1)
-        for flips in ((0, 0), (1, 0), (0, 1)):
-            order += both_cores(now, *flips)
+    unused = [0] * 6
+    order = both_cores(0, 0, 0) + unused
+    for shift in range(n_planes):
+        before, after = max(shift - 1, 0), min(shift + 1, n_planes - 1)
+        order += both_cores(shift, 1, 0) + both_cores(shift, 0, 1)
+        order += both_cores(before, 1, 1) + both_cores(after, 0, 0)
+    order += both_cores(n_planes - 1, 1, 1) + unused
     order = jnp.stack(order)
     cap = lookup_slot.shape[2]
-    cap += -cap % UNROLL
+    cap += -cap % LANES
     spare = ((0, 0), (0, cap - lookup_slot.shape[2]))
     slots = jnp.pad(lookup_slot[0], spare)[order]
     bag_ids = jnp.pad(lookup_bag[0], spare, constant_values=bags)[order]
@@ -364,25 +365,37 @@
     steps = (used + UNROLL - 1) // UNROLL
     sum_rows = bags + 8
     places = jnp.where(bag_ids < bags, bag_ids % F * queries + bag_ids // F, bags)
-    entries = (steps, slots, places)
-
-    sums, far = None, []
-    piece, crossed, turned = own, first_hop(own), second_hop(own)
-    next_piece = next_plane(piece)
+    entries = (steps, slots.reshape(-1), places.reshape(-1))
+
+    def of_chip(array):
+        return [array, other_core(array)]
+
+    crossed, turned, next_piece = first_hop(own), second_hop(own), next_plane(own)
+    sums, _ = pool(0, entries, of_chip(own), None, sum_rows)
+    far = []
     for shift in range(n_planes):
-        near = [piece, other_core(piece), crossed, other_core(crossed), turned, other_core(turned)]
+        last = shift == n_planes - 1
+        near = of_chip(crossed) + of_chip(turned)
         next_far = second_hop(crossed)
-        if shift < n_planes - 1:
-            next_crossed, next_turned = first_hop(next_piece), second_hop(next_piece)
-            passed = [next_piece, next_crossed, next_turned]
+        passed = [next_far]
+        if not last:
+            passed += [first_hop(next_piece), second_hop(next_piece)]
+            piece = of_chip(next_piece)
             if shift < n_planes - 2:
                 passed.append(next_plane(next_piece))
-        sums, done = pool(8 * shift, entries, far + near, sums, sum_rows)
-        if shift < n_planes - 1:
-            next_far, piece, crossed, turned, *next_piece = gate([next_far] + passed, done)
+        else:
+            piece = []
+        if shift == 0:
+            shards, rows = near + piece, [0, 1, 2, 3, 6, 7]
+        else:
+            shards, rows = near + far + piece, list(range(6 + len(piece)))
+        sums, done = pool(8 * shift + 8, entries, shards, sums, sum_rows, rows)
+        next_far, *passed = gate(passed, done)
+        far = of_chip(next_far)
+        if not last:
+            crossed, turned, *next_piece = passed
             next_piece = next_piece[0] if next_piece else None
-        far = [next_far, other_core(next_far)]
-    args = (8 * n_planes, entries, far, sums, dense_rows)
+    args = (8 * n_planes + 8, entries, far, sums, dense_rows)
     if owners == 1:
         return finish(*args, (w_first, w_second, w_out.reshape(1, -1)))
     inter_in = finish(*args, None)[:, : w_first.shape[0]]

time: 130 us -> 119 us (0.915)
  Pallas kernels: 77.1 us -> 54.8 us
  waiting for transfers between devices: 22.2 us -> 27.3 us
  starting transfers between devices: 21.6 us -> 26.4 us
  local copies, waits for them, and re-layouts: 7.91 us -> 9.34 us
    pallas_call x4 -> x5, Pallas kernels: 57.2 us -> 35.1 us  [pool(): pl.pallas_call(functools.partial(pool_kernel, first, rows, is_first), out...]
    ppermute x31, waiting for transfers between devices: 22.2 us -> 27.3 us  [hop(): return lambda array: lax.ppermute(array, 'cache', pairs)]
    ppermute x31, starting transfers between devices: 21.6 us -> 26.4 us  [hop(): return lambda array: lax.ppermute(array, 'cache', pairs)]
    gather x1 -> x2, local copies, waits for them, and re-layouts: 0.63 us -> 2.24 us  [per_device(): slots = jnp.pad(lookup_slot[0], spare)[order]]
    unnamed x38 -> x32, local copies, waits for them, and re-layouts: 5.58 us -> 5.38 us
  transfers between devices with their start and end apart: 31 -> 31, of which waited for: 8 -> 8; matrix products, arithmetic and copies ran while one was open for 2% -> 4% of each run, Pallas kernels for 44% -> 30%
where the time goes in v3:
time: 119 us
  Pallas kernels  54.8 us (46%)
  waiting for transfers between devices  27.3 us (23%)
  starting transfers between devices  26.4 us (22%)
  local copies, waits for them, and re-layouts  9.34 us (8%)
    pallas_call x5, Pallas kernels, pool(): pl.pallas_call(functools.partial(pool_kernel, first, rows, is_first), out...  35.1 us
    ppermute x31, waiting for transfers between devices, hop(): return lambda array: lax.ppermute(array, 'cache', pairs)  27.3 us
    ppermute x31, starting transfers between devices, hop(): return lambda array: lax.ppermute(array, 'cache', pairs)  26.4 us
    pallas_call x1, Pallas kernels, finish(): pl.pallas_call(functools.partial(final_kernel, first, n_shards, head is n...  14.3 us
    unnamed x32, local copies, waits for them, and re-layouts  5.38 us
    pallas_call x1, Pallas kernels, fill(): pl.pallas_call(fill_kernel, out_shape=jax.ShapeDtypeStruct(cache_rows.sha...  2.76 us
    pallas_call x4, Pallas kernels, gate(): pl.pallas_call(gate_kernel, out_shape=[jax.ShapeDtypeStruct(one.shape, on...  2.59 us
  transfers between devices with their start and end apart: 31, of which 8 were waited for; matrix products, arithmetic and copies ran while one was open for 4% of the time, Pallas kernels for 30%

profile of v3, /device:TPU:0, one launch (start us, length us, event | category | flops | bytes accessed | tf_op | source)
XLA Modules:
  0.0 118.6 jit_solution(12842836867817879888)
XLA Ops:
  0.0 2.8 %fill.1.refs_0_ = bf16[2048,128]{1,0:T(8,128)(2,1)} custom-call(s32[2]{0:T(128)} %bitcast.42, s32[2]{0:T(128)} %bitcast.43, bf16[2048,128]{1,0:T(8,128)(2,1)} %cache_ref.1, bf16[1024,128]{1,0:T(8,128)(2,1)} %fills_ref.1), custom_call_target="tpu_custom_call" | custom-call | tf_op jit(solution)/shard_map/fill/pallas_call | solution.py:57
  2.8 3.1 %collective-permute-start.2 = (bf16[2048,128]{1,0:T(8,128)(2,1)}, bf16[2048,128]{1,0:T(8,128)(2,1)}, u32[]{:S(2)}, u32[]{:S(2)}) collective-permute-start(bf16[2048,128]{1,0:T(8,128)(2,1)} %fill.1.refs_0_), channel_id=1, source_target_pairs={{0,8},{1,9},{2,10},{3,11},{4,12},{5,13},{6,14},{7,15},{8,16},{9,17... | collective-permute-start | bytes 1572872 | tf_op jit(solution)/shard_map/ppermute | solution.py:333
  8.9 11.2 %collective-permute-done.2.refs_4_ = bf16[2048,128]{1,0:T(8,128)(2,1)} collective-permute-done((bf16[2048,128]{1,0:T(8,128)(2,1)}, bf16[2048,128]{1,0:T(8,128)(2,1)}, u32[]{:S(2)}, u32[]{:S(2)}) %collective-permute-start.2) | collective-permute-done | bytes 524320 | tf_op jit(solution)/shard_map/ppermute | solution.py:333
  20.8 1.7 %collective-permute-start.3 = (bf16[2048,128]{1,0:T(8,128)(2,1)}, bf16[2048,128]{1,0:T(8,128)(2,1)S(1)}, u32[]{:S(2)}, u32[]{:S(2)}) collective-permute-start(bf16[2048,128]{1,0:T(8,128)(2,1)} %collective-permute-done.2.refs_4_), channel_id=1, source_target_pairs={{0,2},{1,5},{2,0},{3,7},{4,6},{5,1},{6,4},{7,3},{8,10},{9,13},{10,... | collective-permute-start | bytes 1572872 | tf_op jit(solution)/shard_map/ppermute | solution.py:333
  23.3 1.5 %collective-permute-start.4 = (bf16[2048,128]{1,0:T(8,128)(2,1)}, bf16[2048,128]{1,0:T(8,128)(2,1)S(1)}, u32[]{:S(2)}, u32[]{:S(2)}) collective-permute-start(bf16[2048,128]{1,0:T(8,128)(2,1)} %collective-permute-done.2.refs_4_), channel_id=1, source_target_pairs={{0,4},{1,3},{2,6},{3,1},{4,0},{5,7},{6,2},{7,5},{8,12},{9,11},{10,... | collective-permute-start | bytes 1572872 | tf_op jit(solution)/shard_map/ppermute | solution.py:333
  24.8 1.6 %collective-permute-start.5 = (bf16[2048,128]{1,0:T(8,128)(2,1)}, bf16[2048,128]{1,0:T(8,128)(2,1)S(1)}, u32[]{:S(2)}, u32[]{:S(2)}) collective-permute-start(bf16[2048,128]{1,0:T(8,128)(2,1)} %collective-permute-done.2.refs_4_), channel_id=1, source_target_pairs={{0,8},{1,9},{2,10},{3,11},{4,12},{5,13},{6,14},{7,15},{8,16},{9,17... | collective-permute-start | bytes 1572872 | tf_op jit(solution)/shard_map/ppermute | solution.py:333
  27.8 1.6 %gather_fusion.1 = s32[48,624]{1,0:T(8,128)S(1)} fusion(s32[32,624]{1,0:T(8,128)} %bitcast.41, s32[1024]{0:T(1024)S(1)} %pad_clamp_fusion), kind=kCustom, calls=%fused_computation.1 | custom fusion | bytes 239808 | tf_op jit(solution)/shard_map/gather | solution.py:362
  33.1 4.2 %pool.5 = (f32[9992,128]{1,0:T(8,128)S(1)}, f32[9992,128]{1,0:T(8,128)S(1)}, f32[9992,128]{1,0:T(8,128)S(1)}, f32[9992,128]{1,0:T(8,128)S(1)}, s32[1]{0:T(128)}) custom-call(s32[48]{0:T(128)S(1)} %and_select_fusion.count_ref, s32[30720]{0:T(1024)S(1)} %reshape.1462.slot_ref, s32[30720]{0:T(1024)S(1)} %reshape.1463.bag_ref, bf16[2048,128]{1,0:T(8,128)(2,1)S(1)} %copy-done.5, ...), custom_call_target="tpu_custom_call" | custom-call | bytes 12000000 | tf_op jit(solution)/shard_map/pool/pallas_call | solution.py:250
  37.3 7.1 %pool.6 = (f32[9992,128]{1,0:T(8,128)S(1)}, f32[9992,128]{1,0:T(8,128)S(1)}, f32[9992,128]{1,0:T(8,128)S(1)}, f32[9992,128]{1,0:T(8,128)S(1)}, s32[1]{0:T(128)}) custom-call(s32[48]{0:T(128)S(1)} %and_select_fusion.count_ref, s32[30720]{0:T(1024)S(1)} %reshape.1462.slot_ref, ...), custom_call_target="tpu_custom_call", output_to_operand_aliasing={{0}: (9, {}), {1}: (10, {}), {2}: (11, {}), {3}: (12, {})} | custom-call | bytes 36000000 | tf_op jit(solution)/shard_map/pool/pallas_call | solution.py:250
  46.3 2.4 %collective-permute-start.11 = (bf16[2048,128]{1,0:T(8,128)(2,1)S(1)}, bf16[2048,128]{1,0:T(8,128)(2,1)S(1)}, u32[]{:S(2)}, u32[]{:S(2)}) collective-permute-start(bf16[2048,128]{1,0:T(8,128)(2,1)S(1)} %get-tuple-element.46.refs_0_), channel_id=1, source_target_pairs={{0,4},{1,3},{2,6},{3,1},{4,0},{5,7},{6,2},{7,5},{8,12},{9,11},{10,... | collective-permute-start | bytes 1572872 | tf_op jit(solution)/shard_map/ppermute | solution.py:333
  48.6 1.7 %collective-permute-start.13 = (bf16[2048,128]{1,0:T(8,128)(2,1)S(1)}, bf16[2048,128]{1,0:T(8,128)(2,1)S(1)}, u32[]{:S(2)}, u32[]{:S(2)}) collective-permute-start(bf16[2048,128]{1,0:T(8,128)(2,1)S(1)} %get-tuple-element.47.refs_6_), channel_id=1, source_target_pairs={{0,4},{1,3},{2,6},{3,1},{4,0},{5,7},{6,2},{7,5},{8,12},{9,11},{10,... | collective-permute-start | bytes 1572872 | tf_op jit(solution)/shard_map/ppermute | solution.py:333
  52.1 8.9 %pool.7 = (f32[9992,128]{1,0:T(8,128)S(1)}, f32[9992,128]{1,0:T(8,128)S(1)}, f32[9992,128]{1,0:T(8,128)S(1)}, f32[9992,128]{1,0:T(8,128)S(1)}, s32[1]{0:T(128)}) custom-call(s32[48]{0:T(128)S(1)} %and_select_fusion.count_ref, s32[30720]{0:T(1024)S(1)} %reshape.1462.slot_ref, ...), custom_call_target="tpu_custom_call", output_to_operand_aliasing={{0}: (11, {}), {1}: (12, {}), {2}: (13, {}), {3}: (14, {})} | custom-call | bytes 48000000 | tf_op jit(solution)/shard_map/pool/pallas_call | solution.py:250
  61.0 2.5 %collective-permute-done.12.refs_1_ = bf16[2048,128]{1,0:T(8,128)(2,1)S(1)} collective-permute-done((bf16[2048,128]{1,0:T(8,128)(2,1)S(1)}, bf16[2048,128]{1,0:T(8,128)(2,1)S(1)}, u32[]{:S(2)}, u32[]{:S(2)}) %collective-permute-start.12) | collective-permute-done | bytes 524320 | tf_op jit(solution)/shard_map/ppermute | solution.py:333
  63.5 3.5 %collective-permute-done.13.refs_2_ = bf16[2048,128]{1,0:T(8,128)(2,1)S(1)} collective-permute-done((bf16[2048,128]{1,0:T(8,128)(2,1)S(1)}, bf16[2048,128]{1,0:T(8,128)(2,1)S(1)}, u32[]{:S(2)}, u32[]{:S(2)}) %collective-permute-start.13) | collective-permute-done | bytes 524320 | tf_op jit(solution)/shard_map/ppermute | solution.py:333
  68.8 2.0 %collective-permute-start.19 = (bf16[2048,128]{1,0:T(8,128)(2,1)S(1)}, bf16[2048,128]{1,0:T(8,128)(2,1)S(1)}, u32[]{:S(2)}, u32[]{:S(2)}) collective-permute-start(bf16[2048,128]{1,0:T(8,128)(2,1)S(1)} %get-tuple-element.55.refs_0_), channel_id=1, source_target_pairs={{0,4},{1,3},{2,6},{3,1},{4,0},{5,7},{6,2},{7,5},{8,12},{9,11},{10,... | collective-permute-start | bytes 1572872 | tf_op jit(solution)/shard_map/ppermute | solution.py:333
  70.8 1.6 %collective-permute-start.21 = (bf16[2048,128]{1,0:T(8,128)(2,1)S(1)}, bf16[2048,128]{1,0:T(8,128)(2,1)S(1)}, u32[]{:S(2)}, u32[]{:S(2)}) collective-permute-start(bf16[2048,128]{1,0:T(8,128)(2,1)S(1)} %get-tuple-element.56.refs_6_), channel_id=1, source_target_pairs={{0,4},{1,3},{2,6},{3,1},{4,0},{5,7},{6,2},{7,5},{8,12},{9,11},{10,... | collective-permute-start | bytes 1572872 | tf_op jit(solution)/shard_map/ppermute | solution.py:333
  73.4 8.1 %pool.8 = (f32[9992,128]{1,0:T(8,128)S(1)}, f32[9992,128]{1,0:T(8,128)S(1)}, f32[9992,128]{1,0:T(8,128)S(1)}, f32[9992,128]{1,0:T(8,128)S(1)}, s32[1]{0:T(128)}) custom-call(s32[48]{0:T(128)S(1)} %and_select_fusion.count_ref, s32[30720]{0:T(1024)S(1)} %reshape.1462.slot_ref, ...), custom_call_target="tpu_custom_call", output_to_operand_aliasing={{0}: (11, {}), {1}: (12, {}), {2}: (13, {}), {3}: (14, {})} | custom-call | bytes 48000000 | tf_op jit(solution)/shard_map/pool/pallas_call | solution.py:250
  81.6 1.7 %collective-permute-done.19.refs_0_ = bf16[2048,128]{1,0:T(8,128)(2,1)S(1)} collective-permute-done((bf16[2048,128]{1,0:T(8,128)(2,1)S(1)}, bf16[2048,128]{1,0:T(8,128)(2,1)S(1)}, u32[]{:S(2)}, u32[]{:S(2)}) %collective-permute-start.19) | collective-permute-done | bytes 524320 | tf_op jit(solution)/shard_map/ppermute | solution.py:333
  83.2 2.4 %collective-permute-done.20.refs_1_ = bf16[2048,128]{1,0:T(8,128)(2,1)S(1)} collective-permute-done((bf16[2048,128]{1,0:T(8,128)(2,1)S(1)}, bf16[2048,128]{1,0:T(8,128)(2,1)S(1)}, u32[]{:S(2)}, u32[]{:S(2)}) %collective-permute-start.20) | collective-permute-done | bytes 524320 | tf_op jit(solution)/shard_map/ppermute | solution.py:333
  85.7 3.5 %collective-permute-done.21.refs_2_ = bf16[2048,128]{1,0:T(8,128)(2,1)S(1)} collective-permute-done((bf16[2048,128]{1,0:T(8,128)(2,1)S(1)}, bf16[2048,128]{1,0:T(8,128)(2,1)S(1)}, u32[]{:S(2)}, u32[]{:S(2)}) %collective-permute-start.21) | collective-permute-done | bytes 524320 | tf_op jit(solution)/shard_map/ppermute | solution.py:333
  90.5 2.0 %collective-permute-start.26 = (bf16[2048,128]{1,0:T(8,128)(2,1)S(1)}, bf16[2048,128]{1,0:T(8,128)(2,1)S(1)}, u32[]{:S(2)}, u32[]{:S(2)}) collective-permute-start(bf16[2048,128]{1,0:T(8,128)(2,1)S(1)} %get-tuple-element.64.refs_0_), channel_id=1, source_target_pairs={{0,4},{1,3},{2,6},{3,1},{4,0},{5,7},{6,2},{7,5},{8,12},{9,11},{10,... | collective-permute-start | bytes 1572872 | tf_op jit(solution)/shard_map/ppermute | solution.py:333
  94.1 6.8 %pool.9 = (f32[9992,128]{1,0:T(8,128)S(1)}, f32[9992,128]{1,0:T(8,128)S(1)}, f32[9992,128]{1,0:T(8,128)S(1)}, f32[9992,128]{1,0:T(8,128)S(1)}, s32[1]{0:T(128)}) custom-call(s32[48]{0:T(128)S(1)} %and_select_fusion.count_ref, s32[30720]{0:T(1024)S(1)} %reshape.1462.slot_ref, ...), custom_call_target="tpu_custom_call", output_to_operand_aliasing={{0}: (9, {}), {1}: (10, {}), {2}: (11, {}), {3}: (12, {})} | custom-call | bytes 36000000 | tf_op jit(solution)/shard_map/pool/pallas_call | solution.py:250
  102.6 1.5 %collective-permute-done.30.refs_1_ = bf16[2048,128]{1,0:T(8,128)(2,1)S(1)} collective-permute-done((bf16[2048,128]{1,0:T(8,128)(2,1)S(1)}, bf16[2048,128]{1,0:T(8,128)(2,1)S(1)}, u32[]{:S(2)}, u32[]{:S(2)}) %collective-permute-start.30) | collective-permute-done | bytes 524320 | tf_op jit(solution)/shard_map/ppermute | solution.py:333
  104.1 14.3 %finish.1 = (f32[384]{0:T(512)}, f32[9992,128]{1,0:T(8,128)S(1)}, f32[9992,128]{1,0:T(8,128)S(1)}, f32[9992,128]{1,0:T(8,128)S(1)}, f32[9992,128]{1,0:T(8,128)S(1)}) custom-call(s32[48]{0:T(128)S(1)} %and_select_fusion.count_ref, s32[30720]{0:T(1024)S(1)} %reshape.1462.slot_ref, ...), custom_call_target="tpu_custom_call", output_to_operand_aliasing={{1}: (5, {}), {2}: (6, {}), {3}: (7, {}), {4}: (8, {})} | custom-call | tf_op jit(solution)/shard_map/finish/pallas_call | solution.py:284
  (93 shorter events, 20.3 us)
Async XLA Ops:
  2.8 17.3 %collective-permute-start.2 = (bf16[2048,128]{1,0:T(8,128)(2,1)}, bf16[2048,128]{1,0:T(8,128)(2,1)}, u32[]{:S(2)}, u32[]{:S(2)}) collective-permute-start(bf16[2048,128]{1,0:T(8,128)(2,1)} %fill.1.refs_0_), channel_id=1, source_target_pairs={{0,8},{1,9},{2,10},{3,11},{4,12},{5,13},{6,14},{7,15},{8,16},{9,17... | collective-permute-start | bytes 1572872 | tf_op jit(solution)/shard_map/ppermute | solution.py:333
  5.9 14.3 %collective-permute-start = (bf16[2048,128]{1,0:T(8,128)(2,1)}, bf16[2048,128]{1,0:T(8,128)(2,1)S(1)}, u32[]{:S(2)}, u32[]{:S(2)}) collective-permute-start(bf16[2048,128]{1,0:T(8,128)(2,1)} %fill.1.refs_0_), channel_id=1, source_target_pairs={{0,2},{1,5},{2,0},{3,7},{4,6},{5,1},{6,4},{7,3},{8,10},{9,13},{10,... | collective-permute-start | bytes 1572872 | tf_op jit(solution)/shard_map/ppermute | solution.py:333
  7.3 15.2 %collective-permute-start.10 = (bf16[2048,128]{1,0:T(8,128)(2,1)}, bf16[2048,128]{1,0:T(8,128)(2,1)S(1)}, u32[]{:S(2)}, u32[]{:S(2)}) collective-permute-start(bf16[2048,128]{1,0:T(8,128)(2,1)} %fill.1.refs_0_), channel_id=1, source_target_pairs={{0,1},{1,0},{2,3},{3,2},{4,5},{5,4},{6,7},{7,6},{8,9},{9,8},{10,11... | collective-permute-start | bytes 1572872 | tf_op jit(solution)/shard_map/ppermute | solution.py:333
  7.3 17.5 %collective-permute-start.7 = (bf16[2048,128]{1,0:T(8,128)(2,1)}, bf16[2048,128]{1,0:T(8,128)(2,1)S(1)}, u32[]{:S(2)}, u32[]{:S(2)}) collective-permute-start(bf16[2048,128]{1,0:T(8,128)(2,1)} %fill.1.refs_0_), channel_id=1, source_target_pairs={{0,4},{1,3},{2,6},{3,1},{4,0},{5,7},{6,2},{7,5},{8,12},{9,11},{10,... | collective-permute-start | bytes 1572872 | tf_op jit(solution)/shard_map/ppermute | solution.py:333
  20.1 6.3 %collective-permute-start.9 = (bf16[2048,128]{1,0:T(8,128)(2,1)}, bf16[2048,128]{1,0:T(8,128)(2,1)}, u32[]{:S(2)}, u32[]{:S(2)}) collective-permute-start(bf16[2048,128]{1,0:T(8,128)(2,1)} %collective-permute-done.2.refs_4_), channel_id=1, source_target_pairs={{0,1},{1,0},{2,3},{3,2},{4,5},{5,4},{6,7},{7,6},{8,9},{9,8},{10,11... | collective-permute-start | bytes 1572872 | tf_op jit(solution)/shard_map/ppermute | solution.py:333
  20.1 6.8 %collective-permute-start.6 = (bf16[2048,128]{1,0:T(8,128)(2,1)S(1)}, bf16[2048,128]{1,0:T(8,128)(2,1)}, u32[]{:S(2)}, u32[]{:S(2)}) collective-permute-start(bf16[2048,128]{1,0:T(8,128)(2,1)S(1)} %collective-permute-done.refs_0_), channel_id=1, source_target_pairs={{0,1},{1,0},{2,3},{3,2},{4,5},{5,4},{6,7},{7,6},{8,9},{9,8},{10,11... | collective-permute-start | bytes 1572872 | tf_op jit(solution)/shard_map/ppermute | solution.py:333
  20.8 23.7 %collective-permute-start.3 = (bf16[2048,128]{1,0:T(8,128)(2,1)}, bf16[2048,128]{1,0:T(8,128)(2,1)S(1)}, u32[]{:S(2)}, u32[]{:S(2)}) collective-permute-start(bf16[2048,128]{1,0:T(8,128)(2,1)} %collective-permute-done.2.refs_4_), channel_id=1, source_target_pairs={{0,2},{1,5},{2,0},{3,7},{4,6},{5,1},{6,4},{7,3},{8,10},{9,13},{10,... | collective-permute-start | bytes 1572872 | tf_op jit(solution)/shard_map/ppermute | solution.py:333
  23.3 21.2 %collective-permute-start.4 = (bf16[2048,128]{1,0:T(8,128)(2,1)}, bf16[2048,128]{1,0:T(8,128)(2,1)S(1)}, u32[]{:S(2)}, u32[]{:S(2)}) collective-permute-start(bf16[2048,128]{1,0:T(8,128)(2,1)} %collective-permute-done.2.refs_4_), channel_id=1, source_target_pairs={{0,4},{1,3},{2,6},{3,1},{4,0},{5,7},{6,2},{7,5},{8,12},{9,11},{10,... | collective-permute-start | bytes 1572872 | tf_op jit(solution)/shard_map/ppermute | solution.py:333
  24.8 19.7 %collective-permute-start.5 = (bf16[2048,128]{1,0:T(8,128)(2,1)}, bf16[2048,128]{1,0:T(8,128)(2,1)S(1)}, u32[]{:S(2)}, u32[]{:S(2)}) collective-permute-start(bf16[2048,128]{1,0:T(8,128)(2,1)} %collective-permute-done.2.refs_4_), channel_id=1, source_target_pairs={{0,8},{1,9},{2,10},{3,11},{4,12},{5,13},{6,14},{7,15},{8,16},{9,17... | collective-permute-start | bytes 1572872 | tf_op jit(solution)/shard_map/ppermute | solution.py:333
  26.4 18.1 %collective-permute-start.1 = (bf16[2048,128]{1,0:T(8,128)(2,1)S(1)}, bf16[2048,128]{1,0:T(8,128)(2,1)S(1)}, u32[]{:S(2)}, u32[]{:S(2)}) collective-permute-start(bf16[2048,128]{1,0:T(8,128)(2,1)S(1)} %collective-permute-done.refs_0_), channel_id=1, source_target_pairs={{0,4},{1,3},{2,6},{3,1},{4,0},{5,7},{6,2},{7,5},{8,12},{9,11},{10,... | collective-permute-start | bytes 1572872 | tf_op jit(solution)/shard_map/ppermute | solution.py:333
  26.9 10.4 %collective-permute-start.8 = (bf16[2048,128]{1,0:T(8,128)(2,1)S(1)}, bf16[2048,128]{1,0:T(8,128)(2,1)}, u32[]{:S(2)}, u32[]{:S(2)}) collective-permute-start(bf16[2048,128]{1,0:T(8,128)(2,1)S(1)} %collective-permute-done.7.refs_2_), channel_id=1, source_target_pairs={{0,1},{1,0},{2,3},{3,2},{4,5},{5,4},{6,7},{7,6},{8,9},{9,8},{10,11... | collective-permute-start | bytes 1572872 | tf_op jit(solution)/shard_map/ppermute | solution.py:333
  45.2 3.5 %collective-permute-start.15 = (bf16[2048,128]{1,0:T(8,128)(2,1)S(1)}, bf16[2048,128]{1,0:T(8,128)(2,1)S(1)}, u32[]{:S(2)}, u32[]{:S(2)}) collective-permute-start(bf16[2048,128]{1,0:T(8,128)(2,1)S(1)} %get-tuple-element.46.refs_0_), channel_id=1, source_target_pairs={{0,1},{1,0},{2,3},{3,2},{4,5},{5,4},{6,7},{7,6},{8,9},{9,8},{10,11... | collective-permute-start | bytes 1572872 | tf_op jit(solution)/shard_map/ppermute | solution.py:333
  45.8 4.6 %collective-permute-start.17 = (bf16[2048,128]{1,0:T(8,128)(2,1)S(1)}, bf16[2048,128]{1,0:T(8,128)(2,1)S(1)}, u32[]{:S(2)}, u32[]{:S(2)}) collective-permute-start(bf16[2048,128]{1,0:T(8,128)(2,1)S(1)} %get-tuple-element.49.refs_4_), channel_id=1, source_target_pairs={{0,1},{1,0},{2,3},{3,2},{4,5},{5,4},{6,7},{7,6},{8,9},{9,8},{10,11... | collective-permute-start | bytes 1572872 | tf_op jit(solution)/shard_map/ppermute | solution.py:333
  45.9 5.5 %collective-permute-start.18 = (bf16[2048,128]{1,0:T(8,128)(2,1)S(1)}, bf16[2048,128]{1,0:T(8,128)(2,1)S(1)}, u32[]{:S(2)}, u32[]{:S(2)}) collective-permute-start(bf16[2048,128]{1,0:T(8,128)(2,1)S(1)} %get-tuple-element.47.refs_6_), channel_id=1, source_target_pairs={{0,1},{1,0},{2,3},{3,2},{4,5},{5,4},{6,7},{7,6},{8,9},{9,8},{10,11... | collective-permute-start | bytes 1572872 | tf_op jit(solution)/shard_map/ppermute | solution.py:333
  46.3 14.7 %collective-permute-start.11 = (bf16[2048,128]{1,0:T(8,128)(2,1)S(1)}, bf16[2048,128]{1,0:T(8,128)(2,1)S(1)}, u32[]{:S(2)}, u32[]{:S(2)}) collective-permute-start(bf16[2048,128]{1,0:T(8,128)(2,1)S(1)} %get-tuple-element.46.refs_0_), channel_id=1, source_target_pairs={{0,4},{1,3},{2,6},{3,1},{4,0},{5,7},{6,2},{7,5},{8,12},{9,11},{10,... | collective-permute-start | bytes 1572872 | tf_op jit(solution)/shard_map/ppermute | solution.py:333
  48.6 14.9 %collective-permute-start.12 = (bf16[2048,128]{1,0:T(8,128)(2,1)S(1)}, bf16[2048,128]{1,0:T(8,128)(2,1)S(1)}, u32[]{:S(2)}, u32[]{:S(2)}) collective-permute-start(bf16[2048,128]{1,0:T(8,128)(2,1)S(1)} %get-tuple-element.47.refs_6_), channel_id=1, source_target_pairs={{0,2},{1,5},{2,0},{3,7},{4,6},{5,1},{6,4},{7,3},{8,10},{9,13},{10,... | collective-permute-start | bytes 1572872 | tf_op jit(solution)/shard_map/ppermute | solution.py:333
  48.6 18.4 %collective-permute-start.13 = (bf16[2048,128]{1,0:T(8,128)(2,1)S(1)}, bf16[2048,128]{1,0:T(8,128)(2,1)S(1)}, u32[]{:S(2)}, u32[]{:S(2)}) collective-permute-start(bf16[2048,128]{1,0:T(8,128)(2,1)S(1)} %get-tuple-element.47.refs_6_), channel_id=1, source_target_pairs={{0,4},{1,3},{2,6},{3,1},{4,0},{5,7},{6,2},{7,5},{8,12},{9,11},{10,... | collective-permute-start | bytes 1572872 | tf_op jit(solution)/shard_map/ppermute | solution.py:333
  50.3 16.7 %collective-permute-start.14 = (bf16[2048,128]{1,0:T(8,128)(2,1)S(1)}, bf16[2048,128]{1,0:T(8,128)(2,1)S(1)}, u32[]{:S(2)}, u32[]{:S(2)}) collective-permute-start(bf16[2048,128]{1,0:T(8,128)(2,1)S(1)} %get-tuple-element.47.refs_6_), channel_id=1, source_target_pairs={{0,8},{1,9},{2,10},{3,11},{4,12},{5,13},{6,14},{7,15},{8,16},{9,17... | collective-permute-start | bytes 1572872 | tf_op jit(solution)/shard_map/ppermute | solution.py:333
  68.3 4.2 %collective-permute-start.24 = (bf16[2048,128]{1,0:T(8,128)(2,1)S(1)}, bf16[2048,128]{1,0:T(8,128)(2,1)S(1)}, u32[]{:S(2)}, u32[]{:S(2)}) collective-permute-start(bf16[2048,128]{1,0:T(8,128)(2,1)S(1)} %get-tuple-element.58.refs_4_), channel_id=1, source_target_pairs={{0,1},{1,0},{2,3},{3,2},{4,5},{5,4},{6,7},{7,6},{8,9},{9,8},{10,11... | collective-permute-start | bytes 1572872 | tf_op jit(solution)/shard_map/ppermute | solution.py:333
  68.4 4.1 %collective-permute-start.25 = (bf16[2048,128]{1,0:T(8,128)(2,1)S(1)}, bf16[2048,128]{1,0:T(8,128)(2,1)S(1)}, u32[]{:S(2)}, u32[]{:S(2)}) collective-permute-start(bf16[2048,128]{1,0:T(8,128)(2,1)S(1)} %get-tuple-element.56.refs_6_), channel_id=1, source_target_pairs={{0,1},{1,0},{2,3},{3,2},{4,5},{5,4},{6,7},{7,6},{8,9},{9,8},{10,11... | collective-permute-start | bytes 1572872 | tf_op jit(solution)/shard_map/ppermute | solution.py:333
  68.8 14.5 %collective-permute-start.19 = (bf16[2048,128]{1,0:T(8,128)(2,1)S(1)}, bf16[2048,128]{1,0:T(8,128)(2,1)S(1)}, u32[]{:S(2)}, u32[]{:S(2)}) collective-permute-start(bf16[2048,128]{1,0:T(8,128)(2,1)S(1)} %get-tuple-element.55.refs_0_), channel_id=1, source_target_pairs={{0,4},{1,3},{2,6},{3,1},{4,0},{5,7},{6,2},{7,5},{8,12},{9,11},{10,... | collective-permute-start | bytes 1572872 | tf_op jit(solution)/shard_map/ppermute | solution.py:333
  70.8 14.9 %collective-permute-start.20 = (bf16[2048,128]{1,0:T(8,128)(2,1)S(1)}, bf16[2048,128]{1,0:T(8,128)(2,1)S(1)}, u32[]{:S(2)}, u32[]{:S(2)}) collective-permute-start(bf16[2048,128]{1,0:T(8,128)(2,1)S(1)} %get-tuple-element.56.refs_6_), channel_id=1, source_target_pairs={{0,2},{1,5},{2,0},{3,7},{4,6},{5,1},{6,4},{7,3},{8,10},{9,13},{10,... | collective-permute-start | bytes 1572872 | tf_op jit(solution)/shard_map/ppermute | solution.py:333
  70.8 18.4 %collective-permute-start.21 = (bf16[2048,128]{1,0:T(8,128)(2,1)S(1)}, bf16[2048,128]{1,0:T(8,128)(2,1)S(1)}, u32[]{:S(2)}, u32[]{:S(2)}) collective-permute-start(bf16[2048,128]{1,0:T(8,128)(2,1)S(1)} %get-tuple-element.56.refs_6_), channel_id=1, source_target_pairs={{0,4},{1,3},{2,6},{3,1},{4,0},{5,7},{6,2},{7,5},{8,12},{9,11},{10,... | collective-permute-start | bytes 1572872 | tf_op jit(solution)/shard_map/ppermute | solution.py:333
  90.5 10.4 %collective-permute-start.26 = (bf16[2048,128]{1,0:T(8,128)(2,1)S(1)}, bf16[2048,128]{1,0:T(8,128)(2,1)S(1)}, u32[]{:S(2)}, u32[]{:S(2)}) collective-permute-start(bf16[2048,128]{1,0:T(8,128)(2,1)S(1)} %get-tuple-element.64.refs_0_), channel_id=1, source_target_pairs={{0,4},{1,3},{2,6},{3,1},{4,0},{5,7},{6,2},{7,5},{8,12},{9,11},{10,... | collective-permute-start | bytes 1572872 | tf_op jit(solution)/shard_map/ppermute | solution.py:333
  (23 other events, 99.7 us)

commit v4 on v3

--- a/solution.py
+++ b/solution.py
@@ -13,7 +13,7 @@
 LANES = 128
 CHAINS = 4
 UNROLL = 32
-VMEM = 32 << 20
+VMEM = 18 << 20
 SMEM_SPEC = pl.BlockSpec(memory_space=pltpu.SMEM)
 ANY_SPEC = pl.BlockSpec(memory_space=pl.ANY)
 HBM_SPEC = pl.BlockSpec(memory_space=pltpu.HBM)
@@ -64,12 +64,17 @@
     )(miss_slot, fill_block, cache_rows, fills)
 
 
+PICK = [1]
+
+
 def gate_kernel(*refs):
     pass
 
 
 def gate(arrays, after):
     n_arrays = len(arrays)
+    if not arrays:
+        return []
     return pl.pallas_call(
         gate_kernel,
         out_shape=[jax.ShapeDtypeStruct(one.shape, one.dtype) for one in arrays],
@@ -164,7 +169,7 @@
             ).astype(jnp.bfloat16)
         return 0
 
-    lax.fori_loop(0, queries // 16, sixteen_queries, 0)
+    lax.fori_loop(0, queries // 16, sixteen_queries, 0, unroll=4)
 
 
 def inter_columns(masked, dense_ref, inter, queries):
@@ -256,7 +261,7 @@
         input_output_aliases={3 + n_shards + k: k for k in range(len(sums))},
         scratch_shapes=pool_scratch(n_shards, shards[0].shape[0], entries[1].shape[0] // entries[0].shape[0]),
         compiler_params=pltpu.CompilerParams(vmem_limit_bytes=VMEM),
-        cost_estimate=pl.CostEstimate(flops=0, bytes_accessed=n_shards * 6_000_000, transcendentals=0),
+        cost_estimate=pl.CostEstimate(flops=0, bytes_accessed=n_shards * 3000000, transcendentals=0),
         name="pool",
     )(*entries, *shards, *sums)
     return sums, done
@@ -371,12 +376,13 @@
         return [array, other_core(array)]
 
     crossed, turned, next_piece = first_hop(own), second_hop(own), next_plane(own)
-    sums, _ = pool(0, entries, of_chip(own), None, sum_rows)
+    sums, done = pool(0, entries, of_chip(own), None, sum_rows)
+    (next_piece,) = gate([next_piece], done)
     far = []
     for shift in range(n_planes):
         last = shift == n_planes - 1
         near = of_chip(crossed) + of_chip(turned)
-        next_far = second_hop(crossed)
+        next_far = next_plane(far[0]) if shift == n_planes - 2 else second_hop(crossed)
         passed = [next_far]
         if not last:
             passed += [first_hop(next_piece), second_hop(next_piece)]
@@ -390,7 +396,10 @@
         else:
             shards, rows = near + far + piece, list(range(6 + len(piece)))
         sums, done = pool(8 * shift + 8, entries, shards, sums, sum_rows, rows)
-        next_far, *passed = gate(passed, done)
+        chosen = [0] if last else [index for index in PICK if index < len(passed)]
+        for index, one in zip(chosen, gate([passed[index] for index in chosen], done)):
+            passed[index] = one
+        next_far, *passed = passed
         far = of_chip(next_far)
         if not last:
             crossed, turned, *next_piece = passed

time: 119 us -> 104 us (0.87)
  local copies, waits for them, and re-layouts: 9.34 us -> 3.46 us
  starting transfers between devices: 26.4 us -> 22 us
  waiting for transfers between devices: 27.3 us -> 24.3 us
  Pallas kernels: 54.8 us -> 52.7 us
    ppermute x31, starting transfers between devices: 26.4 us -> 22 us  [hop(): return lambda array: lax.ppermute(array, 'cache', pairs)]
    unnamed x32 -> x12, local copies, waits for them, and re-layouts: 5.38 us -> 1.05 us
    pallas_call x1, Pallas kernels: 14.3 us -> 11.3 us  [finish(): pl.pallas_call(functools.partial(final_kernel, first, n_shards, head is n...]
    ppermute x31, waiting for transfers between devices: 27.3 us -> 24.3 us  [hop(): return lambda array: lax.ppermute(array, 'cache', pairs)]
    pallas_call x4 -> x5, Pallas kernels: 2.59 us -> 3.23 us  [gate(): pl.pallas_call(gate_kernel, out_shape=[jax.ShapeDtypeStruct(one.shape, on...]
  transfers between devices with their start and end apart: 31 -> 31, of which waited for: 8 -> 12; matrix products, arithmetic and copies ran while one was open for 4% -> 3% of each run, Pallas kernels for 30% -> 37%
where the time goes in v4:
time: 104 us; the launch traced here: 103 us
  Pallas kernels  52.7 us (51%)
  waiting for transfers between devices  24.3 us (23%)
  starting transfers between devices  22 us (21%)
  local copies, waits for them, and re-layouts  3.46 us (3%)
    pallas_call x5, Pallas kernels, pool(): pl.pallas_call(functools.partial(pool_kernel, first, rows, is_first), out...  35.4 us
    ppermute x31, waiting for transfers between devices, hop(): return lambda array: lax.ppermute(array, 'cache', pairs)  24.3 us
    ppermute x31, starting transfers between devices, hop(): return lambda array: lax.ppermute(array, 'cache', pairs)  22 us
    pallas_call x1, Pallas kernels, finish(): pl.pallas_call(functools.partial(final_kernel, first, n_shards, head is n...  11.3 us
    pallas_call x5, Pallas kernels, gate(): pl.pallas_call(gate_kernel, out_shape=[jax.ShapeDtypeStruct(one.shape, on...  3.23 us
    pallas_call x1, Pallas kernels, fill(): pl.pallas_call(fill_kernel, out_shape=jax.ShapeDtypeStruct(cache_rows.sha...  2.75 us
  transfers between devices with their start and end apart: 31, of which 12 were waited for; matrix products, arithmetic and copies ran while one was open for 3% of the time, Pallas kernels for 37%

profile of v4, /device:TPU:0, one launch (start us, length us, event | category | flops | bytes accessed | tf_op | source)
XLA Modules:
  0.0 103.1 jit_solution(17537061089012902409)
XLA Ops:
  0.0 2.8 %fill.1.refs_0_ = bf16[2048,128]{1,0:T(8,128)(2,1)} custom-call(s32[2]{0:T(128)} %bitcast.42, s32[2]{0:T(128)} %bitcast.43, bf16[2048,128]{1,0:T(8,128)(2,1)} %cache_ref.1, bf16[1024,128]{1,0:T(8,128)(2,1)} %fills_ref.1), custom_call_target="tpu_custom_call" | custom-call | tf_op jit(solution)/shard_map/fill/pallas_call | solution.py:57
  3.3 2.6 %collective-permute-start = (bf16[2048,128]{1,0:T(8,128)(2,1)}, bf16[2048,128]{1,0:T(8,128)(2,1)S(1)}, u32[]{:S(2)}, u32[]{:S(2)}) collective-permute-start(bf16[2048,128]{1,0:T(8,128)(2,1)} %fill.1.refs_0_), channel_id=1, source_target_pairs={{0,8},{1,9},{2,10},{3,11},{4,12},{5,13},{6,14},{7,15},{8,16},{9,17... | collective-permute-start | bytes 1572872 | tf_op jit(solution)/shard_map/ppermute | solution.py:338
  5.9 1.5 %collective-permute-start.7 = (bf16[2048,128]{1,0:T(8,128)(2,1)}, bf16[2048,128]{1,0:T(8,128)(2,1)S(1)}, u32[]{:S(2)}, u32[]{:S(2)}) collective-permute-start(bf16[2048,128]{1,0:T(8,128)(2,1)} %fill.1.refs_0_), channel_id=1, source_target_pairs={{0,2},{1,5},{2,0},{3,7},{4,6},{5,1},{6,4},{7,3},{8,10},{9,13},{10,... | collective-permute-start | bytes 1572872 | tf_op jit(solution)/shard_map/ppermute | solution.py:338
  7.4 1.5 %collective-permute-start.9 = (bf16[2048,128]{1,0:T(8,128)(2,1)}, bf16[2048,128]{1,0:T(8,128)(2,1)S(1)}, u32[]{:S(2)}, u32[]{:S(2)}) collective-permute-start(bf16[2048,128]{1,0:T(8,128)(2,1)} %fill.1.refs_0_), channel_id=1, source_target_pairs={{0,4},{1,3},{2,6},{3,1},{4,0},{5,7},{6,2},{7,5},{8,12},{9,11},{10,... | collective-permute-start | bytes 1572872 | tf_op jit(solution)/shard_map/ppermute | solution.py:338
  10.1 1.6 %gather_fusion.1 = s32[48,624]{1,0:T(8,128)S(1)} fusion(s32[32,624]{1,0:T(8,128)} %bitcast.41, s32[1024]{0:T(1024)S(1)} %pad_clamp_fusion), kind=kCustom, calls=%fused_computation.1 | custom fusion | bytes 239808 | tf_op jit(solution)/shard_map/gather | solution.py:367
  12.7 4.2 %pool.5 = (f32[9992,128]{1,0:T(8,128)S(1)}, f32[9992,128]{1,0:T(8,128)S(1)}, f32[9992,128]{1,0:T(8,128)S(1)}, f32[9992,128]{1,0:T(8,128)S(1)}, s32[1]{0:T(128)}) custom-call(s32[48]{0:T(128)S(1)} %and_select_fusion.count_ref, s32[30720]{0:T(1024)S(1)} %reshape.1462.slot_ref, s32[30720]{0:T(1024)S(1)} %reshape.1463.bag_ref, bf16[2048,128]{1,0:T(8,128)(2,1)S(1)} %copy-done.2, ...), custom_call_target="tpu_custom_call" | custom-call | bytes 6000000 | tf_op jit(solution)/shard_map/pool/pallas_call | solution.py:255
  16.9 3.8 %collective-permute-done.refs_0_ = bf16[2048,128]{1,0:T(8,128)(2,1)S(1)} collective-permute-done((bf16[2048,128]{1,0:T(8,128)(2,1)}, bf16[2048,128]{1,0:T(8,128)(2,1)S(1)}, u32[]{:S(2)}, u32[]{:S(2)}) %collective-permute-start) | collective-permute-done | bytes 524320 | tf_op jit(solution)/shard_map/ppermute | solution.py:338
  22.0 1.5 %collective-permute-start.6 = (bf16[2048,128]{1,0:T(8,128)(2,1)S(1)}, bf16[2048,128]{1,0:T(8,128)(2,1)S(1)}, u32[]{:S(2)}, u32[]{:S(2)}) collective-permute-start(bf16[2048,128]{1,0:T(8,128)(2,1)S(1)} %gate.5.refs_4_), channel_id=1, source_target_pairs={{0,2},{1,5},{2,0},{3,7},{4,6},{5,1},{6,4},{7,3},{8,10},{9,13},{10,... | collective-permute-start | bytes 1572872 | tf_op jit(solution)/shard_map/ppermute | solution.py:338
  23.5 1.5 %collective-permute-start.13 = (bf16[2048,128]{1,0:T(8,128)(2,1)S(1)}, bf16[2048,128]{1,0:T(8,128)(2,1)S(1)}, u32[]{:S(2)}, u32[]{:S(2)}) collective-permute-start(bf16[2048,128]{1,0:T(8,128)(2,1)S(1)} %gate.5.refs_4_), channel_id=1, source_target_pairs={{0,4},{1,3},{2,6},{3,1},{4,0},{5,7},{6,2},{7,5},{8,12},{9,11},{10,... | collective-permute-start | bytes 1572872 | tf_op jit(solution)/shard_map/ppermute | solution.py:338
  26.2 7.0 %pool.6 = (f32[9992,128]{1,0:T(8,128)S(1)}, f32[9992,128]{1,0:T(8,128)S(1)}, f32[9992,128]{1,0:T(8,128)S(1)}, f32[9992,128]{1,0:T(8,128)S(1)}, s32[1]{0:T(128)}) custom-call(s32[48]{0:T(128)S(1)} %and_select_fusion.count_ref, s32[30720]{0:T(1024)S(1)} %reshape.1462.slot_ref, ...), custom_call_target="tpu_custom_call", output_to_operand_aliasing={{0}: (9, {}), {1}: (10, {}), {2}: (11, {}), {3}: (12, {})} | custom-call | bytes 18000000 | tf_op jit(solution)/shard_map/pool/pallas_call | solution.py:255
  33.2 2.9 %collective-permute-done.6.refs_0_ = bf16[2048,128]{1,0:T(8,128)(2,1)S(1)} collective-permute-done((bf16[2048,128]{1,0:T(8,128)(2,1)S(1)}, bf16[2048,128]{1,0:T(8,128)(2,1)S(1)}, u32[]{:S(2)}, u32[]{:S(2)}) %collective-permute-start.6) | collective-permute-done | bytes 524320 | tf_op jit(solution)/shard_map/ppermute | solution.py:338
  37.4 3.1 %collective-permute-done.2.refs_6_ = bf16[2048,128]{1,0:T(8,128)(2,1)S(1)} collective-permute-done((bf16[2048,128]{1,0:T(8,128)(2,1)S(1)}, bf16[2048,128]{1,0:T(8,128)(2,1)S(1)}, u32[]{:S(2)}, u32[]{:S(2)}) %collective-permute-start.2) | collective-permute-done | bytes 524320 | tf_op jit(solution)/shard_map/ppermute | solution.py:338
  40.5 1.4 %collective-permute-done.15.refs_4_ = bf16[2048,128]{1,0:T(8,128)(2,1)S(1)} collective-permute-done((bf16[2048,128]{1,0:T(8,128)(2,1)S(1)}, bf16[2048,128]{1,0:T(8,128)(2,1)S(1)}, u32[]{:S(2)}, u32[]{:S(2)}) %collective-permute-start.15) | collective-permute-done | bytes 524320 | tf_op jit(solution)/shard_map/ppermute | solution.py:338
  42.2 1.5 %collective-permute-start.5 = (bf16[2048,128]{1,0:T(8,128)(2,1)S(1)}, bf16[2048,128]{1,0:T(8,128)(2,1)S(1)}, u32[]{:S(2)}, u32[]{:S(2)}) collective-permute-start(bf16[2048,128]{1,0:T(8,128)(2,1)S(1)} %collective-permute-done.2.refs_6_), channel_id=1, source_target_pairs={{0,2},{1,5},{2,0},{3,7},{4,6},{5,1},{6,4},{7,3},{8,10},{9,13},{10,... | collective-permute-start | bytes 1572872 | tf_op jit(solution)/shard_map/ppermute | solution.py:338
  46.4 8.8 %pool.7 = (f32[9992,128]{1,0:T(8,128)S(1)}, f32[9992,128]{1,0:T(8,128)S(1)}, f32[9992,128]{1,0:T(8,128)S(1)}, f32[9992,128]{1,0:T(8,128)S(1)}, s32[1]{0:T(128)}) custom-call(s32[48]{0:T(128)S(1)} %and_select_fusion.count_ref, s32[30720]{0:T(1024)S(1)} %reshape.1462.slot_ref, ...), custom_call_target="tpu_custom_call", output_to_operand_aliasing={{0}: (11, {}), {1}: (12, {}), {2}: (13, {}), {3}: (14, {})} | custom-call | bytes 24000000 | tf_op jit(solution)/shard_map/pool/pallas_call | solution.py:255
  55.3 1.4 %collective-permute-done.5.refs_0_ = bf16[2048,128]{1,0:T(8,128)(2,1)S(1)} collective-permute-done((bf16[2048,128]{1,0:T(8,128)(2,1)S(1)}, bf16[2048,128]{1,0:T(8,128)(2,1)S(1)}, u32[]{:S(2)}, u32[]{:S(2)}) %collective-permute-start.5) | collective-permute-done | bytes 524320 | tf_op jit(solution)/shard_map/ppermute | solution.py:338
  57.9 3.9 %collective-permute-done.19.refs_2_ = bf16[2048,128]{1,0:T(8,128)(2,1)S(1)} collective-permute-done((bf16[2048,128]{1,0:T(8,128)(2,1)S(1)}, bf16[2048,128]{1,0:T(8,128)(2,1)S(1)}, u32[]{:S(2)}, u32[]{:S(2)}) %collective-permute-start.19) | collective-permute-done | bytes 524320 | tf_op jit(solution)/shard_map/ppermute | solution.py:338
  62.5 1.5 %collective-permute-start.4 = (bf16[2048,128]{1,0:T(8,128)(2,1)S(1)}, bf16[2048,128]{1,0:T(8,128)(2,1)S(1)}, u32[]{:S(2)}, u32[]{:S(2)}) collective-permute-start(bf16[2048,128]{1,0:T(8,128)(2,1)S(1)} %collective-permute-done.3.refs_6_), channel_id=1, source_target_pairs={{0,2},{1,5},{2,0},{3,7},{4,6},{5,1},{6,4},{7,3},{8,10},{9,13},{10,... | collective-permute-start | bytes 1572872 | tf_op jit(solution)/shard_map/ppermute | solution.py:338
  65.4 8.9 %pool.8 = (f32[9992,128]{1,0:T(8,128)S(1)}, f32[9992,128]{1,0:T(8,128)S(1)}, f32[9992,128]{1,0:T(8,128)S(1)}, f32[9992,128]{1,0:T(8,128)S(1)}, s32[1]{0:T(128)}) custom-call(s32[48]{0:T(128)S(1)} %and_select_fusion.count_ref, s32[30720]{0:T(1024)S(1)} %reshape.1462.slot_ref, ...), custom_call_target="tpu_custom_call", output_to_operand_aliasing={{0}: (11, {}), {1}: (12, {}), {2}: (13, {}), {3}: (14, {})} | custom-call | bytes 24000000 | tf_op jit(solution)/shard_map/pool/pallas_call | solution.py:255
  74.3 2.6 %collective-permute-done.4.refs_0_ = bf16[2048,128]{1,0:T(8,128)(2,1)S(1)} collective-permute-done((bf16[2048,128]{1,0:T(8,128)(2,1)S(1)}, bf16[2048,128]{1,0:T(8,128)(2,1)S(1)}, u32[]{:S(2)}, u32[]{:S(2)}) %collective-permute-start.4) | collective-permute-done | bytes 524320 | tf_op jit(solution)/shard_map/ppermute | solution.py:338
  77.7 1.7 %collective-permute-done.28.refs_4_ = bf16[2048,128]{1,0:T(8,128)(2,1)S(1)} collective-permute-done((bf16[2048,128]{1,0:T(8,128)(2,1)S(1)}, bf16[2048,128]{1,0:T(8,128)(2,1)S(1)}, u32[]{:S(2)}, u32[]{:S(2)}) %collective-permute-start.28) | collective-permute-done | bytes 524320 | tf_op jit(solution)/shard_map/ppermute | solution.py:338
  82.0 6.6 %pool.9 = (f32[9992,128]{1,0:T(8,128)S(1)}, f32[9992,128]{1,0:T(8,128)S(1)}, f32[9992,128]{1,0:T(8,128)S(1)}, f32[9992,128]{1,0:T(8,128)S(1)}, s32[1]{0:T(128)}) custom-call(s32[48]{0:T(128)S(1)} %and_select_fusion.count_ref, s32[30720]{0:T(1024)S(1)} %reshape.1462.slot_ref, ...), custom_call_target="tpu_custom_call", output_to_operand_aliasing={{0}: (9, {}), {1}: (10, {}), {2}: (11, {}), {3}: (12, {})} | custom-call | bytes 18000000 | tf_op jit(solution)/shard_map/pool/pallas_call | solution.py:255
  89.8 1.9 %collective-permute-done.30.refs_1_ = bf16[2048,128]{1,0:T(8,128)(2,1)S(1)} collective-permute-done((bf16[2048,128]{1,0:T(8,128)(2,1)S(1)}, bf16[2048,128]{1,0:T(8,128)(2,1)S(1)}, u32[]{:S(2)}, u32[]{:S(2)}) %collective-permute-start.30) | collective-permute-done | bytes 524320 | tf_op jit(solution)/shard_map/ppermute | solution.py:338
  91.7 11.3 %finish.1 = (f32[384]{0:T(512)}, f32[9992,128]{1,0:T(8,128)S(1)}, f32[9992,128]{1,0:T(8,128)S(1)}, f32[9992,128]{1,0:T(8,128)S(1)}, f32[9992,128]{1,0:T(8,128)S(1)}) custom-call(s32[48]{0:T(128)S(1)} %and_select_fusion.count_ref, s32[30720]{0:T(1024)S(1)} %reshape.1462.slot_ref, ...), custom_call_target="tpu_custom_call", output_to_operand_aliasing={{1}: (5, {}), {2}: (6, {}), {3}: (7, {}), {4}: (8, {})} | custom-call | tf_op jit(solution)/shard_map/finish/pallas_call | solution.py:289
  (74 shorter events, 17.3 us)
Async XLA Ops:
  2.8 8.9 %collective-permute-start.1 = (bf16[2048,128]{1,0:T(8,128)(2,1)}, bf16[2048,128]{1,0:T(8,128)(2,1)S(1)}, u32[]{:S(2)}, u32[]{:S(2)}) collective-permute-start(bf16[2048,128]{1,0:T(8,128)(2,1)} %fill.1.refs_0_), channel_id=1, source_target_pairs={{0,1},{1,0},{2,3},{3,2},{4,5},{5,4},{6,7},{7,6},{8,9},{9,8},{10,11... | collective-permute-start | bytes 1572872 | tf_op jit(solution)/shard_map/ppermute | solution.py:338
  3.3 17.4 %collective-permute-start = (bf16[2048,128]{1,0:T(8,128)(2,1)}, bf16[2048,128]{1,0:T(8,128)(2,1)S(1)}, u32[]{:S(2)}, u32[]{:S(2)}) collective-permute-start(bf16[2048,128]{1,0:T(8,128)(2,1)} %fill.1.refs_0_), channel_id=1, source_target_pairs={{0,8},{1,9},{2,10},{3,11},{4,12},{5,13},{6,14},{7,15},{8,16},{9,17... | collective-permute-start | bytes 1572872 | tf_op jit(solution)/shard_map/ppermute | solution.py:338
  5.9 15.5 %collective-permute-start.7 = (bf16[2048,128]{1,0:T(8,128)(2,1)}, bf16[2048,128]{1,0:T(8,128)(2,1)S(1)}, u32[]{:S(2)}, u32[]{:S(2)}) collective-permute-start(bf16[2048,128]{1,0:T(8,128)(2,1)} %fill.1.refs_0_), channel_id=1, source_target_pairs={{0,2},{1,5},{2,0},{3,7},{4,6},{5,1},{6,4},{7,3},{8,10},{9,13},{10,... | collective-permute-start | bytes 1572872 | tf_op jit(solution)/shard_map/ppermute | solution.py:338
  7.4 14.5 %collective-permute-start.9 = (bf16[2048,128]{1,0:T(8,128)(2,1)}, bf16[2048,128]{1,0:T(8,128)(2,1)S(1)}, u32[]{:S(2)}, u32[]{:S(2)}) collective-permute-start(bf16[2048,128]{1,0:T(8,128)(2,1)} %fill.1.refs_0_), channel_id=1, source_target_pairs={{0,4},{1,3},{2,6},{3,1},{4,0},{5,7},{6,2},{7,5},{8,12},{9,11},{10,... | collective-permute-start | bytes 1572872 | tf_op jit(solution)/shard_map/ppermute | solution.py:338
  21.4 4.1 %collective-permute-start.8 = (bf16[2048,128]{1,0:T(8,128)(2,1)S(1)}, bf16[2048,128]{1,0:T(8,128)(2,1)S(1)}, u32[]{:S(2)}, u32[]{:S(2)}) collective-permute-start(bf16[2048,128]{1,0:T(8,128)(2,1)S(1)} %collective-permute-done.7.refs_0_), channel_id=1, source_target_pairs={{0,1},{1,0},{2,3},{3,2},{4,5},{5,4},{6,7},{7,6},{8,9},{9,8},{10,11... | collective-permute-start | bytes 1572872 | tf_op jit(solution)/shard_map/ppermute | solution.py:338
  21.9 4.3 %collective-permute-start.10 = (bf16[2048,128]{1,0:T(8,128)(2,1)S(1)}, bf16[2048,128]{1,0:T(8,128)(2,1)S(1)}, u32[]{:S(2)}, u32[]{:S(2)}) collective-permute-start(bf16[2048,128]{1,0:T(8,128)(2,1)S(1)} %collective-permute-done.9.refs_2_), channel_id=1, source_target_pairs={{0,1},{1,0},{2,3},{3,2},{4,5},{5,4},{6,7},{7,6},{8,9},{9,8},{10,11... | collective-permute-start | bytes 1572872 | tf_op jit(solution)/shard_map/ppermute | solution.py:338
  22.0 14.1 %collective-permute-start.6 = (bf16[2048,128]{1,0:T(8,128)(2,1)S(1)}, bf16[2048,128]{1,0:T(8,128)(2,1)S(1)}, u32[]{:S(2)}, u32[]{:S(2)}) collective-permute-start(bf16[2048,128]{1,0:T(8,128)(2,1)S(1)} %gate.5.refs_4_), channel_id=1, source_target_pairs={{0,2},{1,5},{2,0},{3,7},{4,6},{5,1},{6,4},{7,3},{8,10},{9,13},{10,... | collective-permute-start | bytes 1572872 | tf_op jit(solution)/shard_map/ppermute | solution.py:338
  23.5 13.4 %collective-permute-start.13 = (bf16[2048,128]{1,0:T(8,128)(2,1)S(1)}, bf16[2048,128]{1,0:T(8,128)(2,1)S(1)}, u32[]{:S(2)}, u32[]{:S(2)}) collective-permute-start(bf16[2048,128]{1,0:T(8,128)(2,1)S(1)} %gate.5.refs_4_), channel_id=1, source_target_pairs={{0,4},{1,3},{2,6},{3,1},{4,0},{5,7},{6,2},{7,5},{8,12},{9,11},{10,... | collective-permute-start | bytes 1572872 | tf_op jit(solution)/shard_map/ppermute | solution.py:338
  25.0 15.5 %collective-permute-start.2 = (bf16[2048,128]{1,0:T(8,128)(2,1)S(1)}, bf16[2048,128]{1,0:T(8,128)(2,1)S(1)}, u32[]{:S(2)}, u32[]{:S(2)}) collective-permute-start(bf16[2048,128]{1,0:T(8,128)(2,1)S(1)} %gate.5.refs_4_), channel_id=1, source_target_pairs={{0,8},{1,9},{2,10},{3,11},{4,12},{5,13},{6,14},{7,15},{8,16},{9,17... | collective-permute-start | bytes 1572872 | tf_op jit(solution)/shard_map/ppermute | solution.py:338
  25.5 16.4 %collective-permute-start.15 = (bf16[2048,128]{1,0:T(8,128)(2,1)S(1)}, bf16[2048,128]{1,0:T(8,128)(2,1)S(1)}, u32[]{:S(2)}, u32[]{:S(2)}) collective-permute-start(bf16[2048,128]{1,0:T(8,128)(2,1)S(1)} %collective-permute-done.7.refs_0_), channel_id=1, source_target_pairs={{0,4},{1,3},{2,6},{3,1},{4,0},{5,7},{6,2},{7,5},{8,12},{9,11},{10,... | collective-permute-start | bytes 1572872 | tf_op jit(solution)/shard_map/ppermute | solution.py:338
  36.8 6.9 %collective-permute-start.12 = (bf16[2048,128]{1,0:T(8,128)(2,1)S(1)}, bf16[2048,128]{1,0:T(8,128)(2,1)S(1)}, u32[]{:S(2)}, u32[]{:S(2)}) collective-permute-start(bf16[2048,128]{1,0:T(8,128)(2,1)S(1)} %gate.6.refs_0_), channel_id=1, source_target_pairs={{0,1},{1,0},{2,3},{3,2},{4,5},{5,4},{6,7},{7,6},{8,9},{9,8},{10,11... | collective-permute-start | bytes 1572872 | tf_op jit(solution)/shard_map/ppermute | solution.py:338
  36.9 8.1 %collective-permute-start.14 = (bf16[2048,128]{1,0:T(8,128)(2,1)S(1)}, bf16[2048,128]{1,0:T(8,128)(2,1)S(1)}, u32[]{:S(2)}, u32[]{:S(2)}) collective-permute-start(bf16[2048,128]{1,0:T(8,128)(2,1)S(1)} %collective-permute-done.13.refs_2_), channel_id=1, source_target_pairs={{0,1},{1,0},{2,3},{3,2},{4,5},{5,4},{6,7},{7,6},{8,9},{9,8},{10,11... | collective-permute-start | bytes 1572872 | tf_op jit(solution)/shard_map/ppermute | solution.py:338
  40.5 5.3 %collective-permute-start.17 = (bf16[2048,128]{1,0:T(8,128)(2,1)S(1)}, bf16[2048,128]{1,0:T(8,128)(2,1)S(1)}, u32[]{:S(2)}, u32[]{:S(2)}) collective-permute-start(bf16[2048,128]{1,0:T(8,128)(2,1)S(1)} %collective-permute-done.2.refs_6_), channel_id=1, source_target_pairs={{0,1},{1,0},{2,3},{3,2},{4,5},{5,4},{6,7},{7,6},{8,9},{9,8},{10,11... | collective-permute-start | bytes 1572872 | tf_op jit(solution)/shard_map/ppermute | solution.py:338
  41.9 4.6 %collective-permute-start.16 = (bf16[2048,128]{1,0:T(8,128)(2,1)S(1)}, bf16[2048,128]{1,0:T(8,128)(2,1)S(1)}, u32[]{:S(2)}, u32[]{:S(2)}) collective-permute-start(bf16[2048,128]{1,0:T(8,128)(2,1)S(1)} %collective-permute-done.15.refs_4_), channel_id=1, source_target_pairs={{0,1},{1,0},{2,3},{3,2},{4,5},{5,4},{6,7},{7,6},{8,9},{9,8},{10,11... | collective-permute-start | bytes 1572872 | tf_op jit(solution)/shard_map/ppermute | solution.py:338
  42.2 14.5 %collective-permute-start.5 = (bf16[2048,128]{1,0:T(8,128)(2,1)S(1)}, bf16[2048,128]{1,0:T(8,128)(2,1)S(1)}, u32[]{:S(2)}, u32[]{:S(2)}) collective-permute-start(bf16[2048,128]{1,0:T(8,128)(2,1)S(1)} %collective-permute-done.2.refs_6_), channel_id=1, source_target_pairs={{0,2},{1,5},{2,0},{3,7},{4,6},{5,1},{6,4},{7,3},{8,10},{9,13},{10,... | collective-permute-start | bytes 1572872 | tf_op jit(solution)/shard_map/ppermute | solution.py:338
  43.7 13.7 %collective-permute-start.21 = (bf16[2048,128]{1,0:T(8,128)(2,1)S(1)}, bf16[2048,128]{1,0:T(8,128)(2,1)S(1)}, u32[]{:S(2)}, u32[]{:S(2)}) collective-permute-start(bf16[2048,128]{1,0:T(8,128)(2,1)S(1)} %gate.6.refs_0_), channel_id=1, source_target_pairs={{0,4},{1,3},{2,6},{3,1},{4,0},{5,7},{6,2},{7,5},{8,12},{9,11},{10,... | collective-permute-start | bytes 1572872 | tf_op jit(solution)/shard_map/ppermute | solution.py:338
  45.0 16.8 %collective-permute-start.19 = (bf16[2048,128]{1,0:T(8,128)(2,1)S(1)}, bf16[2048,128]{1,0:T(8,128)(2,1)S(1)}, u32[]{:S(2)}, u32[]{:S(2)}) collective-permute-start(bf16[2048,128]{1,0:T(8,128)(2,1)S(1)} %collective-permute-done.2.refs_6_), channel_id=1, source_target_pairs={{0,4},{1,3},{2,6},{3,1},{4,0},{5,7},{6,2},{7,5},{8,12},{9,11},{10,... | collective-permute-start | bytes 1572872 | tf_op jit(solution)/shard_map/ppermute | solution.py:338
  45.8 16.7 %collective-permute-start.3 = (bf16[2048,128]{1,0:T(8,128)(2,1)S(1)}, bf16[2048,128]{1,0:T(8,128)(2,1)S(1)}, u32[]{:S(2)}, u32[]{:S(2)}) collective-permute-start(bf16[2048,128]{1,0:T(8,128)(2,1)S(1)} %collective-permute-done.2.refs_6_), channel_id=1, source_target_pairs={{0,8},{1,9},{2,10},{3,11},{4,12},{5,13},{6,14},{7,15},{8,16},{9,17... | collective-permute-start | bytes 1572872 | tf_op jit(solution)/shard_map/ppermute | solution.py:338
  57.4 6.6 %collective-permute-start.18 = (bf16[2048,128]{1,0:T(8,128)(2,1)S(1)}, bf16[2048,128]{1,0:T(8,128)(2,1)S(1)}, u32[]{:S(2)}, u32[]{:S(2)}) collective-permute-start(bf16[2048,128]{1,0:T(8,128)(2,1)S(1)} %gate.7.refs_0_), channel_id=1, source_target_pairs={{0,1},{1,0},{2,3},{3,2},{4,5},{5,4},{6,7},{7,6},{8,9},{9,8},{10,11... | collective-permute-start | bytes 1572872 | tf_op jit(solution)/shard_map/ppermute | solution.py:338
  57.4 7.0 %collective-permute-start.22 = (bf16[2048,128]{1,0:T(8,128)(2,1)S(1)}, bf16[2048,128]{1,0:T(8,128)(2,1)S(1)}, u32[]{:S(2)}, u32[]{:S(2)}) collective-permute-start(bf16[2048,128]{1,0:T(8,128)(2,1)S(1)} %collective-permute-done.21.refs_4_), channel_id=1, source_target_pairs={{0,1},{1,0},{2,3},{3,2},{4,5},{5,4},{6,7},{7,6},{8,9},{9,8},{10,11... | collective-permute-start | bytes 1572872 | tf_op jit(solution)/shard_map/ppermute | solution.py:338
  62.5 14.4 %collective-permute-start.4 = (bf16[2048,128]{1,0:T(8,128)(2,1)S(1)}, bf16[2048,128]{1,0:T(8,128)(2,1)S(1)}, u32[]{:S(2)}, u32[]{:S(2)}) collective-permute-start(bf16[2048,128]{1,0:T(8,128)(2,1)S(1)} %collective-permute-done.3.refs_6_), channel_id=1, source_target_pairs={{0,2},{1,5},{2,0},{3,7},{4,6},{5,1},{6,4},{7,3},{8,10},{9,13},{10,... | collective-permute-start | bytes 1572872 | tf_op jit(solution)/shard_map/ppermute | solution.py:338
  64.0 15.4 %collective-permute-start.28 = (bf16[2048,128]{1,0:T(8,128)(2,1)S(1)}, bf16[2048,128]{1,0:T(8,128)(2,1)S(1)}, u32[]{:S(2)}, u32[]{:S(2)}) collective-permute-start(bf16[2048,128]{1,0:T(8,128)(2,1)S(1)} %collective-permute-done.21.refs_4_), channel_id=1, source_target_pairs={{0,8},{1,9},{2,10},{3,11},{4,12},{5,13},{6,14},{7,15},{8,16},{9,17... | collective-permute-start | bytes 1572872 | tf_op jit(solution)/shard_map/ppermute | solution.py:338
  64.5 14.9 %collective-permute-start.26 = (bf16[2048,128]{1,0:T(8,128)(2,1)S(1)}, bf16[2048,128]{1,0:T(8,128)(2,1)S(1)}, u32[]{:S(2)}, u32[]{:S(2)}) collective-permute-start(bf16[2048,128]{1,0:T(8,128)(2,1)S(1)} %collective-permute-done.3.refs_6_), channel_id=1, source_target_pairs={{0,4},{1,3},{2,6},{3,1},{4,0},{5,7},{6,2},{7,5},{8,12},{9,11},{10,... | collective-permute-start | bytes 1572872 | tf_op jit(solution)/shard_map/ppermute | solution.py:338
  79.9 9.2 %collective-permute-start.24 = (bf16[2048,128]{1,0:T(8,128)(2,1)S(1)}, bf16[2048,128]{1,0:T(8,128)(2,1)S(1)}, u32[]{:S(2)}, u32[]{:S(2)}) collective-permute-start(bf16[2048,128]{1,0:T(8,128)(2,1)S(1)} %gate.8.refs_0_), channel_id=1, source_target_pairs={{0,4},{1,3},{2,6},{3,1},{4,0},{5,7},{6,2},{7,5},{8,12},{9,11},{10,... | collective-permute-start | bytes 1572872 | tf_op jit(solution)/shard_map/ppermute | solution.py:338
  (13 other events, 68.9 us)

commit v5 on v4

--- a/solution.py
+++ b/solution.py
@@ -56,7 +56,7 @@
     n_sems = cache_rows.shape[0] // BLOCK + miss_slot.shape[0]
     return pl.pallas_call(
         fill_kernel,
-        out_shape=jax.ShapeDtypeStruct(cache_rows.shape, cache_rows.dtype),
+        out_shape=pltpu.VMEM(cache_rows.shape, cache_rows.dtype),
         in_specs=[SMEM_SPEC] * 2 + [ANY_SPEC] * 2,
         out_specs=VMEM_SPEC,
         scratch_shapes=[pltpu.SemaphoreType.DMA((n_sems,))],
@@ -78,7 +78,7 @@
     return pl.pallas_call(
         gate_kernel,
         out_shape=[jax.ShapeDtypeStruct(one.shape, one.dtype) for one in arrays],
-        in_specs=[ANY_SPEC] * n_arrays + [SMEM_SPEC],
+        in_specs=[ANY_SPEC] * (n_arrays + 1),
         out_specs=[ANY_SPEC] * n_arrays,
         input_output_aliases={index: index for index in range(n_arrays)},
         compiler_params=pltpu.CompilerParams(vmem_limit_bytes=1 << 20),
@@ -86,7 +86,7 @@
     )(*arrays, after)
 
 
-def pool_shards(first, rows, entry_refs, entry_held, count_ref, shards, sems, held, table, sums):
+def pool_shards(first, rows, entry_refs, entry_held, shards, sems, held, table, sums):
     cap = entry_held[0].shape[0] // 8
     copies = [
         pltpu.make_async_copy(ref.at[pl.ds(first * cap, 8 * cap)], to, sems.at[len(shards) + index])
@@ -116,16 +116,16 @@
                     sums[k][pl.ds(bags[k], 1), :] = olds[k] + found[k]
             return 0
 
-        lax.fori_loop(0, count_ref[first + row], add_entries, 0)
-
-
-def pool_kernel(first, rows, is_first, count_ref, slot_ref, bag_ref, *refs):
+        lax.fori_loop(0, slot_ref[row * cap + cap - 1], add_entries, 0)
+
+
+def pool_kernel(first, rows, is_first, slot_ref, bag_ref, *refs):
     shards, refs = refs[: len(rows)], refs[len(rows) :]
     if not is_first:
         refs = refs[CHAINS:]
-    sums, (done, *entry_held, held, table, sems) = refs[:CHAINS], refs[CHAINS:]
+    sums, (_, *entry_held, held, table, sems) = refs[:CHAINS], refs[CHAINS:]
     pooling = pool_shards(
-        first, rows, (slot_ref, bag_ref), entry_held, count_ref, shards, sems, held, table, sums
+        first, rows, (slot_ref, bag_ref), entry_held, shards, sems, held, table, sums
     )
     next(pooling)
     if is_first:
@@ -133,7 +133,6 @@
             one[...] = jnp.zeros_like(one)
     for _ in pooling:
         pass
-    done[0] = 0
 
 
 def interact(sums, dense_ref, masked, queries):
@@ -196,7 +195,7 @@
         inter[:, (tile + 1) * LANES : (tile + 2) * LANES] = tiles[tile].astype(jnp.bfloat16)
 
 
-def final_kernel(first, n_shards, with_head, count_ref, slot_ref, bag_ref, *refs):
+def final_kernel(first, n_shards, with_head, slot_ref, bag_ref, *refs):
     shards, refs = refs[:n_shards], refs[n_shards:]
     old_sums, dense_ref, refs = refs[:CHAINS], refs[CHAINS], refs[CHAINS + 1 :]
     if with_head:
@@ -215,7 +214,7 @@
     masked, *entry_held, held, table, sems = refs
     queries = dense_ref.shape[0]
     for _ in pool_shards(
-        first, (0, 1), (slot_ref, bag_ref), entry_held, count_ref, shards, sems, held, table, old_sums
+        first, (0, 1), (slot_ref, bag_ref), entry_held, shards, sems, held, table, old_sums
     ):
         pass
     interact(old_sums, dense_ref, masked, queries)
@@ -248,18 +247,18 @@
     ]
 
 
-def pool(first, entries, shards, sums, sum_rows, rows=(0, 1)):
+def pool(first, entries, cap, shards, sums, sum_rows, rows=(0, 1)):
     n_shards = len(shards)
     is_first = sums is None
     sums = [] if is_first else sums
     *sums, done = pl.pallas_call(
         functools.partial(pool_kernel, first, rows, is_first),
         out_shape=[pltpu.VMEM((sum_rows, LANES), jnp.float32)] * CHAINS
-        + [jax.ShapeDtypeStruct((1,), jnp.int32)],
-        in_specs=[SMEM_SPEC] + [HBM_SPEC] * 2 + [ANY_SPEC] * n_shards + [VMEM_SPEC] * len(sums),
-        out_specs=[VMEM_SPEC] * CHAINS + [SMEM_SPEC],
-        input_output_aliases={3 + n_shards + k: k for k in range(len(sums))},
-        scratch_shapes=pool_scratch(n_shards, shards[0].shape[0], entries[1].shape[0] // entries[0].shape[0]),
+        + [jax.ShapeDtypeStruct((8, LANES), jnp.int32)],
+        in_specs=[HBM_SPEC] * 2 + [ANY_SPEC] * n_shards + [VMEM_SPEC] * len(sums),
+        out_specs=[VMEM_SPEC] * CHAINS + [ANY_SPEC],
+        input_output_aliases={2 + n_shards + k: k for k in range(len(sums))},
+        scratch_shapes=pool_scratch(n_shards, shards[0].shape[0], cap),
         compiler_params=pltpu.CompilerParams(vmem_limit_bytes=VMEM),
         cost_estimate=pl.CostEstimate(flops=0, bytes_accessed=n_shards * 3000000, transcendentals=0),
         name="pool",
@@ -267,7 +266,7 @@
     return sums, done
 
 
-def finish(first, entries, shards, sums, dense_rows, head):
+def finish(first, entries, cap, shards, sums, dense_rows, head):
     n_shards = len(shards)
     queries = dense_rows.shape[0]
     width = 4 * LANES
@@ -289,10 +288,10 @@
     out = pl.pallas_call(
         functools.partial(final_kernel, first, n_shards, head is not None),
         out_shape=[out_shape] + [pltpu.VMEM(one.shape, one.dtype) for one in sums],
-        in_specs=[SMEM_SPEC] + [HBM_SPEC] * 2 + [ANY_SPEC] * n_shards + [VMEM_SPEC] * (CHAINS + 1) + head_specs,
+        in_specs=[HBM_SPEC] * 2 + [ANY_SPEC] * n_shards + [VMEM_SPEC] * (CHAINS + 1) + head_specs,
         out_specs=[VMEM_SPEC] * (CHAINS + 1),
-        input_output_aliases={3 + n_shards + k: 1 + k for k in range(CHAINS)},
-        scratch_shapes=scratch + pool_scratch(n_shards, shards[0].shape[0], entries[1].shape[0] // entries[0].shape[0]),
+        input_output_aliases={2 + n_shards + k: 1 + k for k in range(CHAINS)},
+        scratch_shapes=scratch + pool_scratch(n_shards, shards[0].shape[0], cap),
         compiler_params=pltpu.CompilerParams(vmem_limit_bytes=VMEM),
         name="finish",
     )(*entries, *shards, *sums, dense_rows, *head_args)
@@ -362,7 +361,7 @@
     order += both_cores(n_planes - 1, 1, 1) + unused
     order = jnp.stack(order)
     cap = lookup_slot.shape[2]
-    cap += -cap % LANES
+    cap += -cap % LANES or LANES
     spare = ((0, 0), (0, cap - lookup_slot.shape[2]))
     slots = jnp.pad(lookup_slot[0], spare)[order]
     bag_ids = jnp.pad(lookup_bag[0], spare, constant_values=bags)[order]
@@ -370,14 +369,15 @@
     steps = (used + UNROLL - 1) // UNROLL
     sum_rows = bags + 8
     places = jnp.where(bag_ids < bags, bag_ids % F * queries + bag_ids // F, bags)
-    entries = (steps, slots.reshape(-1), places.reshape(-1))
+    slots = jnp.where(jnp.arange(cap) == cap - 1, steps[:, None], slots)
+    entries = (slots.reshape(-1), places.reshape(-1))
 
     def of_chip(array):
         return [array, other_core(array)]
 
     crossed, turned, next_piece = first_hop(own), second_hop(own), next_plane(own)
-    sums, done = pool(0, entries, of_chip(own), None, sum_rows)
-    (next_piece,) = gate([next_piece], done)
+    sums, done = pool(0, entries, cap, of_chip(own), None, sum_rows)
+    (crossed,) = gate([crossed], done)
     far = []
     for shift in range(n_planes):
         last = shift == n_planes - 1
@@ -395,7 +395,7 @@
             shards, rows = near + piece, [0, 1, 2, 3, 6, 7]
         else:
             shards, rows = near + far + piece, list(range(6 + len(piece)))
-        sums, done = pool(8 * shift + 8, entries, shards, sums, sum_rows, rows)
+        sums, done = pool(8 * shift + 8, entries, cap, shards, sums, sum_rows, rows)
         chosen = [0] if last else [index for index in PICK if index < len(passed)]
         for index, one in zip(chosen, gate([passed[index] for index in chosen], done)):
             passed[index] = one
@@ -404,7 +404,7 @@
         if not last:
             crossed, turned, *next_piece = passed
             next_piece = next_piece[0] if next_piece else None
-    args = (8 * n_planes + 8, entries, far, sums, dense_rows)
+    args = (8 * n_planes + 8, entries, cap, far, sums, dense_rows)
     if owners == 1:
         return finish(*args, (w_first, w_second, w_out.reshape(1, -1)))
     inter_in = finish(*args, None)[:, : w_first.shape[0]]

time: 104 us -> 101 us (0.971)
  waiting for transfers between devices: 24.3 us -> 35.3 us
  Pallas kernels: 52.7 us -> 43.4 us
  starting transfers between devices: 22 us -> 18.2 us
  local copies, waits for them, and re-layouts: 3.46 us -> 2.41 us
    ppermute x31, waiting for transfers between devices: 24.3 us -> 35.3 us  [hop(): return lambda array: lax.ppermute(array, 'cache', pairs)]
    pallas_call x5, Pallas kernels: 35.4 us -> 30.9 us  [pool(): pl.pallas_call(functools.partial(pool_kernel, first, rows, is_first), out...]
    ppermute x31, starting transfers between devices: 22 us -> 18.2 us  [hop(): return lambda array: lax.ppermute(array, 'cache', pairs)]
    pallas_call x5, Pallas kernels: 3.23 us -> 0.01 us  [gate(): pl.pallas_call(gate_kernel, out_shape=[jax.ShapeDtypeStruct(one.shape, on...]
  transfers between devices with their start and end apart: 31 -> 31, of which waited for: 12 -> 14; matrix products, arithmetic and copies ran while one was open for 3% -> 3% of each run, Pallas kernels for 37% -> 31%
where the time goes in v5:
time: 101 us; the launch traced here: 100 us
  Pallas kernels  43.4 us (43%)
  waiting for transfers between devices  35.3 us (35%)
  starting transfers between devices  18.2 us (18%)
  local copies, waits for them, and re-layouts  2.41 us (2%)
    ppermute x31, waiting for transfers between devices, hop(): return lambda array: lax.ppermute(array, 'cache', pairs)  35.3 us
    pallas_call x5, Pallas kernels, pool(): pl.pallas_call(functools.partial(pool_kernel, first, rows, is_first), out...  30.9 us
    ppermute x31, starting transfers between devices, hop(): return lambda array: lax.ppermute(array, 'cache', pairs)  18.2 us
    pallas_call x1, Pallas kernels, finish(): pl.pallas_call(functools.partial(final_kernel, first, n_shards, head is n...  10.5 us
  transfers between devices with their start and end apart: 31, of which 14 were waited for; matrix products, arithmetic and copies ran while one was open for 3% of the time, Pallas kernels for 31%

profile of v5, /device:TPU:0, one launch (start us, length us, event | category | flops | bytes accessed | tf_op | source)
XLA Modules:
  0.0 100.1 jit_solution(1250635781501525647)
XLA Ops:
  0.0 2.0 %fill.1.refs_0_ = bf16[2048,128]{1,0:T(8,128)(2,1)S(1)} custom-call(s32[2]{0:T(128)} %bitcast.42, s32[2]{0:T(128)} %bitcast.43, bf16[2048,128]{1,0:T(8,128)(2,1)} %cache_ref.1, bf16[1024,128]{1,0:T(8,128)(2,1)} %fills_ref.1), custom_call_target="tpu_custom_call" | custom-call | tf_op jit(solution)/shard_map/fill/pallas_call | solution.py:57
  2.5 2.6 %collective-permute-start.6 = (bf16[2048,128]{1,0:T(8,128)(2,1)S(1)}, bf16[2048,128]{1,0:T(8,128)(2,1)S(1)}, u32[]{:S(2)}, u32[]{:S(2)}) collective-permute-start(bf16[2048,128]{1,0:T(8,128)(2,1)S(1)} %fill.1.refs_0_), channel_id=1, source_target_pairs={{0,2},{1,5},{2,0},{3,7},{4,6},{5,1},{6,4},{7,3},{8,10},{9,13},{10,... | collective-permute-start | bytes 1572872 | tf_op jit(solution)/shard_map/ppermute | solution.py:337
  5.1 1.6 %collective-permute-start = (bf16[2048,128]{1,0:T(8,128)(2,1)S(1)}, bf16[2048,128]{1,0:T(8,128)(2,1)S(1)}, u32[]{:S(2)}, u32[]{:S(2)}) collective-permute-start(bf16[2048,128]{1,0:T(8,128)(2,1)S(1)} %fill.1.refs_0_), channel_id=1, source_target_pairs={{0,8},{1,9},{2,10},{3,11},{4,12},{5,13},{6,14},{7,15},{8,16},{9,17... | collective-permute-start | bytes 1572872 | tf_op jit(solution)/shard_map/ppermute | solution.py:337
  6.6 1.5 %collective-permute-start.9 = (bf16[2048,128]{1,0:T(8,128)(2,1)S(1)}, bf16[2048,128]{1,0:T(8,128)(2,1)S(1)}, u32[]{:S(2)}, u32[]{:S(2)}) collective-permute-start(bf16[2048,128]{1,0:T(8,128)(2,1)S(1)} %fill.1.refs_0_), channel_id=1, source_target_pairs={{0,4},{1,3},{2,6},{3,1},{4,0},{5,7},{6,2},{7,5},{8,12},{9,11},{10,... | collective-permute-start | bytes 1572872 | tf_op jit(solution)/shard_map/ppermute | solution.py:337
  9.2 1.6 %gather_fusion.1 = s32[48,624]{1,0:T(8,128)S(1)} fusion(s32[32,624]{1,0:T(8,128)} %bitcast.41, s32[1024]{0:T(1024)S(1)} %pad_clamp_fusion), kind=kCustom, calls=%fused_computation.1 | custom fusion | bytes 239808 | tf_op jit(solution)/shard_map/gather | solution.py:366
  11.0 3.2 %pool.5 = (f32[9992,128]{1,0:T(8,128)S(1)}, f32[9992,128]{1,0:T(8,128)S(1)}, f32[9992,128]{1,0:T(8,128)S(1)}, f32[9992,128]{1,0:T(8,128)S(1)}, s32[8,128]{1,0:T(8,128)S(1)}) custom-call(s32[30720]{0:T(1024)S(1)} %reshape.1480.slot_ref, s32[30720]{0:T(1024)S(1)} %reshape.1481.bag_ref, bf16[2048,128]{1,0:T(8,128)(2,1)S(1)} %fill.1.refs_0_, ...), custom_call_target="tpu_custom_call" | custom-call | bytes 6000000 | tf_op jit(solution)/shard_map/pool/pallas_call | solution.py:254
  15.3 5.6 %collective-permute-done.refs_4_ = bf16[2048,128]{1,0:T(8,128)(2,1)S(1)} collective-permute-done((bf16[2048,128]{1,0:T(8,128)(2,1)S(1)}, bf16[2048,128]{1,0:T(8,128)(2,1)S(1)}, u32[]{:S(2)}, u32[]{:S(2)}) %collective-permute-start) | collective-permute-done | bytes 524320 | tf_op jit(solution)/shard_map/ppermute | solution.py:337
  22.1 1.3 %collective-permute-start.15 = (bf16[2048,128]{1,0:T(8,128)(2,1)S(1)}, bf16[2048,128]{1,0:T(8,128)(2,1)S(1)}, u32[]{:S(2)}, u32[]{:S(2)}) collective-permute-start(bf16[2048,128]{1,0:T(8,128)(2,1)S(1)} %gate.5.refs_0_), channel_id=1, source_target_pairs={{0,4},{1,3},{2,6},{3,1},{4,0},{5,7},{6,2},{7,5},{8,12},{9,11},{10,... | collective-permute-start | bytes 1572872 | tf_op jit(solution)/shard_map/ppermute | solution.py:337
  24.4 6.1 %pool.6 = (f32[9992,128]{1,0:T(8,128)S(1)}, f32[9992,128]{1,0:T(8,128)S(1)}, f32[9992,128]{1,0:T(8,128)S(1)}, f32[9992,128]{1,0:T(8,128)S(1)}, s32[8,128]{1,0:T(8,128)S(1)}) custom-call(s32[30720]{0:T(1024)S(1)} %reshape.1480.slot_ref, s32[30720]{0:T(1024)S(1)} %reshape.1481.bag_ref, ...), custom_call_target="tpu_custom_call", output_to_operand_aliasing={{0}: (8, {}), {1}: (9, {}), {2}: (10, {}), {3}: (11, {})} | custom-call | bytes 18000000 | tf_op jit(solution)/shard_map/pool/pallas_call | solution.py:254
  30.4 5.8 %collective-permute-done.5.refs_0_ = bf16[2048,128]{1,0:T(8,128)(2,1)S(1)} collective-permute-done((bf16[2048,128]{1,0:T(8,128)(2,1)S(1)}, bf16[2048,128]{1,0:T(8,128)(2,1)S(1)}, u32[]{:S(2)}, u32[]{:S(2)}) %collective-permute-start.5) | collective-permute-done | bytes 524320 | tf_op jit(solution)/shard_map/ppermute | solution.py:337
  36.7 1.8 %collective-permute-done.1.refs_6_ = bf16[2048,128]{1,0:T(8,128)(2,1)S(1)} collective-permute-done((bf16[2048,128]{1,0:T(8,128)(2,1)S(1)}, bf16[2048,128]{1,0:T(8,128)(2,1)S(1)}, u32[]{:S(2)}, u32[]{:S(2)}) %collective-permute-start.1) | collective-permute-done | bytes 524320 | tf_op jit(solution)/shard_map/ppermute | solution.py:337
  38.5 2.4 %collective-permute-done.13.refs_2_ = bf16[2048,128]{1,0:T(8,128)(2,1)S(1)} collective-permute-done((bf16[2048,128]{1,0:T(8,128)(2,1)S(1)}, bf16[2048,128]{1,0:T(8,128)(2,1)S(1)}, u32[]{:S(2)}, u32[]{:S(2)}) %collective-permute-start.13) | collective-permute-done | bytes 524320 | tf_op jit(solution)/shard_map/ppermute | solution.py:337
  41.0 1.3 %collective-permute-start.4 = (bf16[2048,128]{1,0:T(8,128)(2,1)S(1)}, bf16[2048,128]{1,0:T(8,128)(2,1)S(1)}, u32[]{:S(2)}, u32[]{:S(2)}) collective-permute-start(bf16[2048,128]{1,0:T(8,128)(2,1)S(1)} %collective-permute-done.1.refs_6_), channel_id=1, source_target_pairs={{0,2},{1,5},{2,0},{3,7},{4,6},{5,1},{6,4},{7,3},{8,10},{9,13},{10,... | collective-permute-start | bytes 1572872 | tf_op jit(solution)/shard_map/ppermute | solution.py:337
  44.5 7.5 %pool.7 = (f32[9992,128]{1,0:T(8,128)S(1)}, f32[9992,128]{1,0:T(8,128)S(1)}, f32[9992,128]{1,0:T(8,128)S(1)}, f32[9992,128]{1,0:T(8,128)S(1)}, s32[8,128]{1,0:T(8,128)S(1)}) custom-call(s32[30720]{0:T(1024)S(1)} %reshape.1480.slot_ref, s32[30720]{0:T(1024)S(1)} %reshape.1481.bag_ref, ...), custom_call_target="tpu_custom_call", output_to_operand_aliasing={{0}: (10, {}), {1}: (11, {}), {2}: (12, {}), {3}: (13, {})} | custom-call | bytes 24000000 | tf_op jit(solution)/shard_map/pool/pallas_call | solution.py:254
  52.0 3.8 %collective-permute-done.4.refs_0_ = bf16[2048,128]{1,0:T(8,128)(2,1)S(1)} collective-permute-done((bf16[2048,128]{1,0:T(8,128)(2,1)S(1)}, bf16[2048,128]{1,0:T(8,128)(2,1)S(1)}, u32[]{:S(2)}, u32[]{:S(2)}) %collective-permute-start.4) | collective-permute-done | bytes 524320 | tf_op jit(solution)/shard_map/ppermute | solution.py:337
  56.3 2.2 %collective-permute-done.2.refs_6_ = bf16[2048,128]{1,0:T(8,128)(2,1)S(1)} collective-permute-done((bf16[2048,128]{1,0:T(8,128)(2,1)S(1)}, bf16[2048,128]{1,0:T(8,128)(2,1)S(1)}, u32[]{:S(2)}, u32[]{:S(2)}) %collective-permute-start.2) | collective-permute-done | bytes 524320 | tf_op jit(solution)/shard_map/ppermute | solution.py:337
  58.5 2.4 %collective-permute-done.19.refs_2_ = bf16[2048,128]{1,0:T(8,128)(2,1)S(1)} collective-permute-done((bf16[2048,128]{1,0:T(8,128)(2,1)S(1)}, bf16[2048,128]{1,0:T(8,128)(2,1)S(1)}, u32[]{:S(2)}, u32[]{:S(2)}) %collective-permute-start.19) | collective-permute-done | bytes 524320 | tf_op jit(solution)/shard_map/ppermute | solution.py:337
  61.2 1.2 %collective-permute-start.3 = (bf16[2048,128]{1,0:T(8,128)(2,1)S(1)}, bf16[2048,128]{1,0:T(8,128)(2,1)S(1)}, u32[]{:S(2)}, u32[]{:S(2)}) collective-permute-start(bf16[2048,128]{1,0:T(8,128)(2,1)S(1)} %collective-permute-done.2.refs_6_), channel_id=1, source_target_pairs={{0,2},{1,5},{2,0},{3,7},{4,6},{5,1},{6,4},{7,3},{8,10},{9,13},{10,... | collective-permute-start | bytes 1572872 | tf_op jit(solution)/shard_map/ppermute | solution.py:337
  63.5 7.8 %pool.8 = (f32[9992,128]{1,0:T(8,128)S(1)}, f32[9992,128]{1,0:T(8,128)S(1)}, f32[9992,128]{1,0:T(8,128)S(1)}, f32[9992,128]{1,0:T(8,128)S(1)}, s32[8,128]{1,0:T(8,128)S(1)}) custom-call(s32[30720]{0:T(1024)S(1)} %reshape.1480.slot_ref, s32[30720]{0:T(1024)S(1)} %reshape.1481.bag_ref, ...), custom_call_target="tpu_custom_call", output_to_operand_aliasing={{0}: (10, {}), {1}: (11, {}), {2}: (12, {}), {3}: (13, {})} | custom-call | bytes 24000000 | tf_op jit(solution)/shard_map/pool/pallas_call | solution.py:254
  71.2 4.7 %collective-permute-done.3.refs_0_ = bf16[2048,128]{1,0:T(8,128)(2,1)S(1)} collective-permute-done((bf16[2048,128]{1,0:T(8,128)(2,1)S(1)}, bf16[2048,128]{1,0:T(8,128)(2,1)S(1)}, u32[]{:S(2)}, u32[]{:S(2)}) %collective-permute-start.3) | collective-permute-done | bytes 524320 | tf_op jit(solution)/shard_map/ppermute | solution.py:337
  75.9 1.9 %collective-permute-done.28.refs_4_ = bf16[2048,128]{1,0:T(8,128)(2,1)S(1)} collective-permute-done((bf16[2048,128]{1,0:T(8,128)(2,1)S(1)}, bf16[2048,128]{1,0:T(8,128)(2,1)S(1)}, u32[]{:S(2)}, u32[]{:S(2)}) %collective-permute-start.28) | collective-permute-done | bytes 524320 | tf_op jit(solution)/shard_map/ppermute | solution.py:337
  80.5 6.4 %pool.9 = (f32[9992,128]{1,0:T(8,128)S(1)}, f32[9992,128]{1,0:T(8,128)S(1)}, f32[9992,128]{1,0:T(8,128)S(1)}, f32[9992,128]{1,0:T(8,128)S(1)}, s32[8,128]{1,0:T(8,128)S(1)}) custom-call(s32[30720]{0:T(1024)S(1)} %reshape.1480.slot_ref, s32[30720]{0:T(1024)S(1)} %reshape.1481.bag_ref, ...), custom_call_target="tpu_custom_call", output_to_operand_aliasing={{0}: (8, {}), {1}: (9, {}), {2}: (10, {}), {3}: (11, {})} | custom-call | bytes 18000000 | tf_op jit(solution)/shard_map/pool/pallas_call | solution.py:254
  87.5 1.9 %collective-permute-done.30.refs_1_ = bf16[2048,128]{1,0:T(8,128)(2,1)S(1)} collective-permute-done((bf16[2048,128]{1,0:T(8,128)(2,1)S(1)}, bf16[2048,128]{1,0:T(8,128)(2,1)S(1)}, u32[]{:S(2)}, u32[]{:S(2)}) %collective-permute-start.30) | collective-permute-done | bytes 524320 | tf_op jit(solution)/shard_map/ppermute | solution.py:337
  89.4 10.5 %finish.1 = (f32[384]{0:T(512)}, f32[9992,128]{1,0:T(8,128)S(1)}, f32[9992,128]{1,0:T(8,128)S(1)}, f32[9992,128]{1,0:T(8,128)S(1)}, f32[9992,128]{1,0:T(8,128)S(1)}) custom-call(s32[30720]{0:T(1024)S(1)} %reshape.1480.slot_ref, s32[30720]{0:T(1024)S(1)} %reshape.1481.bag_ref, ...), custom_call_target="tpu_custom_call", output_to_operand_aliasing={{1}: (4, {}), {2}: (5, {}), {3}: (6, {}), {4}: (7, {})} | custom-call | tf_op jit(solution)/shard_map/finish/pallas_call | solution.py:288
  (73 shorter events, 12.9 us)
Async XLA Ops:
  2.0 9.0 %collective-permute-start.7 = (bf16[2048,128]{1,0:T(8,128)(2,1)S(1)}, bf16[2048,128]{1,0:T(8,128)(2,1)S(1)}, u32[]{:S(2)}, u32[]{:S(2)}) collective-permute-start(bf16[2048,128]{1,0:T(8,128)(2,1)S(1)} %fill.1.refs_0_), channel_id=1, source_target_pairs={{0,1},{1,0},{2,3},{3,2},{4,5},{5,4},{6,7},{7,6},{8,9},{9,8},{10,11... | collective-permute-start | bytes 1572872 | tf_op jit(solution)/shard_map/ppermute | solution.py:337
  2.5 12.8 %collective-permute-start.6 = (bf16[2048,128]{1,0:T(8,128)(2,1)S(1)}, bf16[2048,128]{1,0:T(8,128)(2,1)S(1)}, u32[]{:S(2)}, u32[]{:S(2)}) collective-permute-start(bf16[2048,128]{1,0:T(8,128)(2,1)S(1)} %fill.1.refs_0_), channel_id=1, source_target_pairs={{0,2},{1,5},{2,0},{3,7},{4,6},{5,1},{6,4},{7,3},{8,10},{9,13},{10,... | collective-permute-start | bytes 1572872 | tf_op jit(solution)/shard_map/ppermute | solution.py:337
  5.1 15.9 %collective-permute-start = (bf16[2048,128]{1,0:T(8,128)(2,1)S(1)}, bf16[2048,128]{1,0:T(8,128)(2,1)S(1)}, u32[]{:S(2)}, u32[]{:S(2)}) collective-permute-start(bf16[2048,128]{1,0:T(8,128)(2,1)S(1)} %fill.1.refs_0_), channel_id=1, source_target_pairs={{0,8},{1,9},{2,10},{3,11},{4,12},{5,13},{6,14},{7,15},{8,16},{9,17... | collective-permute-start | bytes 1572872 | tf_op jit(solution)/shard_map/ppermute | solution.py:337
  6.6 14.3 %collective-permute-start.9 = (bf16[2048,128]{1,0:T(8,128)(2,1)S(1)}, bf16[2048,128]{1,0:T(8,128)(2,1)S(1)}, u32[]{:S(2)}, u32[]{:S(2)}) collective-permute-start(bf16[2048,128]{1,0:T(8,128)(2,1)S(1)} %fill.1.refs_0_), channel_id=1, source_target_pairs={{0,4},{1,3},{2,6},{3,1},{4,0},{5,7},{6,2},{7,5},{8,12},{9,11},{10,... | collective-permute-start | bytes 1572872 | tf_op jit(solution)/shard_map/ppermute | solution.py:337
  15.3 8.1 %collective-permute-start.8 = (bf16[2048,128]{1,0:T(8,128)(2,1)S(1)}, bf16[2048,128]{1,0:T(8,128)(2,1)S(1)}, u32[]{:S(2)}, u32[]{:S(2)}) collective-permute-start(bf16[2048,128]{1,0:T(8,128)(2,1)S(1)} %gate.5.refs_0_), channel_id=1, source_target_pairs={{0,1},{1,0},{2,3},{3,2},{4,5},{5,4},{6,7},{7,6},{8,9},{9,8},{10,11... | collective-permute-start | bytes 1572872 | tf_op jit(solution)/shard_map/ppermute | solution.py:337
  21.4 14.8 %collective-permute-start.5 = (bf16[2048,128]{1,0:T(8,128)(2,1)S(1)}, bf16[2048,128]{1,0:T(8,128)(2,1)S(1)}, u32[]{:S(2)}, u32[]{:S(2)}) collective-permute-start(bf16[2048,128]{1,0:T(8,128)(2,1)S(1)} %collective-permute-done.refs_4_), channel_id=1, source_target_pairs={{0,2},{1,5},{2,0},{3,7},{4,6},{5,1},{6,4},{7,3},{8,10},{9,13},{10,... | collective-permute-start | bytes 1572872 | tf_op jit(solution)/shard_map/ppermute | solution.py:337
  22.1 14.1 %collective-permute-start.15 = (bf16[2048,128]{1,0:T(8,128)(2,1)S(1)}, bf16[2048,128]{1,0:T(8,128)(2,1)S(1)}, u32[]{:S(2)}, u32[]{:S(2)}) collective-permute-start(bf16[2048,128]{1,0:T(8,128)(2,1)S(1)} %gate.5.refs_0_), channel_id=1, source_target_pairs={{0,4},{1,3},{2,6},{3,1},{4,0},{5,7},{6,2},{7,5},{8,12},{9,11},{10,... | collective-permute-start | bytes 1572872 | tf_op jit(solution)/shard_map/ppermute | solution.py:337
  23.5 15.1 %collective-permute-start.1 = (bf16[2048,128]{1,0:T(8,128)(2,1)S(1)}, bf16[2048,128]{1,0:T(8,128)(2,1)S(1)}, u32[]{:S(2)}, u32[]{:S(2)}) collective-permute-start(bf16[2048,128]{1,0:T(8,128)(2,1)S(1)} %collective-permute-done.refs_4_), channel_id=1, source_target_pairs={{0,8},{1,9},{2,10},{3,11},{4,12},{5,13},{6,14},{7,15},{8,16},{9,17... | collective-permute-start | bytes 1572872 | tf_op jit(solution)/shard_map/ppermute | solution.py:337
  23.5 17.4 %collective-permute-start.13 = (bf16[2048,128]{1,0:T(8,128)(2,1)S(1)}, bf16[2048,128]{1,0:T(8,128)(2,1)S(1)}, u32[]{:S(2)}, u32[]{:S(2)}) collective-permute-start(bf16[2048,128]{1,0:T(8,128)(2,1)S(1)} %collective-permute-done.refs_4_), channel_id=1, source_target_pairs={{0,4},{1,3},{2,6},{3,1},{4,0},{5,7},{6,2},{7,5},{8,12},{9,11},{10,... | collective-permute-start | bytes 1572872 | tf_op jit(solution)/shard_map/ppermute | solution.py:337
  36.2 6.2 %collective-permute-start.12 = (bf16[2048,128]{1,0:T(8,128)(2,1)S(1)}, bf16[2048,128]{1,0:T(8,128)(2,1)S(1)}, u32[]{:S(2)}, u32[]{:S(2)}) collective-permute-start(bf16[2048,128]{1,0:T(8,128)(2,1)S(1)} %gate.6.refs_0_), channel_id=1, source_target_pairs={{0,1},{1,0},{2,3},{3,2},{4,5},{5,4},{6,7},{7,6},{8,9},{9,8},{10,11... | collective-permute-start | bytes 1572872 | tf_op jit(solution)/shard_map/ppermute | solution.py:337
  36.2 7.1 %collective-permute-start.16 = (bf16[2048,128]{1,0:T(8,128)(2,1)S(1)}, bf16[2048,128]{1,0:T(8,128)(2,1)S(1)}, u32[]{:S(2)}, u32[]{:S(2)}) collective-permute-start(bf16[2048,128]{1,0:T(8,128)(2,1)S(1)} %collective-permute-done.15.refs_4_), channel_id=1, source_target_pairs={{0,1},{1,0},{2,3},{3,2},{4,5},{5,4},{6,7},{7,6},{8,9},{9,8},{10,11... | collective-permute-start | bytes 1572872 | tf_op jit(solution)/shard_map/ppermute | solution.py:337
  38.5 4.9 %collective-permute-start.17 = (bf16[2048,128]{1,0:T(8,128)(2,1)S(1)}, bf16[2048,128]{1,0:T(8,128)(2,1)S(1)}, u32[]{:S(2)}, u32[]{:S(2)}) collective-permute-start(bf16[2048,128]{1,0:T(8,128)(2,1)S(1)} %collective-permute-done.1.refs_6_), channel_id=1, source_target_pairs={{0,1},{1,0},{2,3},{3,2},{4,5},{5,4},{6,7},{7,6},{8,9},{9,8},{10,11... | collective-permute-start | bytes 1572872 | tf_op jit(solution)/shard_map/ppermute | solution.py:337
  40.9 3.6 %collective-permute-start.14 = (bf16[2048,128]{1,0:T(8,128)(2,1)S(1)}, bf16[2048,128]{1,0:T(8,128)(2,1)S(1)}, u32[]{:S(2)}, u32[]{:S(2)}) collective-permute-start(bf16[2048,128]{1,0:T(8,128)(2,1)S(1)} %collective-permute-done.13.refs_2_), channel_id=1, source_target_pairs={{0,1},{1,0},{2,3},{3,2},{4,5},{5,4},{6,7},{7,6},{8,9},{9,8},{10,11... | collective-permute-start | bytes 1572872 | tf_op jit(solution)/shard_map/ppermute | solution.py:337
  41.0 14.8 %collective-permute-start.4 = (bf16[2048,128]{1,0:T(8,128)(2,1)S(1)}, bf16[2048,128]{1,0:T(8,128)(2,1)S(1)}, u32[]{:S(2)}, u32[]{:S(2)}) collective-permute-start(bf16[2048,128]{1,0:T(8,128)(2,1)S(1)} %collective-permute-done.1.refs_6_), channel_id=1, source_target_pairs={{0,2},{1,5},{2,0},{3,7},{4,6},{5,1},{6,4},{7,3},{8,10},{9,13},{10,... | collective-permute-start | bytes 1572872 | tf_op jit(solution)/shard_map/ppermute | solution.py:337
  42.4 13.4 %collective-permute-start.21 = (bf16[2048,128]{1,0:T(8,128)(2,1)S(1)}, bf16[2048,128]{1,0:T(8,128)(2,1)S(1)}, u32[]{:S(2)}, u32[]{:S(2)}) collective-permute-start(bf16[2048,128]{1,0:T(8,128)(2,1)S(1)} %gate.6.refs_0_), channel_id=1, source_target_pairs={{0,4},{1,3},{2,6},{3,1},{4,0},{5,7},{6,2},{7,5},{8,12},{9,11},{10,... | collective-permute-start | bytes 1572872 | tf_op jit(solution)/shard_map/ppermute | solution.py:337
  43.3 15.1 %collective-permute-start.2 = (bf16[2048,128]{1,0:T(8,128)(2,1)S(1)}, bf16[2048,128]{1,0:T(8,128)(2,1)S(1)}, u32[]{:S(2)}, u32[]{:S(2)}) collective-permute-start(bf16[2048,128]{1,0:T(8,128)(2,1)S(1)} %collective-permute-done.1.refs_6_), channel_id=1, source_target_pairs={{0,8},{1,9},{2,10},{3,11},{4,12},{5,13},{6,14},{7,15},{8,16},{9,17... | collective-permute-start | bytes 1572872 | tf_op jit(solution)/shard_map/ppermute | solution.py:337
  43.4 17.4 %collective-permute-start.19 = (bf16[2048,128]{1,0:T(8,128)(2,1)S(1)}, bf16[2048,128]{1,0:T(8,128)(2,1)S(1)}, u32[]{:S(2)}, u32[]{:S(2)}) collective-permute-start(bf16[2048,128]{1,0:T(8,128)(2,1)S(1)} %collective-permute-done.1.refs_6_), channel_id=1, source_target_pairs={{0,4},{1,3},{2,6},{3,1},{4,0},{5,7},{6,2},{7,5},{8,12},{9,11},{10,... | collective-permute-start | bytes 1572872 | tf_op jit(solution)/shard_map/ppermute | solution.py:337
  55.8 6.6 %collective-permute-start.18 = (bf16[2048,128]{1,0:T(8,128)(2,1)S(1)}, bf16[2048,128]{1,0:T(8,128)(2,1)S(1)}, u32[]{:S(2)}, u32[]{:S(2)}) collective-permute-start(bf16[2048,128]{1,0:T(8,128)(2,1)S(1)} %gate.7.refs_0_), channel_id=1, source_target_pairs={{0,1},{1,0},{2,3},{3,2},{4,5},{5,4},{6,7},{7,6},{8,9},{9,8},{10,11... | collective-permute-start | bytes 1572872 | tf_op jit(solution)/shard_map/ppermute | solution.py:337
  55.8 6.6 %collective-permute-start.22 = (bf16[2048,128]{1,0:T(8,128)(2,1)S(1)}, bf16[2048,128]{1,0:T(8,128)(2,1)S(1)}, u32[]{:S(2)}, u32[]{:S(2)}) collective-permute-start(bf16[2048,128]{1,0:T(8,128)(2,1)S(1)} %collective-permute-done.21.refs_4_), channel_id=1, source_target_pairs={{0,1},{1,0},{2,3},{3,2},{4,5},{5,4},{6,7},{7,6},{8,9},{9,8},{10,11... | collective-permute-start | bytes 1572872 | tf_op jit(solution)/shard_map/ppermute | solution.py:337
  58.5 5.0 %collective-permute-start.23 = (bf16[2048,128]{1,0:T(8,128)(2,1)S(1)}, bf16[2048,128]{1,0:T(8,128)(2,1)S(1)}, u32[]{:S(2)}, u32[]{:S(2)}) collective-permute-start(bf16[2048,128]{1,0:T(8,128)(2,1)S(1)} %collective-permute-done.2.refs_6_), channel_id=1, source_target_pairs={{0,1},{1,0},{2,3},{3,2},{4,5},{5,4},{6,7},{7,6},{8,9},{9,8},{10,11... | collective-permute-start | bytes 1572872 | tf_op jit(solution)/shard_map/ppermute | solution.py:337
  61.2 14.7 %collective-permute-start.3 = (bf16[2048,128]{1,0:T(8,128)(2,1)S(1)}, bf16[2048,128]{1,0:T(8,128)(2,1)S(1)}, u32[]{:S(2)}, u32[]{:S(2)}) collective-permute-start(bf16[2048,128]{1,0:T(8,128)(2,1)S(1)} %collective-permute-done.2.refs_6_), channel_id=1, source_target_pairs={{0,2},{1,5},{2,0},{3,7},{4,6},{5,1},{6,4},{7,3},{8,10},{9,13},{10,... | collective-permute-start | bytes 1572872 | tf_op jit(solution)/shard_map/ppermute | solution.py:337
  62.4 15.4 %collective-permute-start.28 = (bf16[2048,128]{1,0:T(8,128)(2,1)S(1)}, bf16[2048,128]{1,0:T(8,128)(2,1)S(1)}, u32[]{:S(2)}, u32[]{:S(2)}) collective-permute-start(bf16[2048,128]{1,0:T(8,128)(2,1)S(1)} %collective-permute-done.21.refs_4_), channel_id=1, source_target_pairs={{0,8},{1,9},{2,10},{3,11},{4,12},{5,13},{6,14},{7,15},{8,16},{9,17... | collective-permute-start | bytes 1572872 | tf_op jit(solution)/shard_map/ppermute | solution.py:337
  62.4 15.4 %collective-permute-start.26 = (bf16[2048,128]{1,0:T(8,128)(2,1)S(1)}, bf16[2048,128]{1,0:T(8,128)(2,1)S(1)}, u32[]{:S(2)}, u32[]{:S(2)}) collective-permute-start(bf16[2048,128]{1,0:T(8,128)(2,1)S(1)} %collective-permute-done.2.refs_6_), channel_id=1, source_target_pairs={{0,4},{1,3},{2,6},{3,1},{4,0},{5,7},{6,2},{7,5},{8,12},{9,11},{10,... | collective-permute-start | bytes 1572872 | tf_op jit(solution)/shard_map/ppermute | solution.py:337
  78.3 9.2 %collective-permute-start.24 = (bf16[2048,128]{1,0:T(8,128)(2,1)S(1)}, bf16[2048,128]{1,0:T(8,128)(2,1)S(1)}, u32[]{:S(2)}, u32[]{:S(2)}) collective-permute-start(bf16[2048,128]{1,0:T(8,128)(2,1)S(1)} %gate.8.refs_0_), channel_id=1, source_target_pairs={{0,4},{1,3},{2,6},{3,1},{4,0},{5,7},{6,2},{7,5},{8,12},{9,11},{10,... | collective-permute-start | bytes 1572872 | tf_op jit(solution)/shard_map/ppermute | solution.py:337
  (12 other events, 62.5 us)

commit v6 on v5

--- a/solution.py
+++ b/solution.py
@@ -168,7 +168,7 @@
             ).astype(jnp.bfloat16)
         return 0
 
-    lax.fori_loop(0, queries // 16, sixteen_queries, 0, unroll=4)
+    lax.fori_loop(0, queries // 16, sixteen_queries, 0, unroll=8)
 
 
 def inter_columns(masked, dense_ref, inter, queries):
@@ -356,8 +356,10 @@
     order = both_cores(0, 0, 0) + unused
     for shift in range(n_planes):
         before, after = max(shift - 1, 0), min(shift + 1, n_planes - 1)
-        order += both_cores(shift, 1, 0) + both_cores(shift, 0, 1)
-        order += both_cores(before, 1, 1) + both_cores(after, 0, 0)
+        order += both_cores(shift, 1, 0)
+        order += [both_cores(shift, 0, 1)[0], both_cores(before, 0, min(shift, 1))[1]]
+        order += both_cores(before, 1, 1)
+        order += both_cores(after, 0, 0) if after > shift else [both_cores(shift, 0, 1)[1], 0]
     order += both_cores(n_planes - 1, 1, 1) + unused
     order = jnp.stack(order)
     cap = lookup_slot.shape[2]
@@ -376,12 +378,13 @@
         return [array, other_core(array)]
 
     crossed, turned, next_piece = first_hop(own), second_hop(own), next_plane(own)
-    sums, done = pool(0, entries, cap, of_chip(own), None, sum_rows)
+    sums, done = pool(0, entries, cap, [own], None, sum_rows, [0])
     (crossed,) = gate([crossed], done)
-    far = []
+    far, late = [], other_core(own)
     for shift in range(n_planes):
         last = shift == n_planes - 1
-        near = of_chip(crossed) + of_chip(turned)
+        near = of_chip(crossed) + [turned]
+        other_turned = other_core(turned)
         next_far = next_plane(far[0]) if shift == n_planes - 2 else second_hop(crossed)
         passed = [next_far]
         if not last:
@@ -390,17 +393,17 @@
             if shift < n_planes - 2:
                 passed.append(next_plane(next_piece))
         else:
-            piece = []
+            piece = [other_turned]
         if shift == 0:
-            shards, rows = near + piece, [0, 1, 2, 3, 6, 7]
+            shards, rows = near + [late] + piece, [0, 1, 2, 3, 6, 7]
         else:
-            shards, rows = near + far + piece, list(range(6 + len(piece)))
+            shards, rows = near + [late] + far + piece, list(range(6 + len(piece)))
         sums, done = pool(8 * shift + 8, entries, cap, shards, sums, sum_rows, rows)
-        chosen = [0] if last else [index for index in PICK if index < len(passed)]
+        chosen = [0] if last else [1, 0] if shift == n_planes - 2 else [index for index in PICK if index < len(passed)]
         for index, one in zip(chosen, gate([passed[index] for index in chosen], done)):
             passed[index] = one
         next_far, *passed = passed
-        far = of_chip(next_far)
+        far, late = of_chip(next_far), other_turned
         if not last:
             crossed, turned, *next_piece = passed
             next_piece = next_piece[0] if next_piece else None

time: 101 us -> 98.9 us (0.979)
  waiting for transfers between devices: 35.3 us -> 32.6 us
  starting transfers between devices: 18.2 us -> 19.8 us
    ppermute x31, waiting for transfers between devices: 35.3 us -> 32.6 us  [hop(): return lambda array: lax.ppermute(array, 'cache', pairs)]
    ppermute x31, starting transfers between devices: 18.2 us -> 19.8 us  [hop(): return lambda array: lax.ppermute(array, 'cache', pairs)]
  transfers between devices with their start and end apart: 31 -> 31, of which waited for: 14 -> 13; matrix products, arithmetic and copies ran while one was open for 3% -> 3% of each run, Pallas kernels for 31% -> 32%
where the time goes in v6:
time: 98.9 us; the launch traced here: 98.6 us
  Pallas kernels  43.2 us (44%)
  waiting for transfers between devices  32.6 us (33%)
  starting transfers between devices  19.8 us (20%)
  local copies, waits for them, and re-layouts  2.41 us (2%)
    ppermute x31, waiting for transfers between devices, hop(): return lambda array: lax.ppermute(array, 'cache', pairs)  32.6 us
    pallas_call x5, Pallas kernels, pool(): pl.pallas_call(functools.partial(pool_kernel, first, rows, is_first), out...  31.1 us
    ppermute x31, starting transfers between devices, hop(): return lambda array: lax.ppermute(array, 'cache', pairs)  19.8 us
    pallas_call x1, Pallas kernels, finish(): pl.pallas_call(functools.partial(final_kernel, first, n_shards, head is n...  10.1 us
  transfers between devices with their start and end apart: 31, of which 13 were waited for; matrix products, arithmetic and copies ran while one was open for 3% of the time, Pallas kernels for 32%

profile of v6, /device:TPU:0, one launch (start us, length us, event | category | flops | bytes accessed | tf_op | source)
XLA Modules:
  0.0 98.6 jit_solution(2017339133239477399)
XLA Ops:
  0.0 2.0 %fill.1.refs_0_ = bf16[2048,128]{1,0:T(8,128)(2,1)S(1)} custom-call(s32[2]{0:T(128)} %bitcast.42, s32[2]{0:T(128)} %bitcast.43, bf16[2048,128]{1,0:T(8,128)(2,1)} %cache_ref.1, bf16[1024,128]{1,0:T(8,128)(2,1)} %fills_ref.1), custom_call_target="tpu_custom_call" | custom-call | tf_op jit(solution)/shard_map/fill/pallas_call | solution.py:57
  2.0 3.0 %collective-permute-start.5 = (bf16[2048,128]{1,0:T(8,128)(2,1)S(1)}, bf16[2048,128]{1,0:T(8,128)(2,1)S(1)}, u32[]{:S(2)}, u32[]{:S(2)}) collective-permute-start(bf16[2048,128]{1,0:T(8,128)(2,1)S(1)} %fill.1.refs_0_), channel_id=1, source_target_pairs={{0,2},{1,5},{2,0},{3,7},{4,6},{5,1},{6,4},{7,3},{8,10},{9,13},{10,... | collective-permute-start | bytes 1572872 | tf_op jit(solution)/shard_map/ppermute | solution.py:337
  5.0 1.6 %collective-permute-start = (bf16[2048,128]{1,0:T(8,128)(2,1)S(1)}, bf16[2048,128]{1,0:T(8,128)(2,1)S(1)}, u32[]{:S(2)}, u32[]{:S(2)}) collective-permute-start(bf16[2048,128]{1,0:T(8,128)(2,1)S(1)} %fill.1.refs_0_), channel_id=1, source_target_pairs={{0,8},{1,9},{2,10},{3,11},{4,12},{5,13},{6,14},{7,15},{8,16},{9,17... | collective-permute-start | bytes 1572872 | tf_op jit(solution)/shard_map/ppermute | solution.py:337
  6.6 1.5 %collective-permute-start.7 = (bf16[2048,128]{1,0:T(8,128)(2,1)S(1)}, bf16[2048,128]{1,0:T(8,128)(2,1)S(1)}, u32[]{:S(2)}, u32[]{:S(2)}) collective-permute-start(bf16[2048,128]{1,0:T(8,128)(2,1)S(1)} %fill.1.refs_0_), channel_id=1, source_target_pairs={{0,4},{1,3},{2,6},{3,1},{4,0},{5,7},{6,2},{7,5},{8,12},{9,11},{10,... | collective-permute-start | bytes 1572872 | tf_op jit(solution)/shard_map/ppermute | solution.py:337
  9.2 1.6 %gather_fusion.1 = s32[48,624]{1,0:T(8,128)S(1)} fusion(s32[32,624]{1,0:T(8,128)} %bitcast.41, s32[1024]{0:T(1024)S(1)} %pad_clamp_fusion), kind=kCustom, calls=%fused_computation.1 | custom fusion | bytes 239808 | tf_op jit(solution)/shard_map/gather | solution.py:368
  10.9 2.4 %pool.5 = (f32[9992,128]{1,0:T(8,128)S(1)}, f32[9992,128]{1,0:T(8,128)S(1)}, f32[9992,128]{1,0:T(8,128)S(1)}, f32[9992,128]{1,0:T(8,128)S(1)}, s32[8,128]{1,0:T(8,128)S(1)}) custom-call(s32[30720]{0:T(1024)S(1)} %reshape.1470.slot_ref, s32[30720]{0:T(1024)S(1)} %reshape.1471.bag_ref, bf16[2048,128]{1,0:T(8,128)(2,1)S(1)} %fill.1.refs_0_), custom_call_target="tpu_custom_call" | custom-call | bytes 3000000 | tf_op jit(solution)/shard_map/pool/pallas_call | solution.py:254
  13.3 2.5 %collective-permute-done.5.refs_0_ = bf16[2048,128]{1,0:T(8,128)(2,1)S(1)} collective-permute-done((bf16[2048,128]{1,0:T(8,128)(2,1)S(1)}, bf16[2048,128]{1,0:T(8,128)(2,1)S(1)}, u32[]{:S(2)}, u32[]{:S(2)}) %collective-permute-start.5) | collective-permute-done | bytes 524320 | tf_op jit(solution)/shard_map/ppermute | solution.py:337
  15.9 4.4 %collective-permute-done.refs_4_ = bf16[2048,128]{1,0:T(8,128)(2,1)S(1)} collective-permute-done((bf16[2048,128]{1,0:T(8,128)(2,1)S(1)}, bf16[2048,128]{1,0:T(8,128)(2,1)S(1)}, u32[]{:S(2)}, u32[]{:S(2)}) %collective-permute-start) | collective-permute-done | bytes 524320 | tf_op jit(solution)/shard_map/ppermute | solution.py:337
  20.3 1.5 %collective-permute-start.4 = (bf16[2048,128]{1,0:T(8,128)(2,1)S(1)}, bf16[2048,128]{1,0:T(8,128)(2,1)S(1)}, u32[]{:S(2)}, u32[]{:S(2)}) collective-permute-start(bf16[2048,128]{1,0:T(8,128)(2,1)S(1)} %collective-permute-done.refs_4_), channel_id=1, source_target_pairs={{0,2},{1,5},{2,0},{3,7},{4,6},{5,1},{6,4},{7,3},{8,10},{9,13},{10,... | collective-permute-start | bytes 1572872 | tf_op jit(solution)/shard_map/ppermute | solution.py:337
  23.9 6.4 %pool.6 = (f32[9992,128]{1,0:T(8,128)S(1)}, f32[9992,128]{1,0:T(8,128)S(1)}, f32[9992,128]{1,0:T(8,128)S(1)}, f32[9992,128]{1,0:T(8,128)S(1)}, s32[8,128]{1,0:T(8,128)S(1)}) custom-call(s32[30720]{0:T(1024)S(1)} %reshape.1470.slot_ref, s32[30720]{0:T(1024)S(1)} %reshape.1471.bag_ref, ...), custom_call_target="tpu_custom_call", output_to_operand_aliasing={{0}: (8, {}), {1}: (9, {}), {2}: (10, {}), {3}: (11, {})} | custom-call | bytes 18000000 | tf_op jit(solution)/shard_map/pool/pallas_call | solution.py:254
  30.3 4.7 %collective-permute-done.4.refs_0_ = bf16[2048,128]{1,0:T(8,128)(2,1)S(1)} collective-permute-done((bf16[2048,128]{1,0:T(8,128)(2,1)S(1)}, bf16[2048,128]{1,0:T(8,128)(2,1)S(1)}, u32[]{:S(2)}, u32[]{:S(2)}) %collective-permute-start.4) | collective-permute-done | bytes 524320 | tf_op jit(solution)/shard_map/ppermute | solution.py:337
  35.6 2.3 %collective-permute-done.1.refs_6_ = bf16[2048,128]{1,0:T(8,128)(2,1)S(1)} collective-permute-done((bf16[2048,128]{1,0:T(8,128)(2,1)S(1)}, bf16[2048,128]{1,0:T(8,128)(2,1)S(1)}, u32[]{:S(2)}, u32[]{:S(2)}) %collective-permute-start.1) | collective-permute-done | bytes 524320 | tf_op jit(solution)/shard_map/ppermute | solution.py:337
  37.8 2.4 %collective-permute-done.14.refs_2_ = bf16[2048,128]{1,0:T(8,128)(2,1)S(1)} collective-permute-done((bf16[2048,128]{1,0:T(8,128)(2,1)S(1)}, bf16[2048,128]{1,0:T(8,128)(2,1)S(1)}, u32[]{:S(2)}, u32[]{:S(2)}) %collective-permute-start.14) | collective-permute-done | bytes 524320 | tf_op jit(solution)/shard_map/ppermute | solution.py:337
  40.2 1.5 %collective-permute-start.12 = (bf16[2048,128]{1,0:T(8,128)(2,1)S(1)}, bf16[2048,128]{1,0:T(8,128)(2,1)S(1)}, u32[]{:S(2)}, u32[]{:S(2)}) collective-permute-start(bf16[2048,128]{1,0:T(8,128)(2,1)S(1)} %collective-permute-done.1.refs_6_), channel_id=1, source_target_pairs={{0,2},{1,5},{2,0},{3,7},{4,6},{5,1},{6,4},{7,3},{8,10},{9,13},{10,... | collective-permute-start | bytes 1572872 | tf_op jit(solution)/shard_map/ppermute | solution.py:337
  43.8 7.6 %pool.7 = (f32[9992,128]{1,0:T(8,128)S(1)}, f32[9992,128]{1,0:T(8,128)S(1)}, f32[9992,128]{1,0:T(8,128)S(1)}, f32[9992,128]{1,0:T(8,128)S(1)}, s32[8,128]{1,0:T(8,128)S(1)}) custom-call(s32[30720]{0:T(1024)S(1)} %reshape.1470.slot_ref, s32[30720]{0:T(1024)S(1)} %reshape.1471.bag_ref, ...), custom_call_target="tpu_custom_call", output_to_operand_aliasing={{0}: (10, {}), {1}: (11, {}), {2}: (12, {}), {3}: (13, {})} | custom-call | bytes 24000000 | tf_op jit(solution)/shard_map/pool/pallas_call | solution.py:254
  51.4 3.5 %collective-permute-done.12.refs_0_ = bf16[2048,128]{1,0:T(8,128)(2,1)S(1)} collective-permute-done((bf16[2048,128]{1,0:T(8,128)(2,1)S(1)}, bf16[2048,128]{1,0:T(8,128)(2,1)S(1)}, u32[]{:S(2)}, u32[]{:S(2)}) %collective-permute-start.12) | collective-permute-done | bytes 524320 | tf_op jit(solution)/shard_map/ppermute | solution.py:337
  55.5 2.1 %collective-permute-done.2.refs_6_ = bf16[2048,128]{1,0:T(8,128)(2,1)S(1)} collective-permute-done((bf16[2048,128]{1,0:T(8,128)(2,1)S(1)}, bf16[2048,128]{1,0:T(8,128)(2,1)S(1)}, u32[]{:S(2)}, u32[]{:S(2)}) %collective-permute-start.2) | collective-permute-done | bytes 524320 | tf_op jit(solution)/shard_map/ppermute | solution.py:337
  57.6 2.2 %collective-permute-done.20.refs_2_ = bf16[2048,128]{1,0:T(8,128)(2,1)S(1)} collective-permute-done((bf16[2048,128]{1,0:T(8,128)(2,1)S(1)}, bf16[2048,128]{1,0:T(8,128)(2,1)S(1)}, u32[]{:S(2)}, u32[]{:S(2)}) %collective-permute-start.20) | collective-permute-done | bytes 524320 | tf_op jit(solution)/shard_map/ppermute | solution.py:337
  59.8 1.5 %collective-permute-start.3 = (bf16[2048,128]{1,0:T(8,128)(2,1)S(1)}, bf16[2048,128]{1,0:T(8,128)(2,1)S(1)}, u32[]{:S(2)}, u32[]{:S(2)}) collective-permute-start(bf16[2048,128]{1,0:T(8,128)(2,1)S(1)} %collective-permute-done.2.refs_6_), channel_id=1, source_target_pairs={{0,2},{1,5},{2,0},{3,7},{4,6},{5,1},{6,4},{7,3},{8,10},{9,13},{10,... | collective-permute-start | bytes 1572872 | tf_op jit(solution)/shard_map/ppermute | solution.py:337
  62.5 8.1 %pool.8 = (f32[9992,128]{1,0:T(8,128)S(1)}, f32[9992,128]{1,0:T(8,128)S(1)}, f32[9992,128]{1,0:T(8,128)S(1)}, f32[9992,128]{1,0:T(8,128)S(1)}, s32[8,128]{1,0:T(8,128)S(1)}) custom-call(s32[30720]{0:T(1024)S(1)} %reshape.1470.slot_ref, s32[30720]{0:T(1024)S(1)} %reshape.1471.bag_ref, ...), custom_call_target="tpu_custom_call", output_to_operand_aliasing={{0}: (10, {}), {1}: (11, {}), {2}: (12, {}), {3}: (13, {})} | custom-call | bytes 24000000 | tf_op jit(solution)/shard_map/pool/pallas_call | solution.py:254
  70.6 5.0 %collective-permute-done.11.refs_1_ = bf16[2048,128]{1,0:T(8,128)(2,1)S(1)} collective-permute-done((bf16[2048,128]{1,0:T(8,128)(2,1)S(1)}, bf16[2048,128]{1,0:T(8,128)(2,1)S(1)}, u32[]{:S(2)}, u32[]{:S(2)}) %collective-permute-start.11) | collective-permute-done | bytes 524320 | tf_op jit(solution)/shard_map/ppermute | solution.py:337
  79.0 6.5 %pool.9 = (f32[9992,128]{1,0:T(8,128)S(1)}, f32[9992,128]{1,0:T(8,128)S(1)}, f32[9992,128]{1,0:T(8,128)S(1)}, f32[9992,128]{1,0:T(8,128)S(1)}, s32[8,128]{1,0:T(8,128)S(1)}) custom-call(s32[30720]{0:T(1024)S(1)} %reshape.1470.slot_ref, s32[30720]{0:T(1024)S(1)} %reshape.1471.bag_ref, ...), custom_call_target="tpu_custom_call", output_to_operand_aliasing={{0}: (9, {}), {1}: (10, {}), {2}: (11, {}), {3}: (12, {})} | custom-call | bytes 21000000 | tf_op jit(solution)/shard_map/pool/pallas_call | solution.py:254
  86.8 1.5 %collective-permute-done.30.refs_1_ = bf16[2048,128]{1,0:T(8,128)(2,1)S(1)} collective-permute-done((bf16[2048,128]{1,0:T(8,128)(2,1)S(1)}, bf16[2048,128]{1,0:T(8,128)(2,1)S(1)}, u32[]{:S(2)}, u32[]{:S(2)}) %collective-permute-start.30) | collective-permute-done | bytes 524320 | tf_op jit(solution)/shard_map/ppermute | solution.py:337
  88.4 10.1 %finish.1 = (f32[384]{0:T(512)}, f32[9992,128]{1,0:T(8,128)S(1)}, f32[9992,128]{1,0:T(8,128)S(1)}, f32[9992,128]{1,0:T(8,128)S(1)}, f32[9992,128]{1,0:T(8,128)S(1)}) custom-call(s32[30720]{0:T(1024)S(1)} %reshape.1470.slot_ref, s32[30720]{0:T(1024)S(1)} %reshape.1471.bag_ref, ...), custom_call_target="tpu_custom_call", output_to_operand_aliasing={{1}: (4, {}), {2}: (5, {}), {3}: (6, {}), {4}: (7, {})} | custom-call | tf_op jit(solution)/shard_map/finish/pallas_call | solution.py:288
  (73 shorter events, 12.3 us)
Async XLA Ops:
  2.0 13.9 %collective-permute-start.5 = (bf16[2048,128]{1,0:T(8,128)(2,1)S(1)}, bf16[2048,128]{1,0:T(8,128)(2,1)S(1)}, u32[]{:S(2)}, u32[]{:S(2)}) collective-permute-start(bf16[2048,128]{1,0:T(8,128)(2,1)S(1)} %fill.1.refs_0_), channel_id=1, source_target_pairs={{0,2},{1,5},{2,0},{3,7},{4,6},{5,1},{6,4},{7,3},{8,10},{9,13},{10,... | collective-permute-start | bytes 1572872 | tf_op jit(solution)/shard_map/ppermute | solution.py:337
  5.0 15.3 %collective-permute-start = (bf16[2048,128]{1,0:T(8,128)(2,1)S(1)}, bf16[2048,128]{1,0:T(8,128)(2,1)S(1)}, u32[]{:S(2)}, u32[]{:S(2)}) collective-permute-start(bf16[2048,128]{1,0:T(8,128)(2,1)S(1)} %fill.1.refs_0_), channel_id=1, source_target_pairs={{0,8},{1,9},{2,10},{3,11},{4,12},{5,13},{6,14},{7,15},{8,16},{9,17... | collective-permute-start | bytes 1572872 | tf_op jit(solution)/shard_map/ppermute | solution.py:337
  6.6 15.2 %collective-permute-start.7 = (bf16[2048,128]{1,0:T(8,128)(2,1)S(1)}, bf16[2048,128]{1,0:T(8,128)(2,1)S(1)}, u32[]{:S(2)}, u32[]{:S(2)}) collective-permute-start(bf16[2048,128]{1,0:T(8,128)(2,1)S(1)} %fill.1.refs_0_), channel_id=1, source_target_pairs={{0,4},{1,3},{2,6},{3,1},{4,0},{5,7},{6,2},{7,5},{8,12},{9,11},{10,... | collective-permute-start | bytes 1572872 | tf_op jit(solution)/shard_map/ppermute | solution.py:337
  8.1 14.2 %collective-permute-start.8 = (bf16[2048,128]{1,0:T(8,128)(2,1)S(1)}, bf16[2048,128]{1,0:T(8,128)(2,1)S(1)}, u32[]{:S(2)}, u32[]{:S(2)}) collective-permute-start(bf16[2048,128]{1,0:T(8,128)(2,1)S(1)} %fill.1.refs_0_), channel_id=1, source_target_pairs={{0,1},{1,0},{2,3},{3,2},{4,5},{5,4},{6,7},{7,6},{8,9},{9,8},{10,11... | collective-permute-start | bytes 1572872 | tf_op jit(solution)/shard_map/ppermute | solution.py:337
  15.8 7.3 %collective-permute-start.6 = (bf16[2048,128]{1,0:T(8,128)(2,1)S(1)}, bf16[2048,128]{1,0:T(8,128)(2,1)S(1)}, u32[]{:S(2)}, u32[]{:S(2)}) collective-permute-start(bf16[2048,128]{1,0:T(8,128)(2,1)S(1)} %gate.5.refs_0_), channel_id=1, source_target_pairs={{0,1},{1,0},{2,3},{3,2},{4,5},{5,4},{6,7},{7,6},{8,9},{9,8},{10,11... | collective-permute-start | bytes 1572872 | tf_op jit(solution)/shard_map/ppermute | solution.py:337
  20.3 14.8 %collective-permute-start.4 = (bf16[2048,128]{1,0:T(8,128)(2,1)S(1)}, bf16[2048,128]{1,0:T(8,128)(2,1)S(1)}, u32[]{:S(2)}, u32[]{:S(2)}) collective-permute-start(bf16[2048,128]{1,0:T(8,128)(2,1)S(1)} %collective-permute-done.refs_4_), channel_id=1, source_target_pairs={{0,2},{1,5},{2,0},{3,7},{4,6},{5,1},{6,4},{7,3},{8,10},{9,13},{10,... | collective-permute-start | bytes 1572872 | tf_op jit(solution)/shard_map/ppermute | solution.py:337
  21.8 13.3 %collective-permute-start.16 = (bf16[2048,128]{1,0:T(8,128)(2,1)S(1)}, bf16[2048,128]{1,0:T(8,128)(2,1)S(1)}, u32[]{:S(2)}, u32[]{:S(2)}) collective-permute-start(bf16[2048,128]{1,0:T(8,128)(2,1)S(1)} %gate.5.refs_0_), channel_id=1, source_target_pairs={{0,4},{1,3},{2,6},{3,1},{4,0},{5,7},{6,2},{7,5},{8,12},{9,11},{10,... | collective-permute-start | bytes 1572872 | tf_op jit(solution)/shard_map/ppermute | solution.py:337
  22.3 15.6 %collective-permute-start.1 = (bf16[2048,128]{1,0:T(8,128)(2,1)S(1)}, bf16[2048,128]{1,0:T(8,128)(2,1)S(1)}, u32[]{:S(2)}, u32[]{:S(2)}) collective-permute-start(bf16[2048,128]{1,0:T(8,128)(2,1)S(1)} %collective-permute-done.refs_4_), channel_id=1, source_target_pairs={{0,8},{1,9},{2,10},{3,11},{4,12},{5,13},{6,14},{7,15},{8,16},{9,17... | collective-permute-start | bytes 1572872 | tf_op jit(solution)/shard_map/ppermute | solution.py:337
  23.1 17.1 %collective-permute-start.14 = (bf16[2048,128]{1,0:T(8,128)(2,1)S(1)}, bf16[2048,128]{1,0:T(8,128)(2,1)S(1)}, u32[]{:S(2)}, u32[]{:S(2)}) collective-permute-start(bf16[2048,128]{1,0:T(8,128)(2,1)S(1)} %collective-permute-done.refs_4_), channel_id=1, source_target_pairs={{0,4},{1,3},{2,6},{3,1},{4,0},{5,7},{6,2},{7,5},{8,12},{9,11},{10,... | collective-permute-start | bytes 1572872 | tf_op jit(solution)/shard_map/ppermute | solution.py:337
  23.9 17.8 %collective-permute-start.15 = (bf16[2048,128]{1,0:T(8,128)(2,1)S(1)}, bf16[2048,128]{1,0:T(8,128)(2,1)S(1)}, u32[]{:S(2)}, u32[]{:S(2)}) collective-permute-start(bf16[2048,128]{1,0:T(8,128)(2,1)S(1)} %collective-permute-done.7.refs_2_), channel_id=1, source_target_pairs={{0,1},{1,0},{2,3},{3,2},{4,5},{5,4},{6,7},{7,6},{8,9},{9,8},{10,11... | collective-permute-start | bytes 1572872 | tf_op jit(solution)/shard_map/ppermute | solution.py:337
  35.1 7.2 %collective-permute-start.13 = (bf16[2048,128]{1,0:T(8,128)(2,1)S(1)}, bf16[2048,128]{1,0:T(8,128)(2,1)S(1)}, u32[]{:S(2)}, u32[]{:S(2)}) collective-permute-start(bf16[2048,128]{1,0:T(8,128)(2,1)S(1)} %gate.6.refs_0_), channel_id=1, source_target_pairs={{0,1},{1,0},{2,3},{3,2},{4,5},{5,4},{6,7},{7,6},{8,9},{9,8},{10,11... | collective-permute-start | bytes 1572872 | tf_op jit(solution)/shard_map/ppermute | solution.py:337
  35.1 7.5 %collective-permute-start.17 = (bf16[2048,128]{1,0:T(8,128)(2,1)S(1)}, bf16[2048,128]{1,0:T(8,128)(2,1)S(1)}, u32[]{:S(2)}, u32[]{:S(2)}) collective-permute-start(bf16[2048,128]{1,0:T(8,128)(2,1)S(1)} %collective-permute-done.16.refs_4_), channel_id=1, source_target_pairs={{0,1},{1,0},{2,3},{3,2},{4,5},{5,4},{6,7},{7,6},{8,9},{9,8},{10,11... | collective-permute-start | bytes 1572872 | tf_op jit(solution)/shard_map/ppermute | solution.py:337
  40.2 14.7 %collective-permute-start.12 = (bf16[2048,128]{1,0:T(8,128)(2,1)S(1)}, bf16[2048,128]{1,0:T(8,128)(2,1)S(1)}, u32[]{:S(2)}, u32[]{:S(2)}) collective-permute-start(bf16[2048,128]{1,0:T(8,128)(2,1)S(1)} %collective-permute-done.1.refs_6_), channel_id=1, source_target_pairs={{0,2},{1,5},{2,0},{3,7},{4,6},{5,1},{6,4},{7,3},{8,10},{9,13},{10,... | collective-permute-start | bytes 1572872 | tf_op jit(solution)/shard_map/ppermute | solution.py:337
  41.7 13.2 %collective-permute-start.10 = (bf16[2048,128]{1,0:T(8,128)(2,1)S(1)}, bf16[2048,128]{1,0:T(8,128)(2,1)S(1)}, u32[]{:S(2)}, u32[]{:S(2)}) collective-permute-start(bf16[2048,128]{1,0:T(8,128)(2,1)S(1)} %gate.6.refs_0_), channel_id=1, source_target_pairs={{0,4},{1,3},{2,6},{3,1},{4,0},{5,7},{6,2},{7,5},{8,12},{9,11},{10,... | collective-permute-start | bytes 1572872 | tf_op jit(solution)/shard_map/ppermute | solution.py:337
  42.2 15.4 %collective-permute-start.2 = (bf16[2048,128]{1,0:T(8,128)(2,1)S(1)}, bf16[2048,128]{1,0:T(8,128)(2,1)S(1)}, u32[]{:S(2)}, u32[]{:S(2)}) collective-permute-start(bf16[2048,128]{1,0:T(8,128)(2,1)S(1)} %collective-permute-done.1.refs_6_), channel_id=1, source_target_pairs={{0,8},{1,9},{2,10},{3,11},{4,12},{5,13},{6,14},{7,15},{8,16},{9,17... | collective-permute-start | bytes 1572872 | tf_op jit(solution)/shard_map/ppermute | solution.py:337
  42.6 17.2 %collective-permute-start.20 = (bf16[2048,128]{1,0:T(8,128)(2,1)S(1)}, bf16[2048,128]{1,0:T(8,128)(2,1)S(1)}, u32[]{:S(2)}, u32[]{:S(2)}) collective-permute-start(bf16[2048,128]{1,0:T(8,128)(2,1)S(1)} %collective-permute-done.1.refs_6_), channel_id=1, source_target_pairs={{0,4},{1,3},{2,6},{3,1},{4,0},{5,7},{6,2},{7,5},{8,12},{9,11},{10,... | collective-permute-start | bytes 1572872 | tf_op jit(solution)/shard_map/ppermute | solution.py:337
  43.8 16.0 %collective-permute-start.21 = (bf16[2048,128]{1,0:T(8,128)(2,1)S(1)}, bf16[2048,128]{1,0:T(8,128)(2,1)S(1)}, u32[]{:S(2)}, u32[]{:S(2)}) collective-permute-start(bf16[2048,128]{1,0:T(8,128)(2,1)S(1)} %collective-permute-done.14.refs_2_), channel_id=1, source_target_pairs={{0,1},{1,0},{2,3},{3,2},{4,5},{5,4},{6,7},{7,6},{8,9},{9,8},{10,11... | collective-permute-start | bytes 1572872 | tf_op jit(solution)/shard_map/ppermute | solution.py:337
  54.9 6.3 %collective-permute-start.19 = (bf16[2048,128]{1,0:T(8,128)(2,1)S(1)}, bf16[2048,128]{1,0:T(8,128)(2,1)S(1)}, u32[]{:S(2)}, u32[]{:S(2)}) collective-permute-start(bf16[2048,128]{1,0:T(8,128)(2,1)S(1)} %gate.7.refs_0_), channel_id=1, source_target_pairs={{0,1},{1,0},{2,3},{3,2},{4,5},{5,4},{6,7},{7,6},{8,9},{9,8},{10,11... | collective-permute-start | bytes 1572872 | tf_op jit(solution)/shard_map/ppermute | solution.py:337
  54.9 7.5 %collective-permute-start.22 = (bf16[2048,128]{1,0:T(8,128)(2,1)S(1)}, bf16[2048,128]{1,0:T(8,128)(2,1)S(1)}, u32[]{:S(2)}, u32[]{:S(2)}) collective-permute-start(bf16[2048,128]{1,0:T(8,128)(2,1)S(1)} %collective-permute-done.10.refs_4_), channel_id=1, source_target_pairs={{0,1},{1,0},{2,3},{3,2},{4,5},{5,4},{6,7},{7,6},{8,9},{9,8},{10,11... | collective-permute-start | bytes 1572872 | tf_op jit(solution)/shard_map/ppermute | solution.py:337
  59.8 15.8 %collective-permute-start.11 = (bf16[2048,128]{1,0:T(8,128)(2,1)S(1)}, bf16[2048,128]{1,0:T(8,128)(2,1)S(1)}, u32[]{:S(2)}, u32[]{:S(2)}) collective-permute-start(bf16[2048,128]{1,0:T(8,128)(2,1)S(1)} %collective-permute-done.10.refs_4_), channel_id=1, source_target_pairs={{0,8},{1,9},{2,10},{3,11},{4,12},{5,13},{6,14},{7,15},{8,16},{9,17... | collective-permute-start | bytes 1572872 | tf_op jit(solution)/shard_map/ppermute | solution.py:337
  59.8 15.8 %collective-permute-start.3 = (bf16[2048,128]{1,0:T(8,128)(2,1)S(1)}, bf16[2048,128]{1,0:T(8,128)(2,1)S(1)}, u32[]{:S(2)}, u32[]{:S(2)}) collective-permute-start(bf16[2048,128]{1,0:T(8,128)(2,1)S(1)} %collective-permute-done.2.refs_6_), channel_id=1, source_target_pairs={{0,2},{1,5},{2,0},{3,7},{4,6},{5,1},{6,4},{7,3},{8,10},{9,13},{10,... | collective-permute-start | bytes 1572872 | tf_op jit(solution)/shard_map/ppermute | solution.py:337
  61.3 14.9 %collective-permute-start.26 = (bf16[2048,128]{1,0:T(8,128)(2,1)S(1)}, bf16[2048,128]{1,0:T(8,128)(2,1)S(1)}, u32[]{:S(2)}, u32[]{:S(2)}) collective-permute-start(bf16[2048,128]{1,0:T(8,128)(2,1)S(1)} %collective-permute-done.2.refs_6_), channel_id=1, source_target_pairs={{0,4},{1,3},{2,6},{3,1},{4,0},{5,7},{6,2},{7,5},{8,12},{9,11},{10,... | collective-permute-start | bytes 1572872 | tf_op jit(solution)/shard_map/ppermute | solution.py:337
  62.5 14.7 %collective-permute-start.27 = (bf16[2048,128]{1,0:T(8,128)(2,1)S(1)}, bf16[2048,128]{1,0:T(8,128)(2,1)S(1)}, u32[]{:S(2)}, u32[]{:S(2)}) collective-permute-start(bf16[2048,128]{1,0:T(8,128)(2,1)S(1)} %collective-permute-done.20.refs_2_), channel_id=1, source_target_pairs={{0,1},{1,0},{2,3},{3,2},{4,5},{5,4},{6,7},{7,6},{8,9},{9,8},{10,11... | collective-permute-start | bytes 1572872 | tf_op jit(solution)/shard_map/ppermute | solution.py:337
  76.2 9.4 %collective-permute-start.24 = (bf16[2048,128]{1,0:T(8,128)(2,1)S(1)}, bf16[2048,128]{1,0:T(8,128)(2,1)S(1)}, u32[]{:S(2)}, u32[]{:S(2)}) collective-permute-start(bf16[2048,128]{1,0:T(8,128)(2,1)S(1)} %get-tuple-element.49.refs_0_), channel_id=1, source_target_pairs={{0,4},{1,3},{2,6},{3,1},{4,0},{5,7},{6,2},{7,5},{8,12},{9,11},{10,... | collective-permute-start | bytes 1572872 | tf_op jit(solution)/shard_map/ppermute | solution.py:337
  (12 other events, 70.4 us)

commit v7 on v6

--- a/solution.py
+++ b/solution.py
@@ -156,7 +156,7 @@
             stacked = jnp.concatenate(vectors, axis=0).astype(jnp.bfloat16)
             halves.append(
                 lax.dot_general(
-                    stacked, stacked, (((1,), (1,)), ((), ())), preferred_element_type=jnp.float32
+                    stacked[: 8 * F], stacked, (((1,), (1,)), ((), ())), preferred_element_type=jnp.float32
                 )
             )
         for i in range(F):
@@ -168,7 +168,7 @@
             ).astype(jnp.bfloat16)
         return 0
 
-    lax.fori_loop(0, queries // 16, sixteen_queries, 0, unroll=8)
+    lax.fori_loop(0, queries // 16, sixteen_queries, 0, unroll=12)
 
 
 def inter_columns(masked, dense_ref, inter, queries):
@@ -204,21 +204,28 @@
         inter, *refs = refs
     refs = refs[CHAINS:]
     if with_head:
-        inter, first_held, second_held, weight_sems, *refs = refs
+        inter, first_held, second_held, out_held, weight_sems, *refs = refs
+    masked, dense_held, dense_sem, *entry_held, held, table, sems = refs
+    queries = dense_ref.shape[0]
+    pooling = pool_shards(
+        first, (0, 1), (slot_ref, bag_ref), entry_held, shards, sems, held, table, old_sums
+    )
+    next(pooling)
+    dense_copy = pltpu.make_async_copy(dense_ref, dense_held, dense_sem)
+    dense_copy.start()
+    if with_head:
         weights = [
             pltpu.make_async_copy(w_first, first_held, weight_sems.at[0]),
             pltpu.make_async_copy(w_second, second_held, weight_sems.at[1]),
+            pltpu.make_async_copy(w_out, out_held, weight_sems.at[2]),
         ]
         for copy in weights:
             copy.start()
-    masked, *entry_held, held, table, sems = refs
-    queries = dense_ref.shape[0]
-    for _ in pool_shards(
-        first, (0, 1), (slot_ref, bag_ref), entry_held, shards, sems, held, table, old_sums
-    ):
+    for _ in pooling:
         pass
-    interact(old_sums, dense_ref, masked, queries)
-    inter_columns(masked, dense_ref, inter, queries)
+    dense_copy.wait()
+    interact(old_sums, dense_held, masked, queries)
+    inter_columns(masked, dense_held, inter, queries)
     if not with_head:
         return
     for copy in weights:
@@ -230,7 +237,7 @@
         hidden = jnp.dot(inter[rows, :inputs], first_held[...], preferred_element_type=jnp.float32)
         hidden = jnp.maximum(hidden, 0.0).astype(jnp.bfloat16)
         second = jnp.dot(hidden, second_held[...], preferred_element_type=jnp.float32)
-        scored = jnp.maximum(second, 0.0) * w_out[...]
+        scored = jnp.maximum(second, 0.0) * out_held[...]
         folded = scored[:, :LANES]
         for tile in range(1, scored.shape[1] // LANES):
             folded = folded + scored[:, tile * LANES : (tile + 1) * LANES]
@@ -270,25 +277,30 @@
     n_shards = len(shards)
     queries = dense_rows.shape[0]
     width = 4 * LANES
-    masked = pltpu.VMEM((F, queries, 256), jnp.bfloat16)
+    masked = [
+        pltpu.VMEM((F, queries, 256), jnp.bfloat16),
+        pltpu.VMEM(dense_rows.shape, dense_rows.dtype),
+        pltpu.SemaphoreType.DMA,
+    ]
     if head is None:
         head_args, head_specs = [], []
         out_shape = jax.ShapeDtypeStruct((queries, width), jnp.bfloat16)
-        scratch = [masked]
+        scratch = masked
     else:
-        head_args, head_specs = list(head), [HBM_SPEC, HBM_SPEC, VMEM_SPEC]
+        head_args, head_specs = list(head), [HBM_SPEC, HBM_SPEC, ANY_SPEC]
         out_shape = jax.ShapeDtypeStruct((queries,), jnp.float32)
         scratch = [
             pltpu.VMEM((queries, width), jnp.bfloat16),
             pltpu.VMEM(head[0].shape, jnp.bfloat16),
             pltpu.VMEM(head[1].shape, jnp.bfloat16),
-            pltpu.SemaphoreType.DMA((2,)),
-            masked,
+            pltpu.VMEM(head[2].shape, jnp.float32),
+            pltpu.SemaphoreType.DMA((3,)),
+            *masked,
         ]
     out = pl.pallas_call(
         functools.partial(final_kernel, first, n_shards, head is not None),
         out_shape=[out_shape] + [pltpu.VMEM(one.shape, one.dtype) for one in sums],
-        in_specs=[HBM_SPEC] * 2 + [ANY_SPEC] * n_shards + [VMEM_SPEC] * (CHAINS + 1) + head_specs,
+        in_specs=[HBM_SPEC] * 2 + [ANY_SPEC] * n_shards + [VMEM_SPEC] * CHAINS + [ANY_SPEC] + head_specs,
         out_specs=[VMEM_SPEC] * (CHAINS + 1),
         input_output_aliases={2 + n_shards + k: 1 + k for k in range(CHAINS)},
         scratch_shapes=scratch + pool_scratch(n_shards, shards[0].shape[0], cap),

time: 98.9 us -> 98.5 us (level)
  starting transfers between devices: 19.8 us -> 18.6 us
  waiting for transfers between devices: 32.6 us -> 33.8 us
  Pallas kernels: 43.2 us -> 42.2 us
    ppermute x31, waiting for transfers between devices: 32.6 us -> 33.8 us  [hop(): return lambda array: lax.ppermute(array, 'cache', pairs)]
    ppermute x31, starting transfers between devices: 19.8 us -> 18.6 us  [hop(): return lambda array: lax.ppermute(array, 'cache', pairs)]
where the time goes in v7:
time: 98.5 us; the launch traced here: 97.6 us
  Pallas kernels  42.2 us (43%)
  waiting for transfers between devices  33.8 us (34%)
  starting transfers between devices  18.6 us (19%)
  local copies, waits for them, and re-layouts  2.41 us (2%)
    ppermute x31, waiting for transfers between devices, hop(): return lambda array: lax.ppermute(array, 'cache', pairs)  33.8 us
    pallas_call x5, Pallas kernels, pool(): pl.pallas_call(functools.partial(pool_kernel, first, rows, is_first), out...  30.9 us
    ppermute x31, starting transfers between devices, hop(): return lambda array: lax.ppermute(array, 'cache', pairs)  18.6 us
    pallas_call x1, Pallas kernels, finish(): pl.pallas_call(functools.partial(final_kernel, first, n_shards, head is n...  9.3 us
    pallas_call x1, Pallas kernels, fill(): pl.pallas_call(fill_kernel, out_shape=pltpu.VMEM(cache_rows.shape, cache_...  1.97 us
  transfers between devices with their start and end apart: 31, of which 13 were waited for; matrix products, arithmetic and copies ran while one was open for 3% of the time, Pallas kernels for 32%

profile of v7, /device:TPU:0, one launch (start us, length us, event | category | flops | bytes accessed | tf_op | source)
XLA Modules:
  0.0 97.6 jit_solution(7975727556960210225)
XLA Ops:
  0.0 2.0 %fill.1.refs_0_ = bf16[2048,128]{1,0:T(8,128)(2,1)S(1)} custom-call(s32[2]{0:T(128)} %bitcast.42, s32[2]{0:T(128)} %bitcast.43, bf16[2048,128]{1,0:T(8,128)(2,1)} %cache_ref.1, bf16[1024,128]{1,0:T(8,128)(2,1)} %fills_ref.1), custom_call_target="tpu_custom_call" | custom-call | tf_op jit(solution)/shard_map/fill/pallas_call | solution.py:57
  2.0 3.0 %collective-permute-start.5 = (bf16[2048,128]{1,0:T(8,128)(2,1)S(1)}, bf16[2048,128]{1,0:T(8,128)(2,1)S(1)}, u32[]{:S(2)}, u32[]{:S(2)}) collective-permute-start(bf16[2048,128]{1,0:T(8,128)(2,1)S(1)} %fill.1.refs_0_), channel_id=1, source_target_pairs={{0,2},{1,5},{2,0},{3,7},{4,6},{5,1},{6,4},{7,3},{8,10},{9,13},{10,... | collective-permute-start | bytes 1572872 | tf_op jit(solution)/shard_map/ppermute | solution.py:349
  5.0 1.6 %collective-permute-start = (bf16[2048,128]{1,0:T(8,128)(2,1)S(1)}, bf16[2048,128]{1,0:T(8,128)(2,1)S(1)}, u32[]{:S(2)}, u32[]{:S(2)}) collective-permute-start(bf16[2048,128]{1,0:T(8,128)(2,1)S(1)} %fill.1.refs_0_), channel_id=1, source_target_pairs={{0,8},{1,9},{2,10},{3,11},{4,12},{5,13},{6,14},{7,15},{8,16},{9,17... | collective-permute-start | bytes 1572872 | tf_op jit(solution)/shard_map/ppermute | solution.py:349
  6.6 1.5 %collective-permute-start.7 = (bf16[2048,128]{1,0:T(8,128)(2,1)S(1)}, bf16[2048,128]{1,0:T(8,128)(2,1)S(1)}, u32[]{:S(2)}, u32[]{:S(2)}) collective-permute-start(bf16[2048,128]{1,0:T(8,128)(2,1)S(1)} %fill.1.refs_0_), channel_id=1, source_target_pairs={{0,4},{1,3},{2,6},{3,1},{4,0},{5,7},{6,2},{7,5},{8,12},{9,11},{10,... | collective-permute-start | bytes 1572872 | tf_op jit(solution)/shard_map/ppermute | solution.py:349
  9.2 1.6 %gather_fusion.1 = s32[48,624]{1,0:T(8,128)S(1)} fusion(s32[32,624]{1,0:T(8,128)} %bitcast.41, s32[1024]{0:T(1024)S(1)} %pad_clamp_fusion), kind=kCustom, calls=%fused_computation.1 | custom fusion | bytes 239808 | tf_op jit(solution)/shard_map/gather | solution.py:380
  10.9 2.4 %pool.5 = (f32[9992,128]{1,0:T(8,128)S(1)}, f32[9992,128]{1,0:T(8,128)S(1)}, f32[9992,128]{1,0:T(8,128)S(1)}, f32[9992,128]{1,0:T(8,128)S(1)}, s32[8,128]{1,0:T(8,128)S(1)}) custom-call(s32[30720]{0:T(1024)S(1)} %reshape.1470.slot_ref, s32[30720]{0:T(1024)S(1)} %reshape.1471.bag_ref, bf16[2048,128]{1,0:T(8,128)(2,1)S(1)} %fill.1.refs_0_), custom_call_target="tpu_custom_call" | custom-call | bytes 3000000 | tf_op jit(solution)/shard_map/pool/pallas_call | solution.py:261
  13.3 2.5 %collective-permute-done.5.refs_0_ = bf16[2048,128]{1,0:T(8,128)(2,1)S(1)} collective-permute-done((bf16[2048,128]{1,0:T(8,128)(2,1)S(1)}, bf16[2048,128]{1,0:T(8,128)(2,1)S(1)}, u32[]{:S(2)}, u32[]{:S(2)}) %collective-permute-start.5) | collective-permute-done | bytes 524320 | tf_op jit(solution)/shard_map/ppermute | solution.py:349
  15.9 4.4 %collective-permute-done.refs_4_ = bf16[2048,128]{1,0:T(8,128)(2,1)S(1)} collective-permute-done((bf16[2048,128]{1,0:T(8,128)(2,1)S(1)}, bf16[2048,128]{1,0:T(8,128)(2,1)S(1)}, u32[]{:S(2)}, u32[]{:S(2)}) %collective-permute-start) | collective-permute-done | bytes 524320 | tf_op jit(solution)/shard_map/ppermute | solution.py:349
  20.3 1.5 %collective-permute-start.4 = (bf16[2048,128]{1,0:T(8,128)(2,1)S(1)}, bf16[2048,128]{1,0:T(8,128)(2,1)S(1)}, u32[]{:S(2)}, u32[]{:S(2)}) collective-permute-start(bf16[2048,128]{1,0:T(8,128)(2,1)S(1)} %collective-permute-done.refs_4_), channel_id=1, source_target_pairs={{0,2},{1,5},{2,0},{3,7},{4,6},{5,1},{6,4},{7,3},{8,10},{9,13},{10,... | collective-permute-start | bytes 1572872 | tf_op jit(solution)/shard_map/ppermute | solution.py:349
  23.9 6.4 %pool.6 = (f32[9992,128]{1,0:T(8,128)S(1)}, f32[9992,128]{1,0:T(8,128)S(1)}, f32[9992,128]{1,0:T(8,128)S(1)}, f32[9992,128]{1,0:T(8,128)S(1)}, s32[8,128]{1,0:T(8,128)S(1)}) custom-call(s32[30720]{0:T(1024)S(1)} %reshape.1470.slot_ref, s32[30720]{0:T(1024)S(1)} %reshape.1471.bag_ref, ...), custom_call_target="tpu_custom_call", output_to_operand_aliasing={{0}: (8, {}), {1}: (9, {}), {2}: (10, {}), {3}: (11, {})} | custom-call | bytes 18000000 | tf_op jit(solution)/shard_map/pool/pallas_call | solution.py:261
  30.3 4.7 %collective-permute-done.4.refs_0_ = bf16[2048,128]{1,0:T(8,128)(2,1)S(1)} collective-permute-done((bf16[2048,128]{1,0:T(8,128)(2,1)S(1)}, bf16[2048,128]{1,0:T(8,128)(2,1)S(1)}, u32[]{:S(2)}, u32[]{:S(2)}) %collective-permute-start.4) | collective-permute-done | bytes 524320 | tf_op jit(solution)/shard_map/ppermute | solution.py:349
  35.6 2.3 %collective-permute-done.1.refs_6_ = bf16[2048,128]{1,0:T(8,128)(2,1)S(1)} collective-permute-done((bf16[2048,128]{1,0:T(8,128)(2,1)S(1)}, bf16[2048,128]{1,0:T(8,128)(2,1)S(1)}, u32[]{:S(2)}, u32[]{:S(2)}) %collective-permute-start.1) | collective-permute-done | bytes 524320 | tf_op jit(solution)/shard_map/ppermute | solution.py:349
  37.8 2.4 %collective-permute-done.14.refs_2_ = bf16[2048,128]{1,0:T(8,128)(2,1)S(1)} collective-permute-done((bf16[2048,128]{1,0:T(8,128)(2,1)S(1)}, bf16[2048,128]{1,0:T(8,128)(2,1)S(1)}, u32[]{:S(2)}, u32[]{:S(2)}) %collective-permute-start.14) | collective-permute-done | bytes 524320 | tf_op jit(solution)/shard_map/ppermute | solution.py:349
  40.2 1.5 %collective-permute-start.12 = (bf16[2048,128]{1,0:T(8,128)(2,1)S(1)}, bf16[2048,128]{1,0:T(8,128)(2,1)S(1)}, u32[]{:S(2)}, u32[]{:S(2)}) collective-permute-start(bf16[2048,128]{1,0:T(8,128)(2,1)S(1)} %collective-permute-done.1.refs_6_), channel_id=1, source_target_pairs={{0,2},{1,5},{2,0},{3,7},{4,6},{5,1},{6,4},{7,3},{8,10},{9,13},{10,... | collective-permute-start | bytes 1572872 | tf_op jit(solution)/shard_map/ppermute | solution.py:349
  43.8 7.6 %pool.7 = (f32[9992,128]{1,0:T(8,128)S(1)}, f32[9992,128]{1,0:T(8,128)S(1)}, f32[9992,128]{1,0:T(8,128)S(1)}, f32[9992,128]{1,0:T(8,128)S(1)}, s32[8,128]{1,0:T(8,128)S(1)}) custom-call(s32[30720]{0:T(1024)S(1)} %reshape.1470.slot_ref, s32[30720]{0:T(1024)S(1)} %reshape.1471.bag_ref, ...), custom_call_target="tpu_custom_call", output_to_operand_aliasing={{0}: (10, {}), {1}: (11, {}), {2}: (12, {}), {3}: (13, {})} | custom-call | bytes 24000000 | tf_op jit(solution)/shard_map/pool/pallas_call | solution.py:261
  51.4 3.5 %collective-permute-done.12.refs_0_ = bf16[2048,128]{1,0:T(8,128)(2,1)S(1)} collective-permute-done((bf16[2048,128]{1,0:T(8,128)(2,1)S(1)}, bf16[2048,128]{1,0:T(8,128)(2,1)S(1)}, u32[]{:S(2)}, u32[]{:S(2)}) %collective-permute-start.12) | collective-permute-done | bytes 524320 | tf_op jit(solution)/shard_map/ppermute | solution.py:349
  55.4 2.1 %collective-permute-done.2.refs_6_ = bf16[2048,128]{1,0:T(8,128)(2,1)S(1)} collective-permute-done((bf16[2048,128]{1,0:T(8,128)(2,1)S(1)}, bf16[2048,128]{1,0:T(8,128)(2,1)S(1)}, u32[]{:S(2)}, u32[]{:S(2)}) %collective-permute-start.2) | collective-permute-done | bytes 524320 | tf_op jit(solution)/shard_map/ppermute | solution.py:349
  57.6 2.2 %collective-permute-done.20.refs_2_ = bf16[2048,128]{1,0:T(8,128)(2,1)S(1)} collective-permute-done((bf16[2048,128]{1,0:T(8,128)(2,1)S(1)}, bf16[2048,128]{1,0:T(8,128)(2,1)S(1)}, u32[]{:S(2)}, u32[]{:S(2)}) %collective-permute-start.20) | collective-permute-done | bytes 524320 | tf_op jit(solution)/shard_map/ppermute | solution.py:349
  59.8 1.5 %collective-permute-start.3 = (bf16[2048,128]{1,0:T(8,128)(2,1)S(1)}, bf16[2048,128]{1,0:T(8,128)(2,1)S(1)}, u32[]{:S(2)}, u32[]{:S(2)}) collective-permute-start(bf16[2048,128]{1,0:T(8,128)(2,1)S(1)} %collective-permute-done.2.refs_6_), channel_id=1, source_target_pairs={{0,2},{1,5},{2,0},{3,7},{4,6},{5,1},{6,4},{7,3},{8,10},{9,13},{10,... | collective-permute-start | bytes 1572872 | tf_op jit(solution)/shard_map/ppermute | solution.py:349
  62.5 7.3 %pool.8 = (f32[9992,128]{1,0:T(8,128)S(1)}, f32[9992,128]{1,0:T(8,128)S(1)}, f32[9992,128]{1,0:T(8,128)S(1)}, f32[9992,128]{1,0:T(8,128)S(1)}, s32[8,128]{1,0:T(8,128)S(1)}) custom-call(s32[30720]{0:T(1024)S(1)} %reshape.1470.slot_ref, s32[30720]{0:T(1024)S(1)} %reshape.1471.bag_ref, ...), custom_call_target="tpu_custom_call", output_to_operand_aliasing={{0}: (10, {}), {1}: (11, {}), {2}: (12, {}), {3}: (13, {})} | custom-call | bytes 24000000 | tf_op jit(solution)/shard_map/pool/pallas_call | solution.py:261
  69.8 5.8 %collective-permute-done.11.refs_1_ = bf16[2048,128]{1,0:T(8,128)(2,1)S(1)} collective-permute-done((bf16[2048,128]{1,0:T(8,128)(2,1)S(1)}, bf16[2048,128]{1,0:T(8,128)(2,1)S(1)}, u32[]{:S(2)}, u32[]{:S(2)}) %collective-permute-start.11) | collective-permute-done | bytes 524320 | tf_op jit(solution)/shard_map/ppermute | solution.py:349
  79.1 7.1 %pool.9 = (f32[9992,128]{1,0:T(8,128)S(1)}, f32[9992,128]{1,0:T(8,128)S(1)}, f32[9992,128]{1,0:T(8,128)S(1)}, f32[9992,128]{1,0:T(8,128)S(1)}, s32[8,128]{1,0:T(8,128)S(1)}) custom-call(s32[30720]{0:T(1024)S(1)} %reshape.1470.slot_ref, s32[30720]{0:T(1024)S(1)} %reshape.1471.bag_ref, ...), custom_call_target="tpu_custom_call", output_to_operand_aliasing={{0}: (9, {}), {1}: (10, {}), {2}: (11, {}), {3}: (12, {})} | custom-call | bytes 21000000 | tf_op jit(solution)/shard_map/pool/pallas_call | solution.py:261
  86.3 1.9 %collective-permute-done.30.refs_1_ = bf16[2048,128]{1,0:T(8,128)(2,1)S(1)} collective-permute-done((bf16[2048,128]{1,0:T(8,128)(2,1)S(1)}, bf16[2048,128]{1,0:T(8,128)(2,1)S(1)}, u32[]{:S(2)}, u32[]{:S(2)}) %collective-permute-start.30) | collective-permute-done | bytes 524320 | tf_op jit(solution)/shard_map/ppermute | solution.py:349
  88.2 9.3 %finish.1 = (f32[384]{0:T(512)}, f32[9992,128]{1,0:T(8,128)S(1)}, f32[9992,128]{1,0:T(8,128)S(1)}, f32[9992,128]{1,0:T(8,128)S(1)}, f32[9992,128]{1,0:T(8,128)S(1)}) custom-call(s32[30720]{0:T(1024)S(1)} %reshape.1470.slot_ref, s32[30720]{0:T(1024)S(1)} %reshape.1471.bag_ref, ...), custom_call_target="tpu_custom_call", output_to_operand_aliasing={{1}: (4, {}), {2}: (5, {}), {3}: (6, {}), {4}: (7, {})} | custom-call | tf_op jit(solution)/shard_map/finish/pallas_call | solution.py:300
  (73 shorter events, 11.1 us)
Async XLA Ops:
  2.0 13.9 %collective-permute-start.5 = (bf16[2048,128]{1,0:T(8,128)(2,1)S(1)}, bf16[2048,128]{1,0:T(8,128)(2,1)S(1)}, u32[]{:S(2)}, u32[]{:S(2)}) collective-permute-start(bf16[2048,128]{1,0:T(8,128)(2,1)S(1)} %fill.1.refs_0_), channel_id=1, source_target_pairs={{0,2},{1,5},{2,0},{3,7},{4,6},{5,1},{6,4},{7,3},{8,10},{9,13},{10,... | collective-permute-start | bytes 1572872 | tf_op jit(solution)/shard_map/ppermute | solution.py:349
  5.0 15.3 %collective-permute-start = (bf16[2048,128]{1,0:T(8,128)(2,1)S(1)}, bf16[2048,128]{1,0:T(8,128)(2,1)S(1)}, u32[]{:S(2)}, u32[]{:S(2)}) collective-permute-start(bf16[2048,128]{1,0:T(8,128)(2,1)S(1)} %fill.1.refs_0_), channel_id=1, source_target_pairs={{0,8},{1,9},{2,10},{3,11},{4,12},{5,13},{6,14},{7,15},{8,16},{9,17... | collective-permute-start | bytes 1572872 | tf_op jit(solution)/shard_map/ppermute | solution.py:349
  6.6 15.2 %collective-permute-start.7 = (bf16[2048,128]{1,0:T(8,128)(2,1)S(1)}, bf16[2048,128]{1,0:T(8,128)(2,1)S(1)}, u32[]{:S(2)}, u32[]{:S(2)}) collective-permute-start(bf16[2048,128]{1,0:T(8,128)(2,1)S(1)} %fill.1.refs_0_), channel_id=1, source_target_pairs={{0,4},{1,3},{2,6},{3,1},{4,0},{5,7},{6,2},{7,5},{8,12},{9,11},{10,... | collective-permute-start | bytes 1572872 | tf_op jit(solution)/shard_map/ppermute | solution.py:349
  8.1 14.2 %collective-permute-start.8 = (bf16[2048,128]{1,0:T(8,128)(2,1)S(1)}, bf16[2048,128]{1,0:T(8,128)(2,1)S(1)}, u32[]{:S(2)}, u32[]{:S(2)}) collective-permute-start(bf16[2048,128]{1,0:T(8,128)(2,1)S(1)} %fill.1.refs_0_), channel_id=1, source_target_pairs={{0,1},{1,0},{2,3},{3,2},{4,5},{5,4},{6,7},{7,6},{8,9},{9,8},{10,11... | collective-permute-start | bytes 1572872 | tf_op jit(solution)/shard_map/ppermute | solution.py:349
  15.8 7.3 %collective-permute-start.6 = (bf16[2048,128]{1,0:T(8,128)(2,1)S(1)}, bf16[2048,128]{1,0:T(8,128)(2,1)S(1)}, u32[]{:S(2)}, u32[]{:S(2)}) collective-permute-start(bf16[2048,128]{1,0:T(8,128)(2,1)S(1)} %gate.5.refs_0_), channel_id=1, source_target_pairs={{0,1},{1,0},{2,3},{3,2},{4,5},{5,4},{6,7},{7,6},{8,9},{9,8},{10,11... | collective-permute-start | bytes 1572872 | tf_op jit(solution)/shard_map/ppermute | solution.py:349
  20.3 14.8 %collective-permute-start.4 = (bf16[2048,128]{1,0:T(8,128)(2,1)S(1)}, bf16[2048,128]{1,0:T(8,128)(2,1)S(1)}, u32[]{:S(2)}, u32[]{:S(2)}) collective-permute-start(bf16[2048,128]{1,0:T(8,128)(2,1)S(1)} %collective-permute-done.refs_4_), channel_id=1, source_target_pairs={{0,2},{1,5},{2,0},{3,7},{4,6},{5,1},{6,4},{7,3},{8,10},{9,13},{10,... | collective-permute-start | bytes 1572872 | tf_op jit(solution)/shard_map/ppermute | solution.py:349
  21.8 13.3 %collective-permute-start.16 = (bf16[2048,128]{1,0:T(8,128)(2,1)S(1)}, bf16[2048,128]{1,0:T(8,128)(2,1)S(1)}, u32[]{:S(2)}, u32[]{:S(2)}) collective-permute-start(bf16[2048,128]{1,0:T(8,128)(2,1)S(1)} %gate.5.refs_0_), channel_id=1, source_target_pairs={{0,4},{1,3},{2,6},{3,1},{4,0},{5,7},{6,2},{7,5},{8,12},{9,11},{10,... | collective-permute-start | bytes 1572872 | tf_op jit(solution)/shard_map/ppermute | solution.py:349
  22.3 15.6 %collective-permute-start.1 = (bf16[2048,128]{1,0:T(8,128)(2,1)S(1)}, bf16[2048,128]{1,0:T(8,128)(2,1)S(1)}, u32[]{:S(2)}, u32[]{:S(2)}) collective-permute-start(bf16[2048,128]{1,0:T(8,128)(2,1)S(1)} %collective-permute-done.refs_4_), channel_id=1, source_target_pairs={{0,8},{1,9},{2,10},{3,11},{4,12},{5,13},{6,14},{7,15},{8,16},{9,17... | collective-permute-start | bytes 1572872 | tf_op jit(solution)/shard_map/ppermute | solution.py:349
  23.1 17.1 %collective-permute-start.14 = (bf16[2048,128]{1,0:T(8,128)(2,1)S(1)}, bf16[2048,128]{1,0:T(8,128)(2,1)S(1)}, u32[]{:S(2)}, u32[]{:S(2)}) collective-permute-start(bf16[2048,128]{1,0:T(8,128)(2,1)S(1)} %collective-permute-done.refs_4_), channel_id=1, source_target_pairs={{0,4},{1,3},{2,6},{3,1},{4,0},{5,7},{6,2},{7,5},{8,12},{9,11},{10,... | collective-permute-start | bytes 1572872 | tf_op jit(solution)/shard_map/ppermute | solution.py:349
  23.9 17.8 %collective-permute-start.15 = (bf16[2048,128]{1,0:T(8,128)(2,1)S(1)}, bf16[2048,128]{1,0:T(8,128)(2,1)S(1)}, u32[]{:S(2)}, u32[]{:S(2)}) collective-permute-start(bf16[2048,128]{1,0:T(8,128)(2,1)S(1)} %collective-permute-done.7.refs_2_), channel_id=1, source_target_pairs={{0,1},{1,0},{2,3},{3,2},{4,5},{5,4},{6,7},{7,6},{8,9},{9,8},{10,11... | collective-permute-start | bytes 1572872 | tf_op jit(solution)/shard_map/ppermute | solution.py:349
  35.1 7.2 %collective-permute-start.13 = (bf16[2048,128]{1,0:T(8,128)(2,1)S(1)}, bf16[2048,128]{1,0:T(8,128)(2,1)S(1)}, u32[]{:S(2)}, u32[]{:S(2)}) collective-permute-start(bf16[2048,128]{1,0:T(8,128)(2,1)S(1)} %gate.6.refs_0_), channel_id=1, source_target_pairs={{0,1},{1,0},{2,3},{3,2},{4,5},{5,4},{6,7},{7,6},{8,9},{9,8},{10,11... | collective-permute-start | bytes 1572872 | tf_op jit(solution)/shard_map/ppermute | solution.py:349
  35.1 7.5 %collective-permute-start.17 = (bf16[2048,128]{1,0:T(8,128)(2,1)S(1)}, bf16[2048,128]{1,0:T(8,128)(2,1)S(1)}, u32[]{:S(2)}, u32[]{:S(2)}) collective-permute-start(bf16[2048,128]{1,0:T(8,128)(2,1)S(1)} %collective-permute-done.16.refs_4_), channel_id=1, source_target_pairs={{0,1},{1,0},{2,3},{3,2},{4,5},{5,4},{6,7},{7,6},{8,9},{9,8},{10,11... | collective-permute-start | bytes 1572872 | tf_op jit(solution)/shard_map/ppermute | solution.py:349
  40.2 14.7 %collective-permute-start.12 = (bf16[2048,128]{1,0:T(8,128)(2,1)S(1)}, bf16[2048,128]{1,0:T(8,128)(2,1)S(1)}, u32[]{:S(2)}, u32[]{:S(2)}) collective-permute-start(bf16[2048,128]{1,0:T(8,128)(2,1)S(1)} %collective-permute-done.1.refs_6_), channel_id=1, source_target_pairs={{0,2},{1,5},{2,0},{3,7},{4,6},{5,1},{6,4},{7,3},{8,10},{9,13},{10,... | collective-permute-start | bytes 1572872 | tf_op jit(solution)/shard_map/ppermute | solution.py:349
  41.7 13.2 %collective-permute-start.10 = (bf16[2048,128]{1,0:T(8,128)(2,1)S(1)}, bf16[2048,128]{1,0:T(8,128)(2,1)S(1)}, u32[]{:S(2)}, u32[]{:S(2)}) collective-permute-start(bf16[2048,128]{1,0:T(8,128)(2,1)S(1)} %gate.6.refs_0_), channel_id=1, source_target_pairs={{0,4},{1,3},{2,6},{3,1},{4,0},{5,7},{6,2},{7,5},{8,12},{9,11},{10,... | collective-permute-start | bytes 1572872 | tf_op jit(solution)/shard_map/ppermute | solution.py:349
  42.2 15.4 %collective-permute-start.2 = (bf16[2048,128]{1,0:T(8,128)(2,1)S(1)}, bf16[2048,128]{1,0:T(8,128)(2,1)S(1)}, u32[]{:S(2)}, u32[]{:S(2)}) collective-permute-start(bf16[2048,128]{1,0:T(8,128)(2,1)S(1)} %collective-permute-done.1.refs_6_), channel_id=1, source_target_pairs={{0,8},{1,9},{2,10},{3,11},{4,12},{5,13},{6,14},{7,15},{8,16},{9,17... | collective-permute-start | bytes 1572872 | tf_op jit(solution)/shard_map/ppermute | solution.py:349
  42.6 17.2 %collective-permute-start.20 = (bf16[2048,128]{1,0:T(8,128)(2,1)S(1)}, bf16[2048,128]{1,0:T(8,128)(2,1)S(1)}, u32[]{:S(2)}, u32[]{:S(2)}) collective-permute-start(bf16[2048,128]{1,0:T(8,128)(2,1)S(1)} %collective-permute-done.1.refs_6_), channel_id=1, source_target_pairs={{0,4},{1,3},{2,6},{3,1},{4,0},{5,7},{6,2},{7,5},{8,12},{9,11},{10,... | collective-permute-start | bytes 1572872 | tf_op jit(solution)/shard_map/ppermute | solution.py:349
  43.8 16.0 %collective-permute-start.21 = (bf16[2048,128]{1,0:T(8,128)(2,1)S(1)}, bf16[2048,128]{1,0:T(8,128)(2,1)S(1)}, u32[]{:S(2)}, u32[]{:S(2)}) collective-permute-start(bf16[2048,128]{1,0:T(8,128)(2,1)S(1)} %collective-permute-done.14.refs_2_), channel_id=1, source_target_pairs={{0,1},{1,0},{2,3},{3,2},{4,5},{5,4},{6,7},{7,6},{8,9},{9,8},{10,11... | collective-permute-start | bytes 1572872 | tf_op jit(solution)/shard_map/ppermute | solution.py:349
  54.9 6.3 %collective-permute-start.19 = (bf16[2048,128]{1,0:T(8,128)(2,1)S(1)}, bf16[2048,128]{1,0:T(8,128)(2,1)S(1)}, u32[]{:S(2)}, u32[]{:S(2)}) collective-permute-start(bf16[2048,128]{1,0:T(8,128)(2,1)S(1)} %gate.7.refs_0_), channel_id=1, source_target_pairs={{0,1},{1,0},{2,3},{3,2},{4,5},{5,4},{6,7},{7,6},{8,9},{9,8},{10,11... | collective-permute-start | bytes 1572872 | tf_op jit(solution)/shard_map/ppermute | solution.py:349
  54.9 7.5 %collective-permute-start.22 = (bf16[2048,128]{1,0:T(8,128)(2,1)S(1)}, bf16[2048,128]{1,0:T(8,128)(2,1)S(1)}, u32[]{:S(2)}, u32[]{:S(2)}) collective-permute-start(bf16[2048,128]{1,0:T(8,128)(2,1)S(1)} %collective-permute-done.10.refs_4_), channel_id=1, source_target_pairs={{0,1},{1,0},{2,3},{3,2},{4,5},{5,4},{6,7},{7,6},{8,9},{9,8},{10,11... | collective-permute-start | bytes 1572872 | tf_op jit(solution)/shard_map/ppermute | solution.py:349
  59.8 15.8 %collective-permute-start.11 = (bf16[2048,128]{1,0:T(8,128)(2,1)S(1)}, bf16[2048,128]{1,0:T(8,128)(2,1)S(1)}, u32[]{:S(2)}, u32[]{:S(2)}) collective-permute-start(bf16[2048,128]{1,0:T(8,128)(2,1)S(1)} %collective-permute-done.10.refs_4_), channel_id=1, source_target_pairs={{0,8},{1,9},{2,10},{3,11},{4,12},{5,13},{6,14},{7,15},{8,16},{9,17... | collective-permute-start | bytes 1572872 | tf_op jit(solution)/shard_map/ppermute | solution.py:349
  59.8 15.8 %collective-permute-start.3 = (bf16[2048,128]{1,0:T(8,128)(2,1)S(1)}, bf16[2048,128]{1,0:T(8,128)(2,1)S(1)}, u32[]{:S(2)}, u32[]{:S(2)}) collective-permute-start(bf16[2048,128]{1,0:T(8,128)(2,1)S(1)} %collective-permute-done.2.refs_6_), channel_id=1, source_target_pairs={{0,2},{1,5},{2,0},{3,7},{4,6},{5,1},{6,4},{7,3},{8,10},{9,13},{10,... | collective-permute-start | bytes 1572872 | tf_op jit(solution)/shard_map/ppermute | solution.py:349
  61.3 14.9 %collective-permute-start.26 = (bf16[2048,128]{1,0:T(8,128)(2,1)S(1)}, bf16[2048,128]{1,0:T(8,128)(2,1)S(1)}, u32[]{:S(2)}, u32[]{:S(2)}) collective-permute-start(bf16[2048,128]{1,0:T(8,128)(2,1)S(1)} %collective-permute-done.2.refs_6_), channel_id=1, source_target_pairs={{0,4},{1,3},{2,6},{3,1},{4,0},{5,7},{6,2},{7,5},{8,12},{9,11},{10,... | collective-permute-start | bytes 1572872 | tf_op jit(solution)/shard_map/ppermute | solution.py:349
  62.5 14.7 %collective-permute-start.27 = (bf16[2048,128]{1,0:T(8,128)(2,1)S(1)}, bf16[2048,128]{1,0:T(8,128)(2,1)S(1)}, u32[]{:S(2)}, u32[]{:S(2)}) collective-permute-start(bf16[2048,128]{1,0:T(8,128)(2,1)S(1)} %collective-permute-done.20.refs_2_), channel_id=1, source_target_pairs={{0,1},{1,0},{2,3},{3,2},{4,5},{5,4},{6,7},{7,6},{8,9},{9,8},{10,11... | collective-permute-start | bytes 1572872 | tf_op jit(solution)/shard_map/ppermute | solution.py:349
  76.2 10.0 %collective-permute-start.24 = (bf16[2048,128]{1,0:T(8,128)(2,1)S(1)}, bf16[2048,128]{1,0:T(8,128)(2,1)S(1)}, u32[]{:S(2)}, u32[]{:S(2)}) collective-permute-start(bf16[2048,128]{1,0:T(8,128)(2,1)S(1)} %get-tuple-element.49.refs_0_), channel_id=1, source_target_pairs={{0,4},{1,3},{2,6},{3,1},{4,0},{5,7},{6,2},{7,5},{8,12},{9,11},{10,... | collective-permute-start | bytes 1572872 | tf_op jit(solution)/shard_map/ppermute | solution.py:349
  (12 other events, 68.7 us)

commit v8 on v7

--- a/solution.py
+++ b/solution.py
@@ -392,7 +392,7 @@
     crossed, turned, next_piece = first_hop(own), second_hop(own), next_plane(own)
     sums, done = pool(0, entries, cap, [own], None, sum_rows, [0])
     (crossed,) = gate([crossed], done)
-    far, late = [], other_core(own)
+    far, late = [], [other_core(own)]
     for shift in range(n_planes):
         last = shift == n_planes - 1
         near = of_chip(crossed) + [turned]
@@ -406,16 +406,18 @@
                 passed.append(next_plane(next_piece))
         else:
             piece = [other_turned]
-        if shift == 0:
-            shards, rows = near + [late] + piece, [0, 1, 2, 3, 6, 7]
-        else:
-            shards, rows = near + [late] + far + piece, list(range(6 + len(piece)))
+        shards = near + late + far + piece
+        rows = [0, 1, 2] + [3][: len(late)] + [4, 5][: len(far)] + [6, 7][: len(piece)]
         sums, done = pool(8 * shift + 8, entries, cap, shards, sums, sum_rows, rows)
+        if shift == n_planes - 2:
+            sums, done = pool(8 * shift + 16, entries, cap, [other_turned], sums, sum_rows, [3])
         chosen = [0] if last else [1, 0] if shift == n_planes - 2 else [index for index in PICK if index < len(passed)]
         for index, one in zip(chosen, gate([passed[index] for index in chosen], done)):
             passed[index] = one
         next_far, *passed = passed
-        far, late = of_chip(next_far), other_turned
+        far, late = of_chip(next_far), [other_turned]
+        if shift == n_planes - 2:
+            late = []
         if not last:
             crossed, turned, *next_piece = passed
             next_piece = next_piece[0] if next_piece else None

time: 98.5 us -> 97.4 us (0.989)
  waiting for transfers between devices: 33.8 us -> 31.7 us
  Pallas kernels: 42.2 us -> 44 us
    ppermute x31, waiting for transfers between devices: 33.8 us -> 31.7 us  [hop(): return lambda array: lax.ppermute(array, 'cache', pairs)]
    pallas_call x5 -> x6, Pallas kernels: 30.9 us -> 32.5 us  [pool(): pl.pallas_call(functools.partial(pool_kernel, first, rows, is_first), out...]
  transfers between devices with their start and end apart: 31 -> 31, of which waited for: 13 -> 14; matrix products, arithmetic and copies ran while one was open for 3% -> 3% of each run, Pallas kernels for 32% -> 33%
where the time goes in v8:
time: 97.4 us; the launch traced here: 97.3 us
  Pallas kernels  44 us (45%)
  waiting for transfers between devices  31.7 us (33%)
  starting transfers between devices  18.5 us (19%)
  local copies, waits for them, and re-layouts  2.41 us (2%)
    pallas_call x6, Pallas kernels, pool(): pl.pallas_call(functools.partial(pool_kernel, first, rows, is_first), out...  32.5 us
    ppermute x31, waiting for transfers between devices, hop(): return lambda array: lax.ppermute(array, 'cache', pairs)  31.7 us
    ppermute x31, starting transfers between devices, hop(): return lambda array: lax.ppermute(array, 'cache', pairs)  18.5 us
    pallas_call x1, Pallas kernels, finish(): pl.pallas_call(functools.partial(final_kernel, first, n_shards, head is n...  9.49 us
    pallas_call x1, Pallas kernels, fill(): pl.pallas_call(fill_kernel, out_shape=pltpu.VMEM(cache_rows.shape, cache_...  1.97 us
  transfers between devices with their start and end apart: 31, of which 14 were waited for; matrix products, arithmetic and copies ran while one was open for 3% of the time, Pallas kernels for 33%

profile of v8, /device:TPU:0, one launch (start us, length us, event | category | flops | bytes accessed | tf_op | source)
XLA Modules:
  0.0 97.3 jit_solution(16185408018769154445)
XLA Ops:
  0.0 2.0 %fill.1.refs_0_ = bf16[2048,128]{1,0:T(8,128)(2,1)S(1)} custom-call(s32[2]{0:T(128)} %bitcast.42, s32[2]{0:T(128)} %bitcast.43, bf16[2048,128]{1,0:T(8,128)(2,1)} %cache_ref.1, bf16[1024,128]{1,0:T(8,128)(2,1)} %fills_ref.1), custom_call_target="tpu_custom_call" | custom-call | tf_op jit(solution)/shard_map/fill/pallas_call | solution.py:57
  2.0 3.0 %collective-permute-start.5 = (bf16[2048,128]{1,0:T(8,128)(2,1)S(1)}, bf16[2048,128]{1,0:T(8,128)(2,1)S(1)}, u32[]{:S(2)}, u32[]{:S(2)}) collective-permute-start(bf16[2048,128]{1,0:T(8,128)(2,1)S(1)} %fill.1.refs_0_), channel_id=1, source_target_pairs={{0,2},{1,5},{2,0},{3,7},{4,6},{5,1},{6,4},{7,3},{8,10},{9,13},{10,... | collective-permute-start | bytes 1572872 | tf_op jit(solution)/shard_map/ppermute | solution.py:349
  5.0 1.6 %collective-permute-start = (bf16[2048,128]{1,0:T(8,128)(2,1)S(1)}, bf16[2048,128]{1,0:T(8,128)(2,1)S(1)}, u32[]{:S(2)}, u32[]{:S(2)}) collective-permute-start(bf16[2048,128]{1,0:T(8,128)(2,1)S(1)} %fill.1.refs_0_), channel_id=1, source_target_pairs={{0,8},{1,9},{2,10},{3,11},{4,12},{5,13},{6,14},{7,15},{8,16},{9,17... | collective-permute-start | bytes 1572872 | tf_op jit(solution)/shard_map/ppermute | solution.py:349
  6.6 1.5 %collective-permute-start.7 = (bf16[2048,128]{1,0:T(8,128)(2,1)S(1)}, bf16[2048,128]{1,0:T(8,128)(2,1)S(1)}, u32[]{:S(2)}, u32[]{:S(2)}) collective-permute-start(bf16[2048,128]{1,0:T(8,128)(2,1)S(1)} %fill.1.refs_0_), channel_id=1, source_target_pairs={{0,4},{1,3},{2,6},{3,1},{4,0},{5,7},{6,2},{7,5},{8,12},{9,11},{10,... | collective-permute-start | bytes 1572872 | tf_op jit(solution)/shard_map/ppermute | solution.py:349
  9.2 1.6 %gather_fusion.1 = s32[48,624]{1,0:T(8,128)S(1)} fusion(s32[32,624]{1,0:T(8,128)} %bitcast.41, s32[1024]{0:T(1024)S(1)} %pad_clamp_fusion), kind=kCustom, calls=%fused_computation.1 | custom fusion | bytes 239808 | tf_op jit(solution)/shard_map/gather | solution.py:380
  10.9 2.4 %pool.6 = (f32[9992,128]{1,0:T(8,128)S(1)}, f32[9992,128]{1,0:T(8,128)S(1)}, f32[9992,128]{1,0:T(8,128)S(1)}, f32[9992,128]{1,0:T(8,128)S(1)}, s32[8,128]{1,0:T(8,128)S(1)}) custom-call(s32[30720]{0:T(1024)S(1)} %reshape.1470.slot_ref, s32[30720]{0:T(1024)S(1)} %reshape.1471.bag_ref, bf16[2048,128]{1,0:T(8,128)(2,1)S(1)} %fill.1.refs_0_), custom_call_target="tpu_custom_call" | custom-call | bytes 3000000 | tf_op jit(solution)/shard_map/pool/pallas_call | solution.py:261
  13.3 2.5 %collective-permute-done.5.refs_0_ = bf16[2048,128]{1,0:T(8,128)(2,1)S(1)} collective-permute-done((bf16[2048,128]{1,0:T(8,128)(2,1)S(1)}, bf16[2048,128]{1,0:T(8,128)(2,1)S(1)}, u32[]{:S(2)}, u32[]{:S(2)}) %collective-permute-start.5) | collective-permute-done | bytes 524320 | tf_op jit(solution)/shard_map/ppermute | solution.py:349
  15.9 4.4 %collective-permute-done.refs_4_ = bf16[2048,128]{1,0:T(8,128)(2,1)S(1)} collective-permute-done((bf16[2048,128]{1,0:T(8,128)(2,1)S(1)}, bf16[2048,128]{1,0:T(8,128)(2,1)S(1)}, u32[]{:S(2)}, u32[]{:S(2)}) %collective-permute-start) | collective-permute-done | bytes 524320 | tf_op jit(solution)/shard_map/ppermute | solution.py:349
  20.3 1.5 %collective-permute-start.4 = (bf16[2048,128]{1,0:T(8,128)(2,1)S(1)}, bf16[2048,128]{1,0:T(8,128)(2,1)S(1)}, u32[]{:S(2)}, u32[]{:S(2)}) collective-permute-start(bf16[2048,128]{1,0:T(8,128)(2,1)S(1)} %collective-permute-done.refs_4_), channel_id=1, source_target_pairs={{0,2},{1,5},{2,0},{3,7},{4,6},{5,1},{6,4},{7,3},{8,10},{9,13},{10,... | collective-permute-start | bytes 1572872 | tf_op jit(solution)/shard_map/ppermute | solution.py:349
  23.9 5.9 %pool.7 = (f32[9992,128]{1,0:T(8,128)S(1)}, f32[9992,128]{1,0:T(8,128)S(1)}, f32[9992,128]{1,0:T(8,128)S(1)}, f32[9992,128]{1,0:T(8,128)S(1)}, s32[8,128]{1,0:T(8,128)S(1)}) custom-call(s32[30720]{0:T(1024)S(1)} %reshape.1470.slot_ref, s32[30720]{0:T(1024)S(1)} %reshape.1471.bag_ref, ...), custom_call_target="tpu_custom_call", output_to_operand_aliasing={{0}: (8, {}), {1}: (9, {}), {2}: (10, {}), {3}: (11, {})} | custom-call | bytes 18000000 | tf_op jit(solution)/shard_map/pool/pallas_call | solution.py:261
  29.7 5.3 %collective-permute-done.4.refs_0_ = bf16[2048,128]{1,0:T(8,128)(2,1)S(1)} collective-permute-done((bf16[2048,128]{1,0:T(8,128)(2,1)S(1)}, bf16[2048,128]{1,0:T(8,128)(2,1)S(1)}, u32[]{:S(2)}, u32[]{:S(2)}) %collective-permute-start.4) | collective-permute-done | bytes 524320 | tf_op jit(solution)/shard_map/ppermute | solution.py:349
  35.6 2.3 %collective-permute-done.1.refs_6_ = bf16[2048,128]{1,0:T(8,128)(2,1)S(1)} collective-permute-done((bf16[2048,128]{1,0:T(8,128)(2,1)S(1)}, bf16[2048,128]{1,0:T(8,128)(2,1)S(1)}, u32[]{:S(2)}, u32[]{:S(2)}) %collective-permute-start.1) | collective-permute-done | bytes 524320 | tf_op jit(solution)/shard_map/ppermute | solution.py:349
  37.8 2.4 %collective-permute-done.16.refs_2_ = bf16[2048,128]{1,0:T(8,128)(2,1)S(1)} collective-permute-done((bf16[2048,128]{1,0:T(8,128)(2,1)S(1)}, bf16[2048,128]{1,0:T(8,128)(2,1)S(1)}, u32[]{:S(2)}, u32[]{:S(2)}) %collective-permute-start.16) | collective-permute-done | bytes 524320 | tf_op jit(solution)/shard_map/ppermute | solution.py:349
  43.8 8.2 %pool.8 = (f32[9992,128]{1,0:T(8,128)S(1)}, f32[9992,128]{1,0:T(8,128)S(1)}, f32[9992,128]{1,0:T(8,128)S(1)}, f32[9992,128]{1,0:T(8,128)S(1)}, s32[8,128]{1,0:T(8,128)S(1)}) custom-call(s32[30720]{0:T(1024)S(1)} %reshape.1470.slot_ref, s32[30720]{0:T(1024)S(1)} %reshape.1471.bag_ref, ...), custom_call_target="tpu_custom_call", output_to_operand_aliasing={{0}: (10, {}), {1}: (11, {}), {2}: (12, {}), {3}: (13, {})} | custom-call | bytes 24000000 | tf_op jit(solution)/shard_map/pool/pallas_call | solution.py:261
  52.0 2.9 %collective-permute-done.14.refs_0_ = bf16[2048,128]{1,0:T(8,128)(2,1)S(1)} collective-permute-done((bf16[2048,128]{1,0:T(8,128)(2,1)S(1)}, bf16[2048,128]{1,0:T(8,128)(2,1)S(1)}, u32[]{:S(2)}, u32[]{:S(2)}) %collective-permute-start.14) | collective-permute-done | bytes 524320 | tf_op jit(solution)/shard_map/ppermute | solution.py:349
  55.4 2.1 %collective-permute-done.2.refs_6_ = bf16[2048,128]{1,0:T(8,128)(2,1)S(1)} collective-permute-done((bf16[2048,128]{1,0:T(8,128)(2,1)S(1)}, bf16[2048,128]{1,0:T(8,128)(2,1)S(1)}, u32[]{:S(2)}, u32[]{:S(2)}) %collective-permute-start.2) | collective-permute-done | bytes 524320 | tf_op jit(solution)/shard_map/ppermute | solution.py:349
  57.6 2.2 %collective-permute-done.12.refs_2_ = bf16[2048,128]{1,0:T(8,128)(2,1)S(1)} collective-permute-done((bf16[2048,128]{1,0:T(8,128)(2,1)S(1)}, bf16[2048,128]{1,0:T(8,128)(2,1)S(1)}, u32[]{:S(2)}, u32[]{:S(2)}) %collective-permute-start.12) | collective-permute-done | bytes 524320 | tf_op jit(solution)/shard_map/ppermute | solution.py:349
  60.2 1.5 %collective-permute-start.3 = (bf16[2048,128]{1,0:T(8,128)(2,1)S(1)}, bf16[2048,128]{1,0:T(8,128)(2,1)S(1)}, u32[]{:S(2)}, u32[]{:S(2)}) collective-permute-start(bf16[2048,128]{1,0:T(8,128)(2,1)S(1)} %collective-permute-done.2.refs_6_), channel_id=1, source_target_pairs={{0,2},{1,5},{2,0},{3,7},{4,6},{5,1},{6,4},{7,3},{8,10},{9,13},{10,... | collective-permute-start | bytes 1572872 | tf_op jit(solution)/shard_map/ppermute | solution.py:349
  62.7 8.1 %pool.9 = (f32[9992,128]{1,0:T(8,128)S(1)}, f32[9992,128]{1,0:T(8,128)S(1)}, f32[9992,128]{1,0:T(8,128)S(1)}, f32[9992,128]{1,0:T(8,128)S(1)}, s32[8,128]{1,0:T(8,128)}) custom-call(s32[30720]{0:T(1024)S(1)} %reshape.1470.slot_ref, s32[30720]{0:T(1024)S(1)} %reshape.1471.bag_ref, ...), custom_call_target="tpu_custom_call", output_to_operand_aliasing={{0}: (10, {}), {1}: (11, {}), {2}: (12, {}), {3}: (13, {})} | custom-call | bytes 24000000 | tf_op jit(solution)/shard_map/pool/pallas_call | solution.py:261
  70.9 2.2 %pool.10 = (f32[9992,128]{1,0:T(8,128)S(1)}, f32[9992,128]{1,0:T(8,128)S(1)}, f32[9992,128]{1,0:T(8,128)S(1)}, f32[9992,128]{1,0:T(8,128)S(1)}, s32[8,128]{1,0:T(8,128)S(1)}) custom-call(s32[30720]{0:T(1024)S(1)} %reshape.1470.slot_ref, s32[30720]{0:T(1024)S(1)} %reshape.1471.bag_ref, ...), custom_call_target="tpu_custom_call", output_to_operand_aliasing={{0}: (3, {}), {1}: (4, {}), {2}: (5, {}), {3}: (6, {})} | custom-call | bytes 3000000 | tf_op jit(solution)/shard_map/pool/pallas_call | solution.py:261
  73.1 2.8 %collective-permute-done.11.refs_1_ = bf16[2048,128]{1,0:T(8,128)(2,1)S(1)} collective-permute-done((bf16[2048,128]{1,0:T(8,128)(2,1)S(1)}, bf16[2048,128]{1,0:T(8,128)(2,1)S(1)}, u32[]{:S(2)}, u32[]{:S(2)}) %collective-permute-start.11) | collective-permute-done | bytes 524320 | tf_op jit(solution)/shard_map/ppermute | solution.py:349
  79.3 5.7 %pool.11 = (f32[9992,128]{1,0:T(8,128)S(1)}, f32[9992,128]{1,0:T(8,128)S(1)}, f32[9992,128]{1,0:T(8,128)S(1)}, f32[9992,128]{1,0:T(8,128)S(1)}, s32[8,128]{1,0:T(8,128)S(1)}) custom-call(s32[30720]{0:T(1024)S(1)} %reshape.1470.slot_ref, s32[30720]{0:T(1024)S(1)} %reshape.1471.bag_ref, ...), custom_call_target="tpu_custom_call", output_to_operand_aliasing={{0}: (8, {}), {1}: (9, {}), {2}: (10, {}), {3}: (11, {})} | custom-call | bytes 18000000 | tf_op jit(solution)/shard_map/pool/pallas_call | solution.py:261
  85.7 1.9 %collective-permute-done.30.refs_1_ = bf16[2048,128]{1,0:T(8,128)(2,1)S(1)} collective-permute-done((bf16[2048,128]{1,0:T(8,128)(2,1)S(1)}, bf16[2048,128]{1,0:T(8,128)(2,1)S(1)}, u32[]{:S(2)}, u32[]{:S(2)}) %collective-permute-start.30) | collective-permute-done | bytes 524320 | tf_op jit(solution)/shard_map/ppermute | solution.py:349
  87.6 9.5 %finish.1 = (f32[384]{0:T(512)}, f32[9992,128]{1,0:T(8,128)S(1)}, f32[9992,128]{1,0:T(8,128)S(1)}, f32[9992,128]{1,0:T(8,128)S(1)}, f32[9992,128]{1,0:T(8,128)S(1)}) custom-call(s32[30720]{0:T(1024)S(1)} %reshape.1470.slot_ref, s32[30720]{0:T(1024)S(1)} %reshape.1471.bag_ref, ...), custom_call_target="tpu_custom_call", output_to_operand_aliasing={{1}: (4, {}), {2}: (5, {}), {3}: (6, {}), {4}: (7, {})} | custom-call | tf_op jit(solution)/shard_map/finish/pallas_call | solution.py:300
  (74 shorter events, 13.5 us)
Async XLA Ops:
  2.0 13.9 %collective-permute-start.5 = (bf16[2048,128]{1,0:T(8,128)(2,1)S(1)}, bf16[2048,128]{1,0:T(8,128)(2,1)S(1)}, u32[]{:S(2)}, u32[]{:S(2)}) collective-permute-start(bf16[2048,128]{1,0:T(8,128)(2,1)S(1)} %fill.1.refs_0_), channel_id=1, source_target_pairs={{0,2},{1,5},{2,0},{3,7},{4,6},{5,1},{6,4},{7,3},{8,10},{9,13},{10,... | collective-permute-start | bytes 1572872 | tf_op jit(solution)/shard_map/ppermute | solution.py:349
  5.0 15.3 %collective-permute-start = (bf16[2048,128]{1,0:T(8,128)(2,1)S(1)}, bf16[2048,128]{1,0:T(8,128)(2,1)S(1)}, u32[]{:S(2)}, u32[]{:S(2)}) collective-permute-start(bf16[2048,128]{1,0:T(8,128)(2,1)S(1)} %fill.1.refs_0_), channel_id=1, source_target_pairs={{0,8},{1,9},{2,10},{3,11},{4,12},{5,13},{6,14},{7,15},{8,16},{9,17... | collective-permute-start | bytes 1572872 | tf_op jit(solution)/shard_map/ppermute | solution.py:349
  6.6 15.2 %collective-permute-start.7 = (bf16[2048,128]{1,0:T(8,128)(2,1)S(1)}, bf16[2048,128]{1,0:T(8,128)(2,1)S(1)}, u32[]{:S(2)}, u32[]{:S(2)}) collective-permute-start(bf16[2048,128]{1,0:T(8,128)(2,1)S(1)} %fill.1.refs_0_), channel_id=1, source_target_pairs={{0,4},{1,3},{2,6},{3,1},{4,0},{5,7},{6,2},{7,5},{8,12},{9,11},{10,... | collective-permute-start | bytes 1572872 | tf_op jit(solution)/shard_map/ppermute | solution.py:349
  8.1 14.2 %collective-permute-start.8 = (bf16[2048,128]{1,0:T(8,128)(2,1)S(1)}, bf16[2048,128]{1,0:T(8,128)(2,1)S(1)}, u32[]{:S(2)}, u32[]{:S(2)}) collective-permute-start(bf16[2048,128]{1,0:T(8,128)(2,1)S(1)} %fill.1.refs_0_), channel_id=1, source_target_pairs={{0,1},{1,0},{2,3},{3,2},{4,5},{5,4},{6,7},{7,6},{8,9},{9,8},{10,11... | collective-permute-start | bytes 1572872 | tf_op jit(solution)/shard_map/ppermute | solution.py:349
  15.8 7.3 %collective-permute-start.6 = (bf16[2048,128]{1,0:T(8,128)(2,1)S(1)}, bf16[2048,128]{1,0:T(8,128)(2,1)S(1)}, u32[]{:S(2)}, u32[]{:S(2)}) collective-permute-start(bf16[2048,128]{1,0:T(8,128)(2,1)S(1)} %gate.5.refs_0_), channel_id=1, source_target_pairs={{0,1},{1,0},{2,3},{3,2},{4,5},{5,4},{6,7},{7,6},{8,9},{9,8},{10,11... | collective-permute-start | bytes 1572872 | tf_op jit(solution)/shard_map/ppermute | solution.py:349
  20.3 14.8 %collective-permute-start.4 = (bf16[2048,128]{1,0:T(8,128)(2,1)S(1)}, bf16[2048,128]{1,0:T(8,128)(2,1)S(1)}, u32[]{:S(2)}, u32[]{:S(2)}) collective-permute-start(bf16[2048,128]{1,0:T(8,128)(2,1)S(1)} %collective-permute-done.refs_4_), channel_id=1, source_target_pairs={{0,2},{1,5},{2,0},{3,7},{4,6},{5,1},{6,4},{7,3},{8,10},{9,13},{10,... | collective-permute-start | bytes 1572872 | tf_op jit(solution)/shard_map/ppermute | solution.py:349
  21.8 13.3 %collective-permute-start.18 = (bf16[2048,128]{1,0:T(8,128)(2,1)S(1)}, bf16[2048,128]{1,0:T(8,128)(2,1)S(1)}, u32[]{:S(2)}, u32[]{:S(2)}) collective-permute-start(bf16[2048,128]{1,0:T(8,128)(2,1)S(1)} %gate.5.refs_0_), channel_id=1, source_target_pairs={{0,4},{1,3},{2,6},{3,1},{4,0},{5,7},{6,2},{7,5},{8,12},{9,11},{10,... | collective-permute-start | bytes 1572872 | tf_op jit(solution)/shard_map/ppermute | solution.py:349
  22.3 15.6 %collective-permute-start.1 = (bf16[2048,128]{1,0:T(8,128)(2,1)S(1)}, bf16[2048,128]{1,0:T(8,128)(2,1)S(1)}, u32[]{:S(2)}, u32[]{:S(2)}) collective-permute-start(bf16[2048,128]{1,0:T(8,128)(2,1)S(1)} %collective-permute-done.refs_4_), channel_id=1, source_target_pairs={{0,8},{1,9},{2,10},{3,11},{4,12},{5,13},{6,14},{7,15},{8,16},{9,17... | collective-permute-start | bytes 1572872 | tf_op jit(solution)/shard_map/ppermute | solution.py:349
  23.1 17.1 %collective-permute-start.16 = (bf16[2048,128]{1,0:T(8,128)(2,1)S(1)}, bf16[2048,128]{1,0:T(8,128)(2,1)S(1)}, u32[]{:S(2)}, u32[]{:S(2)}) collective-permute-start(bf16[2048,128]{1,0:T(8,128)(2,1)S(1)} %collective-permute-done.refs_4_), channel_id=1, source_target_pairs={{0,4},{1,3},{2,6},{3,1},{4,0},{5,7},{6,2},{7,5},{8,12},{9,11},{10,... | collective-permute-start | bytes 1572872 | tf_op jit(solution)/shard_map/ppermute | solution.py:349
  23.9 17.8 %collective-permute-start.17 = (bf16[2048,128]{1,0:T(8,128)(2,1)S(1)}, bf16[2048,128]{1,0:T(8,128)(2,1)S(1)}, u32[]{:S(2)}, u32[]{:S(2)}) collective-permute-start(bf16[2048,128]{1,0:T(8,128)(2,1)S(1)} %collective-permute-done.7.refs_2_), channel_id=1, source_target_pairs={{0,1},{1,0},{2,3},{3,2},{4,5},{5,4},{6,7},{7,6},{8,9},{9,8},{10,11... | collective-permute-start | bytes 1572872 | tf_op jit(solution)/shard_map/ppermute | solution.py:349
  35.1 7.2 %collective-permute-start.15 = (bf16[2048,128]{1,0:T(8,128)(2,1)S(1)}, bf16[2048,128]{1,0:T(8,128)(2,1)S(1)}, u32[]{:S(2)}, u32[]{:S(2)}) collective-permute-start(bf16[2048,128]{1,0:T(8,128)(2,1)S(1)} %gate.6.refs_0_), channel_id=1, source_target_pairs={{0,1},{1,0},{2,3},{3,2},{4,5},{5,4},{6,7},{7,6},{8,9},{9,8},{10,11... | collective-permute-start | bytes 1572872 | tf_op jit(solution)/shard_map/ppermute | solution.py:349
  35.1 7.5 %collective-permute-start.19 = (bf16[2048,128]{1,0:T(8,128)(2,1)S(1)}, bf16[2048,128]{1,0:T(8,128)(2,1)S(1)}, u32[]{:S(2)}, u32[]{:S(2)}) collective-permute-start(bf16[2048,128]{1,0:T(8,128)(2,1)S(1)} %collective-permute-done.18.refs_4_), channel_id=1, source_target_pairs={{0,1},{1,0},{2,3},{3,2},{4,5},{5,4},{6,7},{7,6},{8,9},{9,8},{10,11... | collective-permute-start | bytes 1572872 | tf_op jit(solution)/shard_map/ppermute | solution.py:349
  37.8 6.0 %collective-permute-start.20 = (bf16[2048,128]{1,0:T(8,128)(2,1)S(1)}, bf16[2048,128]{1,0:T(8,128)(2,1)S(1)}, u32[]{:S(2)}, u32[]{:S(2)}) collective-permute-start(bf16[2048,128]{1,0:T(8,128)(2,1)S(1)} %collective-permute-done.1.refs_6_), channel_id=1, source_target_pairs={{0,1},{1,0},{2,3},{3,2},{4,5},{5,4},{6,7},{7,6},{8,9},{9,8},{10,11... | collective-permute-start | bytes 1572872 | tf_op jit(solution)/shard_map/ppermute | solution.py:349
  40.2 14.7 %collective-permute-start.14 = (bf16[2048,128]{1,0:T(8,128)(2,1)S(1)}, bf16[2048,128]{1,0:T(8,128)(2,1)S(1)}, u32[]{:S(2)}, u32[]{:S(2)}) collective-permute-start(bf16[2048,128]{1,0:T(8,128)(2,1)S(1)} %collective-permute-done.1.refs_6_), channel_id=1, source_target_pairs={{0,2},{1,5},{2,0},{3,7},{4,6},{5,1},{6,4},{7,3},{8,10},{9,13},{10,... | collective-permute-start | bytes 1572872 | tf_op jit(solution)/shard_map/ppermute | solution.py:349
  41.7 13.2 %collective-permute-start.10 = (bf16[2048,128]{1,0:T(8,128)(2,1)S(1)}, bf16[2048,128]{1,0:T(8,128)(2,1)S(1)}, u32[]{:S(2)}, u32[]{:S(2)}) collective-permute-start(bf16[2048,128]{1,0:T(8,128)(2,1)S(1)} %gate.6.refs_0_), channel_id=1, source_target_pairs={{0,4},{1,3},{2,6},{3,1},{4,0},{5,7},{6,2},{7,5},{8,12},{9,11},{10,... | collective-permute-start | bytes 1572872 | tf_op jit(solution)/shard_map/ppermute | solution.py:349
  42.2 15.4 %collective-permute-start.2 = (bf16[2048,128]{1,0:T(8,128)(2,1)S(1)}, bf16[2048,128]{1,0:T(8,128)(2,1)S(1)}, u32[]{:S(2)}, u32[]{:S(2)}) collective-permute-start(bf16[2048,128]{1,0:T(8,128)(2,1)S(1)} %collective-permute-done.1.refs_6_), channel_id=1, source_target_pairs={{0,8},{1,9},{2,10},{3,11},{4,12},{5,13},{6,14},{7,15},{8,16},{9,17... | collective-permute-start | bytes 1572872 | tf_op jit(solution)/shard_map/ppermute | solution.py:349
  42.6 17.2 %collective-permute-start.12 = (bf16[2048,128]{1,0:T(8,128)(2,1)S(1)}, bf16[2048,128]{1,0:T(8,128)(2,1)S(1)}, u32[]{:S(2)}, u32[]{:S(2)}) collective-permute-start(bf16[2048,128]{1,0:T(8,128)(2,1)S(1)} %collective-permute-done.1.refs_6_), channel_id=1, source_target_pairs={{0,4},{1,3},{2,6},{3,1},{4,0},{5,7},{6,2},{7,5},{8,12},{9,11},{10,... | collective-permute-start | bytes 1572872 | tf_op jit(solution)/shard_map/ppermute | solution.py:349
  43.8 16.2 %collective-permute-start.22 = (bf16[2048,128]{1,0:T(8,128)(2,1)S(1)}, bf16[2048,128]{1,0:T(8,128)(2,1)S(1)}, u32[]{:S(2)}, u32[]{:S(2)}) collective-permute-start(bf16[2048,128]{1,0:T(8,128)(2,1)S(1)} %collective-permute-done.16.refs_2_), channel_id=1, source_target_pairs={{0,1},{1,0},{2,3},{3,2},{4,5},{5,4},{6,7},{7,6},{8,9},{9,8},{10,11... | collective-permute-start | bytes 1572872 | tf_op jit(solution)/shard_map/ppermute | solution.py:349
  54.9 6.7 %collective-permute-start.23 = (bf16[2048,128]{1,0:T(8,128)(2,1)S(1)}, bf16[2048,128]{1,0:T(8,128)(2,1)S(1)}, u32[]{:S(2)}, u32[]{:S(2)}) collective-permute-start(bf16[2048,128]{1,0:T(8,128)(2,1)S(1)} %collective-permute-done.10.refs_4_), channel_id=1, source_target_pairs={{0,1},{1,0},{2,3},{3,2},{4,5},{5,4},{6,7},{7,6},{8,9},{9,8},{10,11... | collective-permute-start | bytes 1572872 | tf_op jit(solution)/shard_map/ppermute | solution.py:349
  59.8 11.1 %collective-permute-start.13 = (bf16[2048,128]{1,0:T(8,128)(2,1)S(1)}, bf16[2048,128]{1,0:T(8,128)(2,1)S(1)}, u32[]{:S(2)}, u32[]{:S(2)}) collective-permute-start(bf16[2048,128]{1,0:T(8,128)(2,1)S(1)} %collective-permute-done.12.refs_2_), channel_id=1, source_target_pairs={{0,1},{1,0},{2,3},{3,2},{4,5},{5,4},{6,7},{7,6},{8,9},{9,8},{10,11... | collective-permute-start | bytes 1572872 | tf_op jit(solution)/shard_map/ppermute | solution.py:349
  60.0 15.9 %collective-permute-start.11 = (bf16[2048,128]{1,0:T(8,128)(2,1)S(1)}, bf16[2048,128]{1,0:T(8,128)(2,1)S(1)}, u32[]{:S(2)}, u32[]{:S(2)}) collective-permute-start(bf16[2048,128]{1,0:T(8,128)(2,1)S(1)} %collective-permute-done.10.refs_4_), channel_id=1, source_target_pairs={{0,8},{1,9},{2,10},{3,11},{4,12},{5,13},{6,14},{7,15},{8,16},{9,17... | collective-permute-start | bytes 1572872 | tf_op jit(solution)/shard_map/ppermute | solution.py:349
  60.2 15.7 %collective-permute-start.3 = (bf16[2048,128]{1,0:T(8,128)(2,1)S(1)}, bf16[2048,128]{1,0:T(8,128)(2,1)S(1)}, u32[]{:S(2)}, u32[]{:S(2)}) collective-permute-start(bf16[2048,128]{1,0:T(8,128)(2,1)S(1)} %collective-permute-done.2.refs_6_), channel_id=1, source_target_pairs={{0,2},{1,5},{2,0},{3,7},{4,6},{5,1},{6,4},{7,3},{8,10},{9,13},{10,... | collective-permute-start | bytes 1572872 | tf_op jit(solution)/shard_map/ppermute | solution.py:349
  61.7 14.8 %collective-permute-start.27 = (bf16[2048,128]{1,0:T(8,128)(2,1)S(1)}, bf16[2048,128]{1,0:T(8,128)(2,1)S(1)}, u32[]{:S(2)}, u32[]{:S(2)}) collective-permute-start(bf16[2048,128]{1,0:T(8,128)(2,1)S(1)} %collective-permute-done.2.refs_6_), channel_id=1, source_target_pairs={{0,4},{1,3},{2,6},{3,1},{4,0},{5,7},{6,2},{7,5},{8,12},{9,11},{10,... | collective-permute-start | bytes 1572872 | tf_op jit(solution)/shard_map/ppermute | solution.py:349
  76.5 9.2 %collective-permute-start.25 = (bf16[2048,128]{1,0:T(8,128)(2,1)S(1)}, bf16[2048,128]{1,0:T(8,128)(2,1)S(1)}, u32[]{:S(2)}, u32[]{:S(2)}) collective-permute-start(bf16[2048,128]{1,0:T(8,128)(2,1)S(1)} %get-tuple-element.57.refs_0_), channel_id=1, source_target_pairs={{0,4},{1,3},{2,6},{3,1},{4,0},{5,7},{6,2},{7,5},{8,12},{9,11},{10,... | collective-permute-start | bytes 1572872 | tf_op jit(solution)/shard_map/ppermute | solution.py:349
  (12 other events, 64.7 us)

commit v9 on v8

--- a/solution.py
+++ b/solution.py
@@ -135,10 +135,16 @@
         pass
 
 
+def first_lane(i):
+    return 8 * (i + 1) // LANES * LANES
+
+
 def interact(sums, dense_ref, masked, queries):
-    lane = lax.broadcasted_iota(jnp.int32, (8, 256), 1)
-    row = lax.broadcasted_iota(jnp.int32, (8, 256), 0)
-    own_query = (lane & 7) == row
+    own_query = {
+        low: (lax.broadcasted_iota(jnp.int32, (8, 256 - low), 1) & 7)
+        == lax.broadcasted_iota(jnp.int32, (8, 256 - low), 0)
+        for low in (0, LANES)
+    }
 
     def sixteen_queries(step, _):
         dense = dense_ref[pl.ds(pl.multiple_of(step * 16, 16), 16), :].astype(jnp.float32)
@@ -160,10 +166,11 @@
                 )
             )
         for i in range(F):
+            low = first_lane(i)
             pair = [
-                jnp.where(own_query, products[8 * i : 8 * i + 8, :], 0.0) for products in halves
+                jnp.where(own_query[low], products[8 * i : 8 * i + 8, low:], 0.0) for products in halves
             ]
-            masked[i, pl.ds(pl.multiple_of(step * 16, 16), 16), :] = jnp.concatenate(
+            masked[i, pl.ds(pl.multiple_of(step * 16, 16), 16), low:] = jnp.concatenate(
                 pair, axis=0
             ).astype(jnp.bfloat16)
         return 0
@@ -180,7 +187,8 @@
     first = 0
     for i in range(F):
         length = F - i
-        picked = jnp.dot(masked[i], pick, preferred_element_type=jnp.float32)
+        low = first_lane(i)
+        picked = jnp.dot(masked[i, :, low:], pick[low:], preferred_element_type=jnp.float32)
         shift = (first - (i + 1)) % LANES
         if shift:
             picked = pltpu.roll(picked, shift, 1)

time: 97.4 us -> 97.2 us (level)
  Pallas kernels: 44 us -> 41.6 us
  waiting for transfers between devices: 31.7 us -> 33.7 us
    ppermute x31, waiting for transfers between devices: 31.7 us -> 33.7 us  [hop(): return lambda array: lax.ppermute(array, 'cache', pairs)]
    pallas_call x6, Pallas kernels: 32.5 us -> 30.5 us  [pool(): pl.pallas_call(functools.partial(pool_kernel, first, rows, is_first), out...]
  transfers between devices with their start and end apart: 31 -> 31, of which waited for: 14 -> 14; matrix products, arithmetic and copies ran while one was open for 3% -> 3% of each run, Pallas kernels for 33% -> 31%
where the time goes in v9:
time: 97.2 us; the launch traced here: 96.9 us
  Pallas kernels  41.6 us (43%)
  waiting for transfers between devices  33.7 us (35%)
  starting transfers between devices  18.5 us (19%)
  local copies, waits for them, and re-layouts  2.41 us (2%)
    ppermute x31, waiting for transfers between devices, hop(): return lambda array: lax.ppermute(array, 'cache', pairs)  33.7 us
    pallas_call x6, Pallas kernels, pool(): pl.pallas_call(functools.partial(pool_kernel, first, rows, is_first), out...  30.5 us
    ppermute x31, starting transfers between devices, hop(): return lambda array: lax.ppermute(array, 'cache', pairs)  18.5 us
    pallas_call x1, Pallas kernels, finish(): pl.pallas_call(functools.partial(final_kernel, first, n_shards, head is n...  9.16 us
    pallas_call x1, Pallas kernels, fill(): pl.pallas_call(fill_kernel, out_shape=pltpu.VMEM(cache_rows.shape, cache_...  1.97 us
  transfers between devices with their start and end apart: 31, of which 14 were waited for; matrix products, arithmetic and copies ran while one was open for 3% of the time, Pallas kernels for 31%

profile of v9, /device:TPU:0, one launch (start us, length us, event | category | flops | bytes accessed | tf_op | source)
XLA Modules:
  0.0 96.9 jit_solution(7326248396278807131)
XLA Ops:
  0.0 2.0 %fill.1.refs_0_ = bf16[2048,128]{1,0:T(8,128)(2,1)S(1)} custom-call(s32[2]{0:T(128)} %bitcast.42, s32[2]{0:T(128)} %bitcast.43, bf16[2048,128]{1,0:T(8,128)(2,1)} %cache_ref.1, bf16[1024,128]{1,0:T(8,128)(2,1)} %fills_ref.1), custom_call_target="tpu_custom_call" | custom-call | tf_op jit(solution)/shard_map/fill/pallas_call | solution.py:57
  2.0 3.0 %collective-permute-start.5 = (bf16[2048,128]{1,0:T(8,128)(2,1)S(1)}, bf16[2048,128]{1,0:T(8,128)(2,1)S(1)}, u32[]{:S(2)}, u32[]{:S(2)}) collective-permute-start(bf16[2048,128]{1,0:T(8,128)(2,1)S(1)} %fill.1.refs_0_), channel_id=1, source_target_pairs={{0,2},{1,5},{2,0},{3,7},{4,6},{5,1},{6,4},{7,3},{8,10},{9,13},{10,... | collective-permute-start | bytes 1572872 | tf_op jit(solution)/shard_map/ppermute | solution.py:357
  5.0 1.6 %collective-permute-start = (bf16[2048,128]{1,0:T(8,128)(2,1)S(1)}, bf16[2048,128]{1,0:T(8,128)(2,1)S(1)}, u32[]{:S(2)}, u32[]{:S(2)}) collective-permute-start(bf16[2048,128]{1,0:T(8,128)(2,1)S(1)} %fill.1.refs_0_), channel_id=1, source_target_pairs={{0,8},{1,9},{2,10},{3,11},{4,12},{5,13},{6,14},{7,15},{8,16},{9,17... | collective-permute-start | bytes 1572872 | tf_op jit(solution)/shard_map/ppermute | solution.py:357
  6.6 1.5 %collective-permute-start.7 = (bf16[2048,128]{1,0:T(8,128)(2,1)S(1)}, bf16[2048,128]{1,0:T(8,128)(2,1)S(1)}, u32[]{:S(2)}, u32[]{:S(2)}) collective-permute-start(bf16[2048,128]{1,0:T(8,128)(2,1)S(1)} %fill.1.refs_0_), channel_id=1, source_target_pairs={{0,4},{1,3},{2,6},{3,1},{4,0},{5,7},{6,2},{7,5},{8,12},{9,11},{10,... | collective-permute-start | bytes 1572872 | tf_op jit(solution)/shard_map/ppermute | solution.py:357
  9.2 1.6 %gather_fusion.1 = s32[48,624]{1,0:T(8,128)S(1)} fusion(s32[32,624]{1,0:T(8,128)} %bitcast.41, s32[1024]{0:T(1024)S(1)} %pad_clamp_fusion), kind=kCustom, calls=%fused_computation.1 | custom fusion | bytes 239808 | tf_op jit(solution)/shard_map/gather | solution.py:388
  10.9 2.4 %pool.6 = (f32[9992,128]{1,0:T(8,128)S(1)}, f32[9992,128]{1,0:T(8,128)S(1)}, f32[9992,128]{1,0:T(8,128)S(1)}, f32[9992,128]{1,0:T(8,128)S(1)}, s32[8,128]{1,0:T(8,128)S(1)}) custom-call(s32[30720]{0:T(1024)S(1)} %reshape.1470.slot_ref, s32[30720]{0:T(1024)S(1)} %reshape.1471.bag_ref, bf16[2048,128]{1,0:T(8,128)(2,1)S(1)} %fill.1.refs_0_), custom_call_target="tpu_custom_call" | custom-call | bytes 3000000 | tf_op jit(solution)/shard_map/pool/pallas_call | solution.py:269
  13.3 2.5 %collective-permute-done.5.refs_0_ = bf16[2048,128]{1,0:T(8,128)(2,1)S(1)} collective-permute-done((bf16[2048,128]{1,0:T(8,128)(2,1)S(1)}, bf16[2048,128]{1,0:T(8,128)(2,1)S(1)}, u32[]{:S(2)}, u32[]{:S(2)}) %collective-permute-start.5) | collective-permute-done | bytes 524320 | tf_op jit(solution)/shard_map/ppermute | solution.py:357
  15.9 4.4 %collective-permute-done.refs_4_ = bf16[2048,128]{1,0:T(8,128)(2,1)S(1)} collective-permute-done((bf16[2048,128]{1,0:T(8,128)(2,1)S(1)}, bf16[2048,128]{1,0:T(8,128)(2,1)S(1)}, u32[]{:S(2)}, u32[]{:S(2)}) %collective-permute-start) | collective-permute-done | bytes 524320 | tf_op jit(solution)/shard_map/ppermute | solution.py:357
  20.3 1.5 %collective-permute-start.4 = (bf16[2048,128]{1,0:T(8,128)(2,1)S(1)}, bf16[2048,128]{1,0:T(8,128)(2,1)S(1)}, u32[]{:S(2)}, u32[]{:S(2)}) collective-permute-start(bf16[2048,128]{1,0:T(8,128)(2,1)S(1)} %collective-permute-done.refs_4_), channel_id=1, source_target_pairs={{0,2},{1,5},{2,0},{3,7},{4,6},{5,1},{6,4},{7,3},{8,10},{9,13},{10,... | collective-permute-start | bytes 1572872 | tf_op jit(solution)/shard_map/ppermute | solution.py:357
  23.9 5.8 %pool.7 = (f32[9992,128]{1,0:T(8,128)S(1)}, f32[9992,128]{1,0:T(8,128)S(1)}, f32[9992,128]{1,0:T(8,128)S(1)}, f32[9992,128]{1,0:T(8,128)S(1)}, s32[8,128]{1,0:T(8,128)S(1)}) custom-call(s32[30720]{0:T(1024)S(1)} %reshape.1470.slot_ref, s32[30720]{0:T(1024)S(1)} %reshape.1471.bag_ref, ...), custom_call_target="tpu_custom_call", output_to_operand_aliasing={{0}: (8, {}), {1}: (9, {}), {2}: (10, {}), {3}: (11, {})} | custom-call | bytes 18000000 | tf_op jit(solution)/shard_map/pool/pallas_call | solution.py:269
  29.7 5.4 %collective-permute-done.4.refs_0_ = bf16[2048,128]{1,0:T(8,128)(2,1)S(1)} collective-permute-done((bf16[2048,128]{1,0:T(8,128)(2,1)S(1)}, bf16[2048,128]{1,0:T(8,128)(2,1)S(1)}, u32[]{:S(2)}, u32[]{:S(2)}) %collective-permute-start.4) | collective-permute-done | bytes 524320 | tf_op jit(solution)/shard_map/ppermute | solution.py:357
  35.6 2.3 %collective-permute-done.1.refs_6_ = bf16[2048,128]{1,0:T(8,128)(2,1)S(1)} collective-permute-done((bf16[2048,128]{1,0:T(8,128)(2,1)S(1)}, bf16[2048,128]{1,0:T(8,128)(2,1)S(1)}, u32[]{:S(2)}, u32[]{:S(2)}) %collective-permute-start.1) | collective-permute-done | bytes 524320 | tf_op jit(solution)/shard_map/ppermute | solution.py:357
  37.8 2.4 %collective-permute-done.16.refs_2_ = bf16[2048,128]{1,0:T(8,128)(2,1)S(1)} collective-permute-done((bf16[2048,128]{1,0:T(8,128)(2,1)S(1)}, bf16[2048,128]{1,0:T(8,128)(2,1)S(1)}, u32[]{:S(2)}, u32[]{:S(2)}) %collective-permute-start.16) | collective-permute-done | bytes 524320 | tf_op jit(solution)/shard_map/ppermute | solution.py:357
  43.8 7.4 %pool.8 = (f32[9992,128]{1,0:T(8,128)S(1)}, f32[9992,128]{1,0:T(8,128)S(1)}, f32[9992,128]{1,0:T(8,128)S(1)}, f32[9992,128]{1,0:T(8,128)S(1)}, s32[8,128]{1,0:T(8,128)S(1)}) custom-call(s32[30720]{0:T(1024)S(1)} %reshape.1470.slot_ref, s32[30720]{0:T(1024)S(1)} %reshape.1471.bag_ref, ...), custom_call_target="tpu_custom_call", output_to_operand_aliasing={{0}: (10, {}), {1}: (11, {}), {2}: (12, {}), {3}: (13, {})} | custom-call | bytes 24000000 | tf_op jit(solution)/shard_map/pool/pallas_call | solution.py:269
  51.2 3.7 %collective-permute-done.14.refs_0_ = bf16[2048,128]{1,0:T(8,128)(2,1)S(1)} collective-permute-done((bf16[2048,128]{1,0:T(8,128)(2,1)S(1)}, bf16[2048,128]{1,0:T(8,128)(2,1)S(1)}, u32[]{:S(2)}, u32[]{:S(2)}) %collective-permute-start.14) | collective-permute-done | bytes 524320 | tf_op jit(solution)/shard_map/ppermute | solution.py:357
  55.5 2.1 %collective-permute-done.2.refs_6_ = bf16[2048,128]{1,0:T(8,128)(2,1)S(1)} collective-permute-done((bf16[2048,128]{1,0:T(8,128)(2,1)S(1)}, bf16[2048,128]{1,0:T(8,128)(2,1)S(1)}, u32[]{:S(2)}, u32[]{:S(2)}) %collective-permute-start.2) | collective-permute-done | bytes 524320 | tf_op jit(solution)/shard_map/ppermute | solution.py:357
  57.6 2.2 %collective-permute-done.12.refs_2_ = bf16[2048,128]{1,0:T(8,128)(2,1)S(1)} collective-permute-done((bf16[2048,128]{1,0:T(8,128)(2,1)S(1)}, bf16[2048,128]{1,0:T(8,128)(2,1)S(1)}, u32[]{:S(2)}, u32[]{:S(2)}) %collective-permute-start.12) | collective-permute-done | bytes 524320 | tf_op jit(solution)/shard_map/ppermute | solution.py:357
  60.2 1.5 %collective-permute-start.3 = (bf16[2048,128]{1,0:T(8,128)(2,1)S(1)}, bf16[2048,128]{1,0:T(8,128)(2,1)S(1)}, u32[]{:S(2)}, u32[]{:S(2)}) collective-permute-start(bf16[2048,128]{1,0:T(8,128)(2,1)S(1)} %collective-permute-done.2.refs_6_), channel_id=1, source_target_pairs={{0,2},{1,5},{2,0},{3,7},{4,6},{5,1},{6,4},{7,3},{8,10},{9,13},{10,... | collective-permute-start | bytes 1572872 | tf_op jit(solution)/shard_map/ppermute | solution.py:357
  62.7 6.9 %pool.9 = (f32[9992,128]{1,0:T(8,128)S(1)}, f32[9992,128]{1,0:T(8,128)S(1)}, f32[9992,128]{1,0:T(8,128)S(1)}, f32[9992,128]{1,0:T(8,128)S(1)}, s32[8,128]{1,0:T(8,128)}) custom-call(s32[30720]{0:T(1024)S(1)} %reshape.1470.slot_ref, s32[30720]{0:T(1024)S(1)} %reshape.1471.bag_ref, ...), custom_call_target="tpu_custom_call", output_to_operand_aliasing={{0}: (10, {}), {1}: (11, {}), {2}: (12, {}), {3}: (13, {})} | custom-call | bytes 24000000 | tf_op jit(solution)/shard_map/pool/pallas_call | solution.py:269
  69.6 2.2 %pool.10 = (f32[9992,128]{1,0:T(8,128)S(1)}, f32[9992,128]{1,0:T(8,128)S(1)}, f32[9992,128]{1,0:T(8,128)S(1)}, f32[9992,128]{1,0:T(8,128)S(1)}, s32[8,128]{1,0:T(8,128)S(1)}) custom-call(s32[30720]{0:T(1024)S(1)} %reshape.1470.slot_ref, s32[30720]{0:T(1024)S(1)} %reshape.1471.bag_ref, ...), custom_call_target="tpu_custom_call", output_to_operand_aliasing={{0}: (3, {}), {1}: (4, {}), {2}: (5, {}), {3}: (6, {})} | custom-call | bytes 3000000 | tf_op jit(solution)/shard_map/pool/pallas_call | solution.py:269
  71.9 4.1 %collective-permute-done.11.refs_1_ = bf16[2048,128]{1,0:T(8,128)(2,1)S(1)} collective-permute-done((bf16[2048,128]{1,0:T(8,128)(2,1)S(1)}, bf16[2048,128]{1,0:T(8,128)(2,1)S(1)}, u32[]{:S(2)}, u32[]{:S(2)}) %collective-permute-start.11) | collective-permute-done | bytes 524320 | tf_op jit(solution)/shard_map/ppermute | solution.py:357
  79.3 5.8 %pool.11 = (f32[9992,128]{1,0:T(8,128)S(1)}, f32[9992,128]{1,0:T(8,128)S(1)}, f32[9992,128]{1,0:T(8,128)S(1)}, f32[9992,128]{1,0:T(8,128)S(1)}, s32[8,128]{1,0:T(8,128)S(1)}) custom-call(s32[30720]{0:T(1024)S(1)} %reshape.1470.slot_ref, s32[30720]{0:T(1024)S(1)} %reshape.1471.bag_ref, ...), custom_call_target="tpu_custom_call", output_to_operand_aliasing={{0}: (8, {}), {1}: (9, {}), {2}: (10, {}), {3}: (11, {})} | custom-call | bytes 18000000 | tf_op jit(solution)/shard_map/pool/pallas_call | solution.py:269
  85.7 1.9 %collective-permute-done.30.refs_1_ = bf16[2048,128]{1,0:T(8,128)(2,1)S(1)} collective-permute-done((bf16[2048,128]{1,0:T(8,128)(2,1)S(1)}, bf16[2048,128]{1,0:T(8,128)(2,1)S(1)}, u32[]{:S(2)}, u32[]{:S(2)}) %collective-permute-start.30) | collective-permute-done | bytes 524320 | tf_op jit(solution)/shard_map/ppermute | solution.py:357
  87.6 9.2 %finish.1 = (f32[384]{0:T(512)}, f32[9992,128]{1,0:T(8,128)S(1)}, f32[9992,128]{1,0:T(8,128)S(1)}, f32[9992,128]{1,0:T(8,128)S(1)}, f32[9992,128]{1,0:T(8,128)S(1)}) custom-call(s32[30720]{0:T(1024)S(1)} %reshape.1470.slot_ref, s32[30720]{0:T(1024)S(1)} %reshape.1471.bag_ref, ...), custom_call_target="tpu_custom_call", output_to_operand_aliasing={{1}: (4, {}), {2}: (5, {}), {3}: (6, {}), {4}: (7, {})} | custom-call | tf_op jit(solution)/shard_map/finish/pallas_call | solution.py:308
  (74 shorter events, 13.4 us)
Async XLA Ops:
  2.0 13.9 %collective-permute-start.5 = (bf16[2048,128]{1,0:T(8,128)(2,1)S(1)}, bf16[2048,128]{1,0:T(8,128)(2,1)S(1)}, u32[]{:S(2)}, u32[]{:S(2)}) collective-permute-start(bf16[2048,128]{1,0:T(8,128)(2,1)S(1)} %fill.1.refs_0_), channel_id=1, source_target_pairs={{0,2},{1,5},{2,0},{3,7},{4,6},{5,1},{6,4},{7,3},{8,10},{9,13},{10,... | collective-permute-start | bytes 1572872 | tf_op jit(solution)/shard_map/ppermute | solution.py:357
  5.0 15.3 %collective-permute-start = (bf16[2048,128]{1,0:T(8,128)(2,1)S(1)}, bf16[2048,128]{1,0:T(8,128)(2,1)S(1)}, u32[]{:S(2)}, u32[]{:S(2)}) collective-permute-start(bf16[2048,128]{1,0:T(8,128)(2,1)S(1)} %fill.1.refs_0_), channel_id=1, source_target_pairs={{0,8},{1,9},{2,10},{3,11},{4,12},{5,13},{6,14},{7,15},{8,16},{9,17... | collective-permute-start | bytes 1572872 | tf_op jit(solution)/shard_map/ppermute | solution.py:357
  6.6 15.2 %collective-permute-start.7 = (bf16[2048,128]{1,0:T(8,128)(2,1)S(1)}, bf16[2048,128]{1,0:T(8,128)(2,1)S(1)}, u32[]{:S(2)}, u32[]{:S(2)}) collective-permute-start(bf16[2048,128]{1,0:T(8,128)(2,1)S(1)} %fill.1.refs_0_), channel_id=1, source_target_pairs={{0,4},{1,3},{2,6},{3,1},{4,0},{5,7},{6,2},{7,5},{8,12},{9,11},{10,... | collective-permute-start | bytes 1572872 | tf_op jit(solution)/shard_map/ppermute | solution.py:357
  8.1 14.2 %collective-permute-start.8 = (bf16[2048,128]{1,0:T(8,128)(2,1)S(1)}, bf16[2048,128]{1,0:T(8,128)(2,1)S(1)}, u32[]{:S(2)}, u32[]{:S(2)}) collective-permute-start(bf16[2048,128]{1,0:T(8,128)(2,1)S(1)} %fill.1.refs_0_), channel_id=1, source_target_pairs={{0,1},{1,0},{2,3},{3,2},{4,5},{5,4},{6,7},{7,6},{8,9},{9,8},{10,11... | collective-permute-start | bytes 1572872 | tf_op jit(solution)/shard_map/ppermute | solution.py:357
  15.8 7.3 %collective-permute-start.6 = (bf16[2048,128]{1,0:T(8,128)(2,1)S(1)}, bf16[2048,128]{1,0:T(8,128)(2,1)S(1)}, u32[]{:S(2)}, u32[]{:S(2)}) collective-permute-start(bf16[2048,128]{1,0:T(8,128)(2,1)S(1)} %gate.5.refs_0_), channel_id=1, source_target_pairs={{0,1},{1,0},{2,3},{3,2},{4,5},{5,4},{6,7},{7,6},{8,9},{9,8},{10,11... | collective-permute-start | bytes 1572872 | tf_op jit(solution)/shard_map/ppermute | solution.py:357
  20.3 14.8 %collective-permute-start.4 = (bf16[2048,128]{1,0:T(8,128)(2,1)S(1)}, bf16[2048,128]{1,0:T(8,128)(2,1)S(1)}, u32[]{:S(2)}, u32[]{:S(2)}) collective-permute-start(bf16[2048,128]{1,0:T(8,128)(2,1)S(1)} %collective-permute-done.refs_4_), channel_id=1, source_target_pairs={{0,2},{1,5},{2,0},{3,7},{4,6},{5,1},{6,4},{7,3},{8,10},{9,13},{10,... | collective-permute-start | bytes 1572872 | tf_op jit(solution)/shard_map/ppermute | solution.py:357
  21.8 13.3 %collective-permute-start.18 = (bf16[2048,128]{1,0:T(8,128)(2,1)S(1)}, bf16[2048,128]{1,0:T(8,128)(2,1)S(1)}, u32[]{:S(2)}, u32[]{:S(2)}) collective-permute-start(bf16[2048,128]{1,0:T(8,128)(2,1)S(1)} %gate.5.refs_0_), channel_id=1, source_target_pairs={{0,4},{1,3},{2,6},{3,1},{4,0},{5,7},{6,2},{7,5},{8,12},{9,11},{10,... | collective-permute-start | bytes 1572872 | tf_op jit(solution)/shard_map/ppermute | solution.py:357
  22.3 15.6 %collective-permute-start.1 = (bf16[2048,128]{1,0:T(8,128)(2,1)S(1)}, bf16[2048,128]{1,0:T(8,128)(2,1)S(1)}, u32[]{:S(2)}, u32[]{:S(2)}) collective-permute-start(bf16[2048,128]{1,0:T(8,128)(2,1)S(1)} %collective-permute-done.refs_4_), channel_id=1, source_target_pairs={{0,8},{1,9},{2,10},{3,11},{4,12},{5,13},{6,14},{7,15},{8,16},{9,17... | collective-permute-start | bytes 1572872 | tf_op jit(solution)/shard_map/ppermute | solution.py:357
  23.1 17.1 %collective-permute-start.16 = (bf16[2048,128]{1,0:T(8,128)(2,1)S(1)}, bf16[2048,128]{1,0:T(8,128)(2,1)S(1)}, u32[]{:S(2)}, u32[]{:S(2)}) collective-permute-start(bf16[2048,128]{1,0:T(8,128)(2,1)S(1)} %collective-permute-done.refs_4_), channel_id=1, source_target_pairs={{0,4},{1,3},{2,6},{3,1},{4,0},{5,7},{6,2},{7,5},{8,12},{9,11},{10,... | collective-permute-start | bytes 1572872 | tf_op jit(solution)/shard_map/ppermute | solution.py:357
  23.9 17.8 %collective-permute-start.17 = (bf16[2048,128]{1,0:T(8,128)(2,1)S(1)}, bf16[2048,128]{1,0:T(8,128)(2,1)S(1)}, u32[]{:S(2)}, u32[]{:S(2)}) collective-permute-start(bf16[2048,128]{1,0:T(8,128)(2,1)S(1)} %collective-permute-done.7.refs_2_), channel_id=1, source_target_pairs={{0,1},{1,0},{2,3},{3,2},{4,5},{5,4},{6,7},{7,6},{8,9},{9,8},{10,11... | collective-permute-start | bytes 1572872 | tf_op jit(solution)/shard_map/ppermute | solution.py:357
  35.1 7.2 %collective-permute-start.15 = (bf16[2048,128]{1,0:T(8,128)(2,1)S(1)}, bf16[2048,128]{1,0:T(8,128)(2,1)S(1)}, u32[]{:S(2)}, u32[]{:S(2)}) collective-permute-start(bf16[2048,128]{1,0:T(8,128)(2,1)S(1)} %gate.6.refs_0_), channel_id=1, source_target_pairs={{0,1},{1,0},{2,3},{3,2},{4,5},{5,4},{6,7},{7,6},{8,9},{9,8},{10,11... | collective-permute-start | bytes 1572872 | tf_op jit(solution)/shard_map/ppermute | solution.py:357
  35.1 7.5 %collective-permute-start.19 = (bf16[2048,128]{1,0:T(8,128)(2,1)S(1)}, bf16[2048,128]{1,0:T(8,128)(2,1)S(1)}, u32[]{:S(2)}, u32[]{:S(2)}) collective-permute-start(bf16[2048,128]{1,0:T(8,128)(2,1)S(1)} %collective-permute-done.18.refs_4_), channel_id=1, source_target_pairs={{0,1},{1,0},{2,3},{3,2},{4,5},{5,4},{6,7},{7,6},{8,9},{9,8},{10,11... | collective-permute-start | bytes 1572872 | tf_op jit(solution)/shard_map/ppermute | solution.py:357
  37.8 6.0 %collective-permute-start.20 = (bf16[2048,128]{1,0:T(8,128)(2,1)S(1)}, bf16[2048,128]{1,0:T(8,128)(2,1)S(1)}, u32[]{:S(2)}, u32[]{:S(2)}) collective-permute-start(bf16[2048,128]{1,0:T(8,128)(2,1)S(1)} %collective-permute-done.1.refs_6_), channel_id=1, source_target_pairs={{0,1},{1,0},{2,3},{3,2},{4,5},{5,4},{6,7},{7,6},{8,9},{9,8},{10,11... | collective-permute-start | bytes 1572872 | tf_op jit(solution)/shard_map/ppermute | solution.py:357
  40.2 14.7 %collective-permute-start.14 = (bf16[2048,128]{1,0:T(8,128)(2,1)S(1)}, bf16[2048,128]{1,0:T(8,128)(2,1)S(1)}, u32[]{:S(2)}, u32[]{:S(2)}) collective-permute-start(bf16[2048,128]{1,0:T(8,128)(2,1)S(1)} %collective-permute-done.1.refs_6_), channel_id=1, source_target_pairs={{0,2},{1,5},{2,0},{3,7},{4,6},{5,1},{6,4},{7,3},{8,10},{9,13},{10,... | collective-permute-start | bytes 1572872 | tf_op jit(solution)/shard_map/ppermute | solution.py:357
  41.7 13.2 %collective-permute-start.10 = (bf16[2048,128]{1,0:T(8,128)(2,1)S(1)}, bf16[2048,128]{1,0:T(8,128)(2,1)S(1)}, u32[]{:S(2)}, u32[]{:S(2)}) collective-permute-start(bf16[2048,128]{1,0:T(8,128)(2,1)S(1)} %gate.6.refs_0_), channel_id=1, source_target_pairs={{0,4},{1,3},{2,6},{3,1},{4,0},{5,7},{6,2},{7,5},{8,12},{9,11},{10,... | collective-permute-start | bytes 1572872 | tf_op jit(solution)/shard_map/ppermute | solution.py:357
  42.2 15.4 %collective-permute-start.2 = (bf16[2048,128]{1,0:T(8,128)(2,1)S(1)}, bf16[2048,128]{1,0:T(8,128)(2,1)S(1)}, u32[]{:S(2)}, u32[]{:S(2)}) collective-permute-start(bf16[2048,128]{1,0:T(8,128)(2,1)S(1)} %collective-permute-done.1.refs_6_), channel_id=1, source_target_pairs={{0,8},{1,9},{2,10},{3,11},{4,12},{5,13},{6,14},{7,15},{8,16},{9,17... | collective-permute-start | bytes 1572872 | tf_op jit(solution)/shard_map/ppermute | solution.py:357
  42.6 17.2 %collective-permute-start.12 = (bf16[2048,128]{1,0:T(8,128)(2,1)S(1)}, bf16[2048,128]{1,0:T(8,128)(2,1)S(1)}, u32[]{:S(2)}, u32[]{:S(2)}) collective-permute-start(bf16[2048,128]{1,0:T(8,128)(2,1)S(1)} %collective-permute-done.1.refs_6_), channel_id=1, source_target_pairs={{0,4},{1,3},{2,6},{3,1},{4,0},{5,7},{6,2},{7,5},{8,12},{9,11},{10,... | collective-permute-start | bytes 1572872 | tf_op jit(solution)/shard_map/ppermute | solution.py:357
  43.8 16.2 %collective-permute-start.22 = (bf16[2048,128]{1,0:T(8,128)(2,1)S(1)}, bf16[2048,128]{1,0:T(8,128)(2,1)S(1)}, u32[]{:S(2)}, u32[]{:S(2)}) collective-permute-start(bf16[2048,128]{1,0:T(8,128)(2,1)S(1)} %collective-permute-done.16.refs_2_), channel_id=1, source_target_pairs={{0,1},{1,0},{2,3},{3,2},{4,5},{5,4},{6,7},{7,6},{8,9},{9,8},{10,11... | collective-permute-start | bytes 1572872 | tf_op jit(solution)/shard_map/ppermute | solution.py:357
  54.9 6.7 %collective-permute-start.23 = (bf16[2048,128]{1,0:T(8,128)(2,1)S(1)}, bf16[2048,128]{1,0:T(8,128)(2,1)S(1)}, u32[]{:S(2)}, u32[]{:S(2)}) collective-permute-start(bf16[2048,128]{1,0:T(8,128)(2,1)S(1)} %collective-permute-done.10.refs_4_), channel_id=1, source_target_pairs={{0,1},{1,0},{2,3},{3,2},{4,5},{5,4},{6,7},{7,6},{8,9},{9,8},{10,11... | collective-permute-start | bytes 1572872 | tf_op jit(solution)/shard_map/ppermute | solution.py:357
  59.8 9.9 %collective-permute-start.13 = (bf16[2048,128]{1,0:T(8,128)(2,1)S(1)}, bf16[2048,128]{1,0:T(8,128)(2,1)S(1)}, u32[]{:S(2)}, u32[]{:S(2)}) collective-permute-start(bf16[2048,128]{1,0:T(8,128)(2,1)S(1)} %collective-permute-done.12.refs_2_), channel_id=1, source_target_pairs={{0,1},{1,0},{2,3},{3,2},{4,5},{5,4},{6,7},{7,6},{8,9},{9,8},{10,11... | collective-permute-start | bytes 1572872 | tf_op jit(solution)/shard_map/ppermute | solution.py:357
  60.0 15.9 %collective-permute-start.11 = (bf16[2048,128]{1,0:T(8,128)(2,1)S(1)}, bf16[2048,128]{1,0:T(8,128)(2,1)S(1)}, u32[]{:S(2)}, u32[]{:S(2)}) collective-permute-start(bf16[2048,128]{1,0:T(8,128)(2,1)S(1)} %collective-permute-done.10.refs_4_), channel_id=1, source_target_pairs={{0,8},{1,9},{2,10},{3,11},{4,12},{5,13},{6,14},{7,15},{8,16},{9,17... | collective-permute-start | bytes 1572872 | tf_op jit(solution)/shard_map/ppermute | solution.py:357
  60.2 15.7 %collective-permute-start.3 = (bf16[2048,128]{1,0:T(8,128)(2,1)S(1)}, bf16[2048,128]{1,0:T(8,128)(2,1)S(1)}, u32[]{:S(2)}, u32[]{:S(2)}) collective-permute-start(bf16[2048,128]{1,0:T(8,128)(2,1)S(1)} %collective-permute-done.2.refs_6_), channel_id=1, source_target_pairs={{0,2},{1,5},{2,0},{3,7},{4,6},{5,1},{6,4},{7,3},{8,10},{9,13},{10,... | collective-permute-start | bytes 1572872 | tf_op jit(solution)/shard_map/ppermute | solution.py:357
  61.7 14.8 %collective-permute-start.27 = (bf16[2048,128]{1,0:T(8,128)(2,1)S(1)}, bf16[2048,128]{1,0:T(8,128)(2,1)S(1)}, u32[]{:S(2)}, u32[]{:S(2)}) collective-permute-start(bf16[2048,128]{1,0:T(8,128)(2,1)S(1)} %collective-permute-done.2.refs_6_), channel_id=1, source_target_pairs={{0,4},{1,3},{2,6},{3,1},{4,0},{5,7},{6,2},{7,5},{8,12},{9,11},{10,... | collective-permute-start | bytes 1572872 | tf_op jit(solution)/shard_map/ppermute | solution.py:357
  76.5 9.2 %collective-permute-start.25 = (bf16[2048,128]{1,0:T(8,128)(2,1)S(1)}, bf16[2048,128]{1,0:T(8,128)(2,1)S(1)}, u32[]{:S(2)}, u32[]{:S(2)}) collective-permute-start(bf16[2048,128]{1,0:T(8,128)(2,1)S(1)} %get-tuple-element.57.refs_0_), channel_id=1, source_target_pairs={{0,4},{1,3},{2,6},{3,1},{4,0},{5,7},{6,2},{7,5},{8,12},{9,11},{10,... | collective-permute-start | bytes 1572872 | tf_op jit(solution)/shard_map/ppermute | solution.py:357
  (12 other events, 64.7 us)
